TPU v7x, 512 devices: a whole 4x8x8 slice. The times are simulated.
512 devices in a mesh: seq: 64 (over z, y), head: 8 (over x, core).
Axes of the slice: x: 4, y: 8, z: 8, core: 2. Of those that a mesh axis runs over, the one named last changes fastest.
Arguments:
- hidden: bfloat16 [32768, 4096], P('seq', 'head'), may hold values from -6 to 6
- queries: bfloat16 [32768, 4096], P('seq', 'head'), may hold values from -120 to 120
- keys_low: bfloat16 [32768, 1024], P('seq', 'head'), may hold values from -6 to 6
- values_low: bfloat16 [32768, 1024], P('seq', 'head'), may hold values from -6 to 6
- out_weight: bfloat16 [4096, 4096], P('head', 'seq'), may hold values from -0.09375 to 0.09375
- norm_gain: float32 [4096], replicated, may hold values from 0.25 to 1.75
- query_weight: bfloat16 [4096, 4096], P('seq', 'head'), may hold values from -3 to 3
- key_weight: bfloat16 [4096, 1024], P('seq', 'head'), may hold values from -0.09375 to 0.09375
- value_weight: bfloat16 [4096, 1024], P('seq', 'head'), may hold values from -0.09375 to 0.09375
- keep_index: int32 [64, 256], P('seq'), may hold values from 0 to 511, as said below
- keep_count: int32 [64], replicated, may hold values from 128 to 256, as said below
Outputs:
- merged_attention: bfloat16 [16384, 4096], P('seq', 'head')
Inputs may be any that keep to these rules, and one draw needn't show every extreme that they name: `keep_index`: each block's valid positions are distinct, in increasing order; padded slots hold 0. `keep_count`: the first block keeps 256 positions.
All inputs are finite; a program needn't handle non-finite values.
Results may differ from a plain program's by a relative error of at most 0.04.
Values may be sent and summed in bfloat16 or wider, within the bound.
No kernel may reach another device: no remote copies, remote signals or barrier semaphores. Data moves between devices by JAX's collectives and lax.ppermute only.
A program may use at most 64 MiB of HBM per device.

v0:
```python
import jax
import jax.numpy as jnp
from jax import lax
from jax.sharding import PartitionSpec as P

D = 4096
HEADS = 32
KV_HEADS = 8
HD = 128
BLOCK = 512
KMAX = 256


def from_behind(x, axis, by):
    peers = lax.axis_size(axis)
    pairs = [(i, i + by) for i in range(peers) if 0 <= i + by < peers]
    return lax.ppermute(x, axis, pairs)


def per_device(
    hidden,
    queries,
    keys_low,
    values_low,
    out_weight,
    norm_gain,
    query_weight,
    key_weight,
    value_weight,
    keep_index,
    keep_count,
):
    n_blocks = keep_index.shape[0]
    kv_local = keys_low.shape[1] // HD
    group = HEADS // KV_HEADS
    query_heads = queries.reshape(n_blocks, BLOCK, kv_local, group, HD)
    key_heads = keys_low.reshape(n_blocks, BLOCK, kv_local, HD)
    value_heads = values_low.reshape(n_blocks, BLOCK, kv_local, HD)
    scores = (
        jnp.einsum("cqhgd,ckhd->chgqk", query_heads, key_heads, preferred_element_type=jnp.float32)
        / HD**0.5
    )
    position = jnp.arange(BLOCK)
    causal = position[:, None] >= position[None, :]
    scores = jnp.where(causal, scores, -1e30)
    weights = jax.nn.softmax(scores, axis=-1).astype(jnp.bfloat16)
    attention = jnp.einsum(
        "chgqk,ckhd->cqhgd", weights, value_heads, preferred_element_type=jnp.float32
    )
    attention = attention.astype(jnp.bfloat16).reshape(n_blocks * BLOCK, queries.shape[1])
    flat_index = (keep_index + jnp.arange(n_blocks, dtype=jnp.int32)[:, None] * BLOCK).reshape(-1)
    projected = jnp.dot(
        attention,
        lax.all_gather(out_weight, "seq", axis=1, tiled=True),
        preferred_element_type=jnp.float32,
    )
    summed = lax.psum_scatter(
        projected.astype(jnp.bfloat16), "head", scatter_dimension=1, tiled=True
    ).astype(jnp.float32)
    updated = (hidden.astype(jnp.float32) + summed).astype(jnp.bfloat16)
    state = updated[flat_index]
    share = state.shape[1]
    gain_share = lax.dynamic_slice_in_dim(norm_gain, lax.axis_index("head") * share, share)
    state_f = state.astype(jnp.float32)
    squares = lax.psum(jnp.sum(state_f * state_f, axis=-1), "head")
    scaled = state_f * lax.rsqrt(squares[:, None] / D + 1e-05) * gain_share[None, :]
    features = lax.all_gather(scaled.astype(jnp.bfloat16), "head", axis=1, tiled=True)
    pieces = (
        lax.all_gather(query_weight, "seq", axis=0, tiled=True),
        lax.all_gather(key_weight, "seq", axis=0, tiled=True),
        lax.all_gather(value_weight, "seq", axis=0, tiled=True),
    )
    upper_q, upper_k, upper_v = tuple(
        (jnp.dot(features, piece, preferred_element_type=jnp.float32) for piece in pieces)
    )
    upper_q = upper_q.astype(jnp.bfloat16)
    upper_k = upper_k.astype(jnp.bfloat16)
    upper_v = upper_v.astype(jnp.bfloat16)
    partner_k, partner_v = from_behind((upper_k, upper_v), "seq", 1)
    seq_pos = lax.axis_index("seq")
    is_right = seq_pos % 2 == 1
    own_count = lax.dynamic_slice_in_dim(keep_count, seq_pos * n_blocks, n_blocks)
    left_count = lax.dynamic_slice_in_dim(
        keep_count, jnp.maximum(seq_pos - 1, 0) * n_blocks, n_blocks
    )
    query_up = upper_q.reshape(n_blocks, KMAX, kv_local, group, HD)
    key_up = jnp.concatenate(
        [
            partner_k.reshape(n_blocks, KMAX, kv_local, HD),
            upper_k.reshape(n_blocks, KMAX, kv_local, HD),
        ],
        axis=1,
    )
    value_up = jnp.concatenate(
        [
            partner_v.reshape(n_blocks, KMAX, kv_local, HD),
            upper_v.reshape(n_blocks, KMAX, kv_local, HD),
        ],
        axis=1,
    )
    slot = jnp.arange(KMAX)
    column = jnp.arange(2 * KMAX)
    own_column = column - KMAX
    from_left = (
        (column[None, None, :] < KMAX)
        & is_right
        & (column[None, None, :] < left_count[:, None, None])
    )
    from_own = (
        (column[None, None, :] >= KMAX)
        & (own_column[None, None, :] <= slot[None, :, None])
        & (own_column[None, None, :] < own_count[:, None, None])
    )
    allowed = from_left | from_own
    upper_scores = (
        jnp.einsum("cqhgd,ckhd->chgqk", query_up, key_up, preferred_element_type=jnp.float32)
        / HD**0.5
    )
    upper_scores = jnp.where(allowed[:, None, None, :, :], upper_scores, -1e30)
    upper_weights = jax.nn.softmax(upper_scores, axis=-1).astype(jnp.bfloat16)
    merged = jnp.einsum(
        "chgqk,ckhd->cqhgd", upper_weights, value_up, preferred_element_type=jnp.float32
    )
    merged = merged.reshape(n_blocks, KMAX, upper_q.shape[1])
    valid_rows = slot[None, :] < own_count[:, None]
    merged = jnp.where(valid_rows[:, :, None], merged, 0.0)
    return merged.astype(jnp.bfloat16).reshape(n_blocks * KMAX, upper_q.shape[1])


def solution(mesh):
    in_specs = (
        P("seq", "head"),
        P("seq", "head"),
        P("seq", "head"),
        P("seq", "head"),
        P("head", "seq"),
        P(),
        P("seq", "head"),
        P("seq", "head"),
        P("seq", "head"),
        P("seq", None),
        P(),
    )
    out_specs = P("seq", "head")
    return jax.shard_map(
        per_device, mesh=mesh, in_specs=in_specs, out_specs=out_specs, check_vma=False
    )
```

profile of v0, /device:TPU:1, one launch (start us, length us, event | category | flops | bytes accessed | tf_op | source)
XLA Modules:
  0.0 444.2 jit_solution(13393170369497059944)
XLA Ops:
  6.5 0.7 all-gather.6.cloned.1.call-update
  7.3 0.0 reduce-scatter.2.cloned.1.call-start
  7.3 0.1 iota_compare_fusion
  7.4 0.2 copy-done
  7.6 1.8 fusion.1
  9.4 0.9 fusion
  10.3 0.0 copy-done.5
  10.3 1.3 fusion.6
  11.6 87.6 %all-gather.6.cloned.1.call-done = bf16[512,4096]{0,1:T(8,128)(2,1)} async-done(((bf16[512,64]{0,1:T(8,128)(2,1)}), bf16[512,4096]{0,1:T(8,128)(2,1)}) %all-gather.6.cloned.1.call-update) | async-done | bytes 4194320 | tf_op jit(solution)/shard_map/all_gather | solution.py:54
  99.2 6.5 %convolution_convert_fusion = bf16[512,4096]{1,0:T(8,128)(2,1)} fusion(bf16[512,512]{0,1:T(8,128)(2,1)S(1)} %bitcast.98, bf16[512,4096]{0,1:T(8,128)(2,1)} %all-gather.6.cloned.1.call-done), kind=kOutput, calls=%fused_computation.1 | convolution fusion | flops 2149580800 | bytes 8912896 | tf_op jit(solution)/shard_map/dot_general | solution.py:52
  105.7 0.0 reduce-scatter.2.cloned.1.call-update
  105.8 0.0 all-gather.12.cloned.1.call-start
  105.8 0.7 all-gather.12.cloned.1.call-update
  106.5 0.0 all-gather.8.cloned.1.call-start
  106.5 0.8 dynamic_slice.10
  107.3 40.1 %reduce-scatter.2.cloned.1.call-done = bf16[512,512]{1,0:T(8,128)(2,1)} async-done(((bf16[512,4096]{1,0:T(8,128)(2,1)}), bf16[512,512]{1,0:T(8,128)(2,1)}) %reduce-scatter.2.cloned.1.call-update) | async-done | bytes 524304 | tf_op jit(solution)/shard_map/reduce_scatter | solution.py:57
  147.5 0.0 copy-done.2
  147.5 1.2 add_convert_fusion
  148.6 1.2 gather_fusion
  149.8 0.1 fusion.12
  149.9 14.6 %psum.7 = f32[256]{0:T(256)S(1)} all-reduce(f32[256]{0:T(256)S(1)} %fusion.12), channel_id=1, replica_groups=mesh['seq'=64,'head'=8] {'head'}, use_global_device_ids=true, to_apply=%region_4.5 | all-reduce | flops 256 | bytes 2048 | tf_op jit(solution)/shard_map/psum | solution.py:65
  164.5 0.8 fusion.14
  165.4 0.0 all-gather.8.cloned.1.call-update
  165.4 0.0 all-gather.10.cloned.1.call-start
  165.5 0.5 all-gather.10.cloned.1.call-update
  166.0 0.0 all-gather.14.cloned.1.call-start
  166.0 0.5 all-gather.14.cloned.1.call-update
  166.6 0.7 fusion.35
  167.3 0.6 broadcast_compare_fusion
  167.9 0.6 iota_compare_fusion.5
  168.5 0.7 iota_compare_fusion.2
  169.2 0.3 fusion.20
  169.6 59.8 %all-gather.12.cloned.1.call-done = bf16[4096,128]{1,0:T(8,128)(2,1)} async-done(((bf16[64,128]{1,0:T(8,128)(2,1)}), bf16[4096,128]{1,0:T(8,128)(2,1)}) %all-gather.12.cloned.1.call-update) | async-done | bytes 1048592 | tf_op jit(solution)/shard_map/all_gather | solution.py:70
  229.4 34.3 %all-gather.8.cloned.1.call-done = bf16[256,4096]{1,0:T(8,128)(2,1)} async-done(((bf16[256,512]{1,0:T(8,128)(2,1)}), bf16[256,4096]{1,0:T(8,128)(2,1)}) %all-gather.8.cloned.1.call-update) | async-done | bytes 2097168 | tf_op jit(solution)/shard_map/all_gather | solution.py:67
  263.6 2.7 convolution_convert_fusion.2
  266.4 3.1 collective-permute-start.1
  269.5 74.6 %all-gather.10.cloned.1.call-done = bf16[4096,128]{1,0:T(8,128)(2,1)} async-done(((bf16[64,128]{1,0:T(8,128)(2,1)}), bf16[4096,128]{1,0:T(8,128)(2,1)}) %all-gather.10.cloned.1.call-update) | async-done | bytes 1048592 | tf_op jit(solution)/shard_map/all_gather | solution.py:71
  344.0 2.6 convolution_convert_fusion.3
  346.6 2.9 collective-permute-start
  349.5 82.1 %all-gather.14.cloned.1.call-done = bf16[4096,512]{1,0:T(8,128)(2,1)} async-done(((bf16[64,512]{1,0:T(8,128)(2,1)}), bf16[4096,512]{1,0:T(8,128)(2,1)}) %all-gather.14.cloned.1.call-update) | async-done | bytes 4194320 | tf_op jit(solution)/shard_map/all_gather | solution.py:69
  431.6 3.4 fusion.9
  435.0 0.0 collective-permute-done.1
  435.0 0.5 fusion.36
  435.5 0.3 fusion.5
  435.8 0.0 collective-permute-done
  435.8 0.5 fusion.10
  436.4 0.1 copy.25
  436.5 0.8 select_convert_fusion
  (14 shorter events, 0.0 us)
Async XLA Ops:
  6.5 1.0 copy-start
  6.5 92.6 %all-gather.6.cloned.1.call-start = ((), (), s32[]{:S(2)}) async-start(), calls=%async_computation.1 | async-start | bytes 4259840 | tf_op jit(solution)/shard_map/all_gather | solution.py:54
  7.3 140.2 %reduce-scatter.2.cloned.1.call-start = ((), (), s32[]{:S(2)}) async-start(), calls=%async_computation.2 | async-start | bytes 4718592 | tf_op jit(solution)/shard_map/reduce_scatter | solution.py:57
  7.6 2.7 copy-start.5
  105.7 1.6 copy-start.4
  105.7 41.7 %copy-start.2 = (bf16[512,512]{1,0:T(8,128)(2,1)S(1)}, bf16[512,512]{1,0:T(8,128)(2,1)}, u32[]{:S(2)}) copy-start(bf16[512,512]{1,0:T(8,128)(2,1)} %param.11) | copy-start | bytes 1572868
  105.7 60.9 %copy-start.3 = (s32[64]{0:T(128)S(1)}, s32[64]{0:T(128)}, u32[]{:S(2)}) copy-start(s32[64]{0:T(128)} %param.21) | copy-start | bytes 772
  105.8 123.6 %all-gather.12.cloned.1.call-start = ((), (), s32[]{:S(2)}) async-start(), calls=%async_computation.5 | async-start | bytes 1064960 | tf_op jit(solution)/shard_map/all_gather | solution.py:70
  106.5 157.2 %all-gather.8.cloned.1.call-start = ((), (), s32[]{:S(2)}) async-start(), calls=%async_computation.3 | async-start | bytes 2359296 | tf_op jit(solution)/shard_map/all_gather | solution.py:67
  165.4 178.6 %all-gather.10.cloned.1.call-start = ((), (), s32[]{:S(2)}) async-start(), calls=%async_computation.4 | async-start | bytes 1064960 | tf_op jit(solution)/shard_map/all_gather | solution.py:71
  166.0 265.6 %all-gather.14.cloned.1.call-start = ((), (), s32[]{:S(2)}) async-start(), calls=%async_computation.6 | async-start | bytes 4259840 | tf_op jit(solution)/shard_map/all_gather | solution.py:69
  263.6 167.9 %copy-start.1 = (bf16[256,4096]{1,0:T(8,128)(2,1)S(1)}, bf16[256,4096]{1,0:T(8,128)(2,1)}, u32[]{:S(2)}) copy-start(bf16[256,4096]{1,0:T(8,128)(2,1)} %all-gather.8.cloned.1.call-done) | copy-start | bytes 6291460
  266.4 168.7 %collective-permute-start.1 = (bf16[256,128]{1,0:T(8,128)(2,1)S(1)}, bf16[256,128]{1,0:T(8,128)(2,1)S(1)}, u32[]{:S(2)}, u32[]{:S(2)}) collective-permute-start(bf16[256,128]{1,0:T(8,128)(2,1)S(1)} %convolution_convert_fusion.2), channel_id=1, source_target_pairs={{0,8},{8,16},{16,24},{24,32},{32,40},{40,48},{48,56},{56,64},{64,7... | collective-permute-start | bytes 196616 | tf_op jit(solution)/shard_map/ppermute | solution.py:17
  346.6 89.2 %collective-permute-start = (bf16[256,128]{1,0:T(8,128)(2,1)S(1)}, bf16[256,128]{1,0:T(8,128)(2,1)S(1)}, u32[]{:S(2)}, u32[]{:S(2)}) collective-permute-start(bf16[256,128]{1,0:T(8,128)(2,1)S(1)} %convolution_convert_fusion.3), channel_id=1, source_target_pairs={{0,8},{8,16},{16,24},{24,32},{32,40},{40,48},{48,56},{56,64},{64,7... | collective-permute-start | bytes 196616 | tf_op jit(solution)/shard_map/ppermute | solution.py:17
Sparse Core Ops, SparseCore 0:
  10.4 88.7 all-gather.5
  105.9 41.5 reduce-scatter.1
  150.5 78.8 all-gather.11
  231.4 32.2 all-gather.7
  266.6 77.4 all-gather.9
  347.0 84.5 all-gather.13
where the time goes:
time: 448 us; the launch traced here: 444 us
  waiting for transfers between devices  381 us (85%)
  matrix products  19.3 us (4%)
  blocking collectives  14.6 us (3%)
  between operations  13.6 us (3%)
  other arithmetic  6.54 us (1%)
  starting transfers between devices  6.21 us (1%)
    all_gather x1, waiting for transfers between devices, per_device(): lax.all_gather(out_weight, 'seq', axis=1, tiled=True)  87.6 us
    all_gather x1, waiting for transfers between devices, per_device(): lax.all_gather(query_weight, 'seq', axis=0, tiled=True)  82.1 us
    all_gather x1, waiting for transfers between devices, per_device(): lax.all_gather(value_weight, 'seq', axis=0, tiled=True)  74.6 us
    all_gather x1, waiting for transfers between devices, per_device(): lax.all_gather(key_weight, 'seq', axis=0, tiled=True)  59.8 us
    reduce_scatter x1, waiting for transfers between devices, per_device(): lax.psum_scatter(projected.astype(jnp.bfloat16), 'head', scatter_dimensio...  40.1 us
    all_gather x1, waiting for transfers between devices, per_device(): lax.all_gather(scaled.astype(jnp.bfloat16), 'head', axis=1, tiled=True)  34.3 us
    psum x1, blocking collectives, per_device(): squares = lax.psum(jnp.sum(state_f * state_f, axis=-1), 'head')  14.6 us
  transfers between devices with their start and end apart: 8, of which 6 were waited for; matrix products, arithmetic and copies ran while one was open for 5% of the time, Pallas kernels for 0%

commit v1 on v0

v1 whole, which is shorter than its diff:
```python
import functools

import jax
import jax.numpy as jnp
from jax import lax
from jax.experimental import pallas as pl
from jax.experimental.pallas import tpu as pltpu
from jax.sharding import PartitionSpec as P

D = 4096
HEADS = 32
KV_HEADS = 8
HD = 128
BLOCK = 512
KMAX = 256
GROUP = HEADS // KV_HEADS
N_Z = 8
N_Y = 8
N_X = 4
STRIP = D // (N_Z * N_Y)
HALF = N_Y // 2 * STRIP
QW = GROUP * HD
KVW = 2 * HD
QKV = QW + KVW
LOG2E = 1.4426950408889634
SCALE = HD**-0.5 * LOG2E
NEG = -1e30
VMEM_LIMIT = 48 * 1024 * 1024

PARITY_GROUPS = [[z * N_Y + 2 * p + q for z in range(N_Z) for p in range(N_Y // 2)] for q in range(2)]
X_GROUPS = [[2 * x + c for x in range(N_X)] for c in range(2)]
CORE_SWAP = [(i, i ^ 1) for i in range(2 * N_X)]
SIBLING_SWAP = [(i, i ^ 1) for i in range(N_Z * N_Y)]
Z_HEAD_SWAP = [
    ((z * N_Y + y) * 8 + h, (h * N_Y + y) * 8 + z)
    for z in range(N_Z)
    for y in range(N_Y)
    for h in range(8)
]


def params():
    return pltpu.CompilerParams(vmem_limit_bytes=VMEM_LIMIT)


def dot(a, b):
    return jnp.dot(a, b, preferred_element_type=jnp.float32)


def dot_t(a, b):
    return lax.dot_general(a, b, (((1,), (1,)), ((), ())), preferred_element_type=jnp.float32)


def attend(scores, values):
    top = jnp.max(scores, axis=1, keepdims=True)
    unnormed = jnp.exp2(scores - top)
    total = jnp.sum(unnormed, axis=1, keepdims=True)
    return dot(unnormed.astype(jnp.bfloat16), values) / total


def lower_kernel(index_ref, q_ref, k_ref, v_ref, hidden_ref, out_ref):
    index = index_ref[...]
    column = lax.broadcasted_iota(jnp.int32, (KMAX, BLOCK), 1)
    pick = (column == index).astype(jnp.bfloat16)
    causal = column <= index
    queries = dot(pick, q_ref[...]).astype(jnp.bfloat16)
    keys = k_ref[...]
    values = v_ref[...]
    for g in range(GROUP):
        cols = slice(g * HD, (g + 1) * HD)
        scores = jnp.where(causal, dot_t(queries[:, cols], keys) * SCALE, NEG)
        out_ref[:, cols] = attend(scores, values).astype(jnp.bfloat16)
    out_ref[:, QW:] = dot(pick, hidden_ref[...]).astype(jnp.bfloat16)


def lower(index, queries, keys, values, hidden):
    return pl.pallas_call(
        lower_kernel,
        out_shape=jax.ShapeDtypeStruct((KMAX, 2 * QW), jnp.bfloat16),
        compiler_params=params(),
        name="lower",
    )(index, queries, keys, values, hidden)


def project_kernel(place_ref, mine_ref, other_ref, weight_ref, hid_ref, hid_pair_ref, out_ref, acc_ref):
    step = pl.program_id(0)
    core = place_ref[0]
    parity = place_ref[1]

    @pl.when(step == 0)
    def _():
        row = lax.broadcasted_iota(jnp.int32, (QW, HALF), 0)
        col = lax.broadcasted_iota(jnp.int32, (QW, HALF), 1)
        source = (col // STRIP) * (2 * STRIP) + parity * STRIP + col % STRIP
        pick = (row == source).astype(jnp.bfloat16)
        acc_ref[:KMAX] = dot(hid_ref[...], pick)
        acc_ref[KMAX:] = dot(hid_pair_ref[...], pick)

    def share(core_of):
        return weight_ref[pl.ds(core_of * 4, 4)].reshape(HALF, QW)

    acc_ref[...] += dot_t(mine_ref[0], share(core)) + dot_t(other_ref[0], share(1 - core))

    @pl.when(step == N_X - 1)
    def _():
        state = acc_ref[...].astype(jnp.bfloat16)
        for x in range(N_X):
            out_ref[x] = state


def project(place, mine, other, weights, hid, hid_pair):
    rows = 2 * KMAX
    return pl.pallas_call(
        project_kernel,
        grid=(N_X,),
        in_specs=[
            pl.BlockSpec(memory_space=pltpu.SMEM),
            pl.BlockSpec((1, rows, QW), lambda i: (i, 0, 0)),
            pl.BlockSpec((1, rows, QW), lambda i: (i, 0, 0)),
            pl.BlockSpec((8, STRIP, QW), lambda i: (i, 0, 0)),
            pl.BlockSpec((KMAX, QW), lambda i: (0, 1)),
            pl.BlockSpec((KMAX, QW), lambda i: (0, 1)),
        ],
        out_specs=pl.BlockSpec((N_X, rows, HALF), lambda i: (0, 0, 0)),
        out_shape=jax.ShapeDtypeStruct((N_X, rows, HALF), jnp.bfloat16),
        scratch_shapes=[pltpu.VMEM((rows, HALF), jnp.float32)],
        compiler_params=params(),
        name="project",
    )(place, mine, other, weights, hid, hid_pair)


def qkv_kernel(
    place_ref, mine_ref, other_ref, wq_ref, wkv_ref, gain_ref, own_ref, pair_kv_ref, square_ref, send_ref, acc_ref, sq_ref
):
    step = pl.program_id(0)
    core = place_ref[0]

    @pl.when(step == 0)
    def _():
        acc_ref[...] = jnp.zeros_like(acc_ref)
        sq_ref[...] = jnp.zeros_like(sq_ref)

    def add(part_ref, core_of):
        state = part_ref[0].astype(jnp.float32)
        squares = state * state
        sq_ref[...] += squares[:, :HD] + squares[:, HD:]
        scaled = (state * gain_ref[2 * step + core_of]).astype(jnp.bfloat16)
        wq = wq_ref[pl.ds(core_of * 4, 4)].reshape(HALF, QW)
        packed = wkv_ref[pl.ds(core_of * 4, 4)]
        wkv = jnp.concatenate([packed[:, :, :KVW], packed[:, :, KVW:]], axis=1).reshape(HALF, KVW)
        acc_ref[:, :QW] += dot(scaled, wq)
        acc_ref[:, QW:] += dot(scaled, wkv)

    add(mine_ref, core)
    add(other_ref, 1 - core)

    @pl.when(step == N_X - 1)
    def _():
        total = jnp.sum(sq_ref[...], axis=1, keepdims=True)
        own_ref[...] = acc_ref[:KMAX]
        pair_kv_ref[...] = acc_ref[KMAX:, QW:]
        square_ref[...] = jnp.broadcast_to(total, square_ref.shape)
        send_ref[:, :QKV] = acc_ref[KMAX:].astype(jnp.bfloat16)
        send_ref[:, QKV : QKV + KVW] = acc_ref[:KMAX, QW:].astype(jnp.bfloat16)
        high = total.astype(jnp.bfloat16).astype(jnp.float32)
        low = total - high
        lane = lax.broadcasted_iota(jnp.int32, (KMAX, HD), 1)
        tail = jnp.where(
            lane == 0,
            high[KMAX:],
            jnp.where(lane == 1, low[KMAX:], jnp.where(lane == 2, high[:KMAX], low[:KMAX])),
        )
        send_ref[:, QKV + KVW :] = tail.astype(jnp.bfloat16)


def qkv(place, mine, other, weights, gain):
    rows = 2 * KMAX
    sent = QKV + KVW + HD
    return pl.pallas_call(
        qkv_kernel,
        grid=(N_X,),
        in_specs=[
            pl.BlockSpec(memory_space=pltpu.SMEM),
            pl.BlockSpec((1, rows, HALF), lambda i: (i, 0, 0)),
            pl.BlockSpec((1, rows, HALF), lambda i: (i, 0, 0)),
            pl.BlockSpec((8, STRIP, QW), lambda i: (i, 1, 0)),
            pl.BlockSpec((8, STRIP // 2, QW), lambda i: (i, 4, 0)),
            pl.BlockSpec((8, 1, HALF), lambda i: (0, 0, 0)),
        ],
        out_specs=[
            pl.BlockSpec((KMAX, QKV), lambda i: (0, 0)),
            pl.BlockSpec((KMAX, KVW), lambda i: (0, 0)),
            pl.BlockSpec((rows, HD), lambda i: (0, 0)),
            pl.BlockSpec((KMAX, sent), lambda i: (0, 0)),
        ],
        out_shape=[
            jax.ShapeDtypeStruct((KMAX, QKV), jnp.float32),
            jax.ShapeDtypeStruct((KMAX, KVW), jnp.float32),
            jax.ShapeDtypeStruct((rows, HD), jnp.float32),
            jax.ShapeDtypeStruct((KMAX, sent), jnp.bfloat16),
        ],
        scratch_shapes=[
            pltpu.VMEM((rows, QKV), jnp.float32),
            pltpu.VMEM((rows, HD), jnp.float32),
        ],
        compiler_params=params(),
        name="qkv",
    )(place, mine, other, weights, weights, gain)


def upper_kernel(place_ref, own_ref, pair_kv_ref, square_ref, got_ref, out_ref):
    parity = place_ref[1]
    own_count = place_ref[2]
    left_count = place_ref[3]
    tail = got_ref[:, QKV + KVW :].astype(jnp.float32)
    own_sum = square_ref[:KMAX, :1] + (tail[:, 0:1] + tail[:, 1:2])
    pair_sum = square_ref[KMAX:, :1] + (tail[:, 2:3] + tail[:, 3:4])
    own_inv = lax.rsqrt(own_sum / D + 1e-05)
    pair_inv = lax.rsqrt(pair_sum / D + 1e-05)
    own = ((own_ref[...] + got_ref[:, :QKV].astype(jnp.float32)) * own_inv).astype(jnp.bfloat16)
    pair = (pair_kv_ref[...] + got_ref[:, QKV : QKV + KVW].astype(jnp.float32)) * pair_inv
    pair = pair.astype(jnp.bfloat16)
    keys = jnp.concatenate([pair[:, :HD], own[:, QW : QW + HD]], axis=0)
    values = jnp.concatenate([pair[:, HD:], own[:, QW + HD :]], axis=0)
    row = lax.broadcasted_iota(jnp.int32, (KMAX, 2 * KMAX), 0)
    col = lax.broadcasted_iota(jnp.int32, (KMAX, 2 * KMAX), 1)
    from_left = col < left_count * parity
    from_own = (col >= KMAX) & (col - KMAX <= row) & (col - KMAX < own_count)
    allowed = from_left | from_own
    valid = lax.broadcasted_iota(jnp.int32, (KMAX, HD), 0) < own_count
    for g in range(GROUP):
        cols = slice(g * HD, (g + 1) * HD)
        scores = jnp.where(allowed, dot_t(own[:, cols], keys) * SCALE, NEG)
        out_ref[:, cols] = jnp.where(valid, attend(scores, values), 0.0).astype(jnp.bfloat16)


def upper(place, own, pair_kv, squares, got):
    return pl.pallas_call(
        upper_kernel,
        in_specs=[pl.BlockSpec(memory_space=pltpu.SMEM)] + [pl.BlockSpec(memory_space=pltpu.VMEM)] * 4,
        out_shape=jax.ShapeDtypeStruct((KMAX, QW), jnp.bfloat16),
        compiler_params=params(),
        name="upper",
    )(place, own, pair_kv, squares, got)


def gather_head(x):
    mine = lax.all_to_all(x, "head", 0, 0, axis_index_groups=X_GROUPS, tiled=True)
    return mine, lax.ppermute(mine, "head", CORE_SWAP)


def per_device(
    hidden,
    queries,
    keys_low,
    values_low,
    out_weight,
    norm_gain,
    query_weight,
    key_weight,
    value_weight,
    keep_index,
    keep_count,
):
    seq = lax.axis_index("seq")
    parity = seq % 2
    core = lax.axis_index("head") % 2
    own_count = lax.dynamic_index_in_dim(keep_count, seq, keepdims=False)
    left_count = lax.dynamic_index_in_dim(keep_count, jnp.maximum(seq - 1, 0), keepdims=False)
    place = jnp.stack([core, parity, own_count, left_count]).astype(jnp.int32)

    columns = lax.ppermute(out_weight.T, ("seq", "head"), Z_HEAD_SWAP)
    kv = jnp.concatenate([key_weight, value_weight], axis=1)
    kv = jnp.concatenate([kv[: STRIP // 2], kv[STRIP // 2 :]], axis=1)
    packed = jnp.concatenate([columns, query_weight, kv], axis=0)
    weights = lax.all_gather(packed, "seq", axis=0, axis_index_groups=PARITY_GROUPS)

    kept = lower(keep_index.reshape(KMAX, 1), queries, keys_low, values_low, hidden)
    kept_pair = lax.ppermute(kept, "seq", SIBLING_SWAP)
    attention = jnp.concatenate([kept[:, :QW], kept_pair[:, :QW]], axis=0)
    mine, other = gather_head(jnp.broadcast_to(attention[None], (N_X,) + attention.shape))

    state = project(place, mine, other, weights, kept, kept_pair)
    mine, other = gather_head(state)
    gain = lax.dynamic_index_in_dim(
        norm_gain.reshape(8, N_Y // 2, 2, STRIP), parity, axis=2, keepdims=False
    ).reshape(8, 1, HALF)
    own, pair_kv, squares, send = qkv(place, mine, other, weights, gain)
    got = lax.ppermute(send, "seq", SIBLING_SWAP)
    return upper(place, own, pair_kv, squares, got)


def solution(mesh):
    in_specs = (
        P("seq", "head"),
        P("seq", "head"),
        P("seq", "head"),
        P("seq", "head"),
        P("head", "seq"),
        P(),
        P("seq", "head"),
        P("seq", "head"),
        P("seq", "head"),
        P("seq", None),
        P(),
    )
    out_specs = P("seq", "head")
    return jax.shard_map(
        per_device, mesh=mesh, in_specs=in_specs, out_specs=out_specs, check_vma=False
    )
```

time: 448 us -> 196 us (0.44)
  waiting for transfers between devices: 381 us -> 74.5 us
  blocking collectives: 14.6 us -> 60.3 us
  matrix products: 19.3 us -> 0 us
  starting transfers between devices: 6.21 us -> 23.1 us
  Pallas kernels: 0 us -> 13.4 us
    all_gather x5 -> x1, waiting for transfers between devices: 338 us -> 46 us  [per_device(): lax.all_gather(packed, 'seq', axis=0, axis_index_groups=PARITY_GROUPS)]
    all_to_all x0 -> x2, blocking collectives: none -> 60.3 us  [gather_head(): lax.all_to_all(x, 'head', 0, 0, axis_index_groups=X_GROUPS, tiled=True)]
    reduce_scatter x1 -> x0, waiting for transfers between devices: 40.1 us -> none  [per_device(): lax.psum_scatter(projected.astype(jnp.bfloat16), 'head', scatter_dimensio...]
    ppermute x2 -> x5, waiting for transfers between devices: 0.01 us -> 28.4 us  [the longest x1 13.4 us: per_device(): got = lax.ppermute(send, 'seq', SIBLING_SWAP)]
    dot_general x8 -> x0, matrix products: 19.3 us -> none  [the longest x3 8.68 us: per_device(): jnp.dot(features, piece, preferred_element_type=jnp.float32)]
    ppermute x2 -> x5, starting transfers between devices: 6.01 us -> 23.1 us  [the longest x2 8.86 us: gather_head(): return (mine, lax.ppermute(mine, 'head', CORE_SWAP))]
    psum x1 -> x0, blocking collectives: 14.6 us -> none  [per_device(): squares = lax.psum(jnp.sum(state_f * state_f, axis=-1), 'head')]
    pallas_call x0 -> x4, Pallas kernels: none -> 13.4 us  [the longest x1 4.41 us: qkv(): pl.pallas_call(qkv_kernel, grid=(N_X,), in_specs=[pl.BlockSpec(memory_spa...]
  transfers between devices with their start and end apart: 8 -> 6, of which waited for: 6 -> 6; matrix products, arithmetic and copies ran while one was open for 5% -> 2% of each run, Pallas kernels for 0% -> 1%
where the time goes in v1:
time: 196 us; the launch traced here: 195 us
  waiting for transfers between devices  74.5 us (38%)
  blocking collectives  60.3 us (31%)
  starting transfers between devices  23.1 us (12%)
  between operations  13.6 us (7%)
  Pallas kernels  13.4 us (7%)
  local copies, waits for them, and re-layouts  7.24 us (4%)
  other arithmetic  2.88 us (1%)
    all_to_all x2, blocking collectives, gather_head(): lax.all_to_all(x, 'head', 0, 0, axis_index_groups=X_GROUPS, tiled=True)  60.3 us
    all_gather x1, waiting for transfers between devices, per_device(): lax.all_gather(packed, 'seq', axis=0, axis_index_groups=PARITY_GROUPS)  46 us
    ppermute x1, waiting for transfers between devices, per_device(): got = lax.ppermute(send, 'seq', SIBLING_SWAP)  13.4 us
    ppermute x1, waiting for transfers between devices, per_device(): kept_pair = lax.ppermute(kept, 'seq', SIBLING_SWAP)  10.5 us
    ppermute x2, starting transfers between devices, gather_head(): return (mine, lax.ppermute(mine, 'head', CORE_SWAP))  8.86 us
    ppermute x1, starting transfers between devices, per_device(): got = lax.ppermute(send, 'seq', SIBLING_SWAP)  5.63 us
    ppermute x1, starting transfers between devices, per_device(): columns = lax.ppermute(out_weight.T, ('seq', 'head'), Z_HEAD_SWAP)  5.38 us
    unnamed x13, local copies, waits for them, and re-layouts  4.62 us
  transfers between devices with their start and end apart: 6, of which 6 were waited for; matrix products, arithmetic and copies ran while one was open for 2% of the time, Pallas kernels for 1%

profile of v1, /device:TPU:1, one launch (start us, length us, event | category | flops | bytes accessed | tf_op | source)
XLA Modules:
  0.0 194.9 jit_solution(8691466889898156889)
XLA Ops:
  6.5 0.0 all-gather.3.cloned.1.call-start
  6.5 5.4 %collective-permute-start.2 = (bf16[64,512]{1,0:T(8,128)(2,1)}, bf16[64,512]{1,0:T(8,128)(2,1)S(1)}, u32[]{:S(2)}, u32[]{:S(2)}) collective-permute-start(bf16[64,512]{1,0:T(8,128)(2,1)} %bitcast.9), channel_id=1, source_target_pairs={{0,0},{1,64},{2,128},{3,192},{4,256},{5,320},{6,384},{7,448},{8,8}... | collective-permute-start | bytes 196616 | tf_op jit(solution)/shard_map/ppermute | solution.py:272
  11.9 0.7 constant_dynamic-update-slice_fusion.1
  12.6 0.7 constant_dynamic-update-slice_fusion
  13.4 0.7 collective-permute-done.2
  14.1 1.5 maximum_maximum_fusion
  15.6 0.0 all-gather.3.cloned.1.call-update
  15.6 0.8 copy.12.index_ref
  16.4 0.0 copy-start
  16.4 1.0 copy-done
  17.5 0.0 copy-start.1
  17.5 1.0 copy-done.1
  18.5 0.0 copy-start.2
  18.5 0.9 copy-done.2
  19.4 0.0 copy-start.3
  19.4 0.9 copy-done.3
  20.3 1.8 lower.1.hid_ref
  22.1 3.2 %collective-permute-start = (bf16[256,1024]{1,0:T(8,128)(2,1)S(1)}, bf16[256,1024]{1,0:T(8,128)(2,1)S(1)}, u32[]{:S(2)}, u32[]{:S(2)}) collective-permute-start(bf16[256,1024]{1,0:T(8,128)(2,1)S(1)} %lower.1.hid_ref), channel_id=1, source_target_pairs={{0,8},{8,0},{16,24},{24,16},{32,40},{40,32},{48,56},{56,48},{64,72... | collective-permute-start | bytes 1572872 | tf_op jit(solution)/shard_map/ppermute | solution.py:279
  25.3 10.5 %collective-permute-done.hid_pair_ref = bf16[256,1024]{1,0:T(8,128)(2,1)S(1)} collective-permute-done((bf16[256,1024]{1,0:T(8,128)(2,1)S(1)}, bf16[256,1024]{1,0:T(8,128)(2,1)S(1)}, u32[]{:S(2)}, u32[]{:S(2)}) %collective-permute-start) | collective-permute-done | bytes 524320 | tf_op jit(solution)/shard_map/ppermute | solution.py:279
  35.9 0.2 broadcast_in_dim.2
  36.0 0.0 copy-start.5
  36.1 43.5 %all_to_all.10.mine_ref = bf16[4,512,512]{2,1,0:T(8,128)(2,1)S(1)} all-to-all(bf16[4,512,512]{2,1,0:T(8,128)(2,1)S(1)} %broadcast_in_dim.2), channel_id=1, replica_groups={{0,2,4,6},{1,3,5,7},{8,10,12,14},{9,11,13,15},{16,18,20,22},{17,19,21,2..., dimensions={0} | all-to-all | bytes 4194304 | tf_op jit(solution)/shard_map/all_to_all | solution.py:248
  79.6 3.1 %collective-permute-start.1 = (bf16[4,512,512]{2,1,0:T(8,128)(2,1)S(1)}, bf16[4,512,512]{2,1,0:T(8,128)(2,1)}, u32[]{:S(2)}, u32[]{:S(2)}) collective-permute-start(bf16[4,512,512]{2,1,0:T(8,128)(2,1)S(1)} %all_to_all.10.mine_ref), channel_id=1, source_target_pairs={{0,1},{1,0},{2,3},{3,2},{4,5},{5,4},{6,7},{7,6},{8,9},{9,8},{10,11... | collective-permute-start | bytes 6291464 | tf_op jit(solution)/shard_map/ppermute | solution.py:249
  82.7 0.0 copy-done.5
  82.7 0.6 fusion.1
  83.3 1.3 pad_add_fusion.place_ref
  84.7 1.9 collective-permute-done.1.other_ref
  86.5 46.0 %all-gather.3.cloned.1.call-done = bf16[5120,512]{1,0:T(8,128)(2,1)} async-done(((bf16[160,512]{1,0:T(8,128)(2,1)}), bf16[5120,512]{1,0:T(8,128)(2,1)}) %all-gather.3.cloned.1.call-update) | async-done | bytes 5242896 | tf_op jit(solution)/shard_map/all_gather | solution.py:276
  132.6 4.4 %project.1 = bf16[4,512,256]{2,1,0:T(8,128)(2,1)S(1)} custom-call(s32[4]{0:T(128)S(1)} %pad_add_fusion.place_ref, bf16[4,512,512]{2,1,0:T(8,128)(2,1)S(1)} %all_to_all.10.mine_ref, bf16[4,512,512]{2,1,0:T(8,128)(2,1)} %collective-permute-done.1.other_ref, bf16[32,160,512]{2,1,0:T(8,128)(2,1)} %bitcast.5, bf16[256,1024]{1,0:T(8,128)(2,1)S(1)} %lower.1.hid_ref, ...), custom_call_target="tpu_custom_call" | custom-call | tf_op jit(solution)/shard_map/project/pallas_call | solution.py:113
  137.0 0.0 copy-start.4
  137.0 16.7 %all_to_all.11.mine_ref = bf16[4,512,256]{2,1,0:T(8,128)(2,1)S(1)} all-to-all(bf16[4,512,256]{2,1,0:T(8,128)(2,1)S(1)} %project.1), channel_id=1, replica_groups={{0,2,4,6},{1,3,5,7},{8,10,12,14},{9,11,13,15},{16,18,20,22},{17,19,21,2..., dimensions={0} | all-to-all | bytes 2097152 | tf_op jit(solution)/shard_map/all_to_all | solution.py:248
  153.7 5.8 %collective-permute-start.3 = (bf16[4,512,256]{2,1,0:T(8,128)(2,1)S(1)}, bf16[4,512,256]{2,1,0:T(8,128)(2,1)S(1)}, u32[]{:S(2)}, u32[]{:S(2)}) collective-permute-start(bf16[4,512,256]{2,1,0:T(8,128)(2,1)S(1)} %all_to_all.11.mine_ref), channel_id=1, source_target_pairs={{0,1},{1,0},{2,3},{3,2},{4,5},{5,4},{6,7},{7,6},{8,9},{9,8},{10,11... | collective-permute-start | bytes 3145736 | tf_op jit(solution)/shard_map/ppermute | solution.py:249
  159.5 0.0 copy-done.4
  159.6 0.1 reshape.12
  159.7 0.1 dynamic-slice_reduce_fusion
  159.7 0.1 reshape.13.gain_ref
  159.8 2.0 %collective-permute-done.3.other_ref = bf16[4,512,256]{2,1,0:T(8,128)(2,1)S(1)} collective-permute-done((bf16[4,512,256]{2,1,0:T(8,128)(2,1)S(1)}, bf16[4,512,256]{2,1,0:T(8,128)(2,1)S(1)}, u32[]{:S(2)}, u32[]{:S(2)}) %collective-permute-start.3) | collective-permute-done | bytes 1048608 | tf_op jit(solution)/shard_map/ppermute | solution.py:249
  161.8 4.4 %qkv.1 = (f32[256,768]{1,0:T(8,128)S(1)}, f32[256,256]{1,0:T(8,128)S(1)}, f32[512,128]{1,0:T(8,128)S(1)}, bf16[256,1152]{1,0:T(8,128)(2,1)S(1)}) custom-call(s32[4]{0:T(128)S(1)} %pad_add_fusion.place_ref, bf16[4,512,256]{2,1,0:T(8,128)(2,1)S(1)} %all_to_all.11.mine_ref, bf16[4,512,256]{2,1,0:T(8,128)(2,1)S(1)} %collective-permute-done.3.other_ref, ...), custom_call_target="tpu_custom_call" | custom-call | tf_op jit(solution)/shard_map/qkv/pallas_call | solution.py:179
  166.2 5.6 %collective-permute-start.4 = (bf16[256,1152]{1,0:T(8,128)(2,1)S(1)}, bf16[256,1152]{1,0:T(8,128)(2,1)S(1)}, u32[]{:S(2)}, u32[]{:S(2)}) collective-permute-start(bf16[256,1152]{1,0:T(8,128)(2,1)S(1)} %get-tuple-element.12), channel_id=1, source_target_pairs={{0,8},{8,0},{16,24},{24,16},{32,40},{40,32},{48,56},{56,48},{64,72... | collective-permute-start | bytes 1769480 | tf_op jit(solution)/shard_map/ppermute | solution.py:289
  171.9 13.4 %collective-permute-done.4.got_ref = bf16[256,1152]{1,0:T(8,128)(2,1)S(1)} collective-permute-done((bf16[256,1152]{1,0:T(8,128)(2,1)S(1)}, bf16[256,1152]{1,0:T(8,128)(2,1)S(1)}, u32[]{:S(2)}, u32[]{:S(2)}) %collective-permute-start.4) | collective-permute-done | bytes 589856 | tf_op jit(solution)/shard_map/ppermute | solution.py:289
  185.2 2.8 %upper.1 = bf16[256,512]{1,0:T(8,128)(2,1)} custom-call(s32[4]{0:T(128)S(1)} %pad_add_fusion.place_ref, f32[256,768]{1,0:T(8,128)S(1)} %get-tuple-element.9.own_ref, f32[256,256]{1,0:T(8,128)S(1)} %get-tuple-element.10.pair_kv_ref, f32[512,128]{1,0:T(8,128)S(1)} %get-tuple-element.11.square_ref, bf16[256,1152]{1,0:T(8,128)(2,1)S(1)} %collective-permute-done.4.got_ref), custom_call_target="tpu_custom_call" | custom-call | tf_op jit(solution)/shard_map/upper/pallas_call | solution.py:238
  (4 shorter events, 0.1 us)
Async XLA Ops:
  6.5 126.0 %all-gather.3.cloned.1.call-start = ((), (), s32[]{:S(2)}) async-start(), calls=%async_computation.2 | async-start | bytes 5406720 | tf_op jit(solution)/shard_map/all_gather | solution.py:276
  6.5 7.5 %collective-permute-start.2 = (bf16[64,512]{1,0:T(8,128)(2,1)}, bf16[64,512]{1,0:T(8,128)(2,1)S(1)}, u32[]{:S(2)}, u32[]{:S(2)}) collective-permute-start(bf16[64,512]{1,0:T(8,128)(2,1)} %bitcast.9), channel_id=1, source_target_pairs={{0,0},{1,64},{2,128},{3,192},{4,256},{5,320},{6,384},{7,448},{8,8}... | collective-permute-start | bytes 196616 | tf_op jit(solution)/shard_map/ppermute | solution.py:272
  16.4 1.0 copy-start
  17.5 1.0 copy-start.1
  18.5 0.9 copy-start.2
  19.4 0.9 copy-start.3
  22.1 13.7 %collective-permute-start = (bf16[256,1024]{1,0:T(8,128)(2,1)S(1)}, bf16[256,1024]{1,0:T(8,128)(2,1)S(1)}, u32[]{:S(2)}, u32[]{:S(2)}) collective-permute-start(bf16[256,1024]{1,0:T(8,128)(2,1)S(1)} %lower.1.hid_ref), channel_id=1, source_target_pairs={{0,8},{8,0},{16,24},{24,16},{32,40},{40,32},{48,56},{56,48},{64,72... | collective-permute-start | bytes 1572872 | tf_op jit(solution)/shard_map/ppermute | solution.py:279
  36.0 46.6 %copy-start.5 = (s32[64]{0:T(128)S(1)}, s32[64]{0:T(128)}, u32[]{:S(2)}) copy-start(s32[64]{0:T(128)} %param.21) | copy-start | bytes 772
  79.6 7.0 %collective-permute-start.1 = (bf16[4,512,512]{2,1,0:T(8,128)(2,1)S(1)}, bf16[4,512,512]{2,1,0:T(8,128)(2,1)}, u32[]{:S(2)}, u32[]{:S(2)}) collective-permute-start(bf16[4,512,512]{2,1,0:T(8,128)(2,1)S(1)} %all_to_all.10.mine_ref), channel_id=1, source_target_pairs={{0,1},{1,0},{2,3},{3,2},{4,5},{5,4},{6,7},{7,6},{8,9},{9,8},{10,11... | collective-permute-start | bytes 6291464 | tf_op jit(solution)/shard_map/ppermute | solution.py:249
  137.0 22.6 %copy-start.4 = (f32[4096]{0:T(1024)S(1)}, f32[4096]{0:T(1024)}, u32[]{:S(2)}) copy-start(f32[4096]{0:T(1024)} %param.16) | copy-start | bytes 49156
  153.7 8.1 %collective-permute-start.3 = (bf16[4,512,256]{2,1,0:T(8,128)(2,1)S(1)}, bf16[4,512,256]{2,1,0:T(8,128)(2,1)S(1)}, u32[]{:S(2)}, u32[]{:S(2)}) collective-permute-start(bf16[4,512,256]{2,1,0:T(8,128)(2,1)S(1)} %all_to_all.11.mine_ref), channel_id=1, source_target_pairs={{0,1},{1,0},{2,3},{3,2},{4,5},{5,4},{6,7},{7,6},{8,9},{9,8},{10,11... | collective-permute-start | bytes 3145736 | tf_op jit(solution)/shard_map/ppermute | solution.py:249
  166.2 19.0 %collective-permute-start.4 = (bf16[256,1152]{1,0:T(8,128)(2,1)S(1)}, bf16[256,1152]{1,0:T(8,128)(2,1)S(1)}, u32[]{:S(2)}, u32[]{:S(2)}) collective-permute-start(bf16[256,1152]{1,0:T(8,128)(2,1)S(1)} %get-tuple-element.12), channel_id=1, source_target_pairs={{0,8},{8,0},{16,24},{24,16},{32,40},{40,32},{48,56},{56,48},{64,72... | collective-permute-start | bytes 1769480 | tf_op jit(solution)/shard_map/ppermute | solution.py:289
Sparse Core Ops, SparseCore 0:
  15.7 116.8 all-gather.2

commit v2 on v1

--- a/solution.py
+++ b/solution.py
@@ -27,16 +27,11 @@
 NEG = -1e30
 VMEM_LIMIT = 48 * 1024 * 1024
 
-PARITY_GROUPS = [[z * N_Y + 2 * p + q for z in range(N_Z) for p in range(N_Y // 2)] for q in range(2)]
+Z_GROUPS = [[z * N_Y + y for z in range(N_Z)] for y in range(N_Y)]
 X_GROUPS = [[2 * x + c for x in range(N_X)] for c in range(2)]
 CORE_SWAP = [(i, i ^ 1) for i in range(2 * N_X)]
 SIBLING_SWAP = [(i, i ^ 1) for i in range(N_Z * N_Y)]
-Z_HEAD_SWAP = [
-    ((z * N_Y + y) * 8 + h, (h * N_Y + y) * 8 + z)
-    for z in range(N_Z)
-    for y in range(N_Y)
-    for h in range(8)
-]
+PARITY_GROUPS = [[z * N_Y + 2 * p + q for p in range(N_Y // 2)] for z in range(N_Z) for q in range(2)]
 
 
 def params():
@@ -82,51 +77,70 @@
     )(index, queries, keys, values, hidden)
 
 
-def project_kernel(place_ref, mine_ref, other_ref, weight_ref, hid_ref, hid_pair_ref, out_ref, acc_ref):
-    step = pl.program_id(0)
+def project_kernel(place_ref, own_ref, pair_ref, weight_ref, keep_ref, send_ref):
     core = place_ref[0]
-    parity = place_ref[1]
-
-    @pl.when(step == 0)
-    def _():
-        row = lax.broadcasted_iota(jnp.int32, (QW, HALF), 0)
-        col = lax.broadcasted_iota(jnp.int32, (QW, HALF), 1)
-        source = (col // STRIP) * (2 * STRIP) + parity * STRIP + col % STRIP
-        pick = (row == source).astype(jnp.bfloat16)
-        acc_ref[:KMAX] = dot(hid_ref[...], pick)
-        acc_ref[KMAX:] = dot(hid_pair_ref[...], pick)
-
-    def share(core_of):
-        return weight_ref[pl.ds(core_of * 4, 4)].reshape(HALF, QW)
-
-    acc_ref[...] += dot_t(mine_ref[0], share(core)) + dot_t(other_ref[0], share(1 - core))
-
-    @pl.when(step == N_X - 1)
-    def _():
-        state = acc_ref[...].astype(jnp.bfloat16)
-        for x in range(N_X):
-            out_ref[x] = state
-
-
-def project(place, mine, other, weights, hid, hid_pair):
-    rows = 2 * KMAX
+    mine = weight_ref[core]
+    other = weight_ref[1 - core]
+    keep_ref[0, :KMAX] = dot_t(own_ref[...], mine)
+    keep_ref[0, KMAX:] = dot_t(pair_ref[...], mine)
+    send_ref[0, :KMAX] = dot_t(own_ref[...], other).astype(jnp.bfloat16)
+    send_ref[0, KMAX:] = dot_t(pair_ref[...], other).astype(jnp.bfloat16)
+
+
+def project(place, kept, kept_pair, weights):
+    shape = (N_X, 2 * KMAX, HALF)
+    block = pl.BlockSpec((1, 2 * KMAX, HALF), lambda i: (i, 0, 0))
     return pl.pallas_call(
         project_kernel,
         grid=(N_X,),
         in_specs=[
             pl.BlockSpec(memory_space=pltpu.SMEM),
-            pl.BlockSpec((1, rows, QW), lambda i: (i, 0, 0)),
-            pl.BlockSpec((1, rows, QW), lambda i: (i, 0, 0)),
-            pl.BlockSpec((8, STRIP, QW), lambda i: (i, 0, 0)),
+            pl.BlockSpec((KMAX, QW), lambda i: (0, 0)),
+            pl.BlockSpec((KMAX, QW), lambda i: (0, 0)),
+            pl.BlockSpec((2, HALF, QW), lambda i: (i, 0, 0)),
+        ],
+        out_specs=[block, block],
+        out_shape=[
+            jax.ShapeDtypeStruct(shape, jnp.float32),
+            jax.ShapeDtypeStruct(shape, jnp.bfloat16),
+        ],
+        compiler_params=params(),
+        name="project",
+    )(place, kept, kept_pair, weights)
+
+
+def state_kernel(place_ref, parts_ref, hid_ref, hid_pair_ref, out_ref):
+    parity = place_ref[1]
+    row = lax.broadcasted_iota(jnp.int32, (QW, HALF), 0)
+    col = lax.broadcasted_iota(jnp.int32, (QW, HALF), 1)
+    source = (col // STRIP) * (2 * STRIP) + parity * STRIP + col % STRIP
+    pick = (row == source).astype(jnp.bfloat16)
+    for half, hid in enumerate((hid_ref, hid_pair_ref)):
+        rows = slice(half * KMAX, (half + 1) * KMAX)
+        total = dot(hid[...], pick)
+        for x in range(N_X):
+            total += parts_ref[x, rows].astype(jnp.float32)
+        state = total.astype(jnp.bfloat16)
+        for x in range(N_X):
+            out_ref[x, rows] = state
+
+
+def add_up(place, parts, kept, kept_pair):
+    shape = (N_X, 2 * KMAX, HALF)
+    return pl.pallas_call(
+        state_kernel,
+        grid=(1,),
+        in_specs=[
+            pl.BlockSpec(memory_space=pltpu.SMEM),
+            pl.BlockSpec(shape, lambda i: (0, 0, 0)),
             pl.BlockSpec((KMAX, QW), lambda i: (0, 1)),
             pl.BlockSpec((KMAX, QW), lambda i: (0, 1)),
         ],
-        out_specs=pl.BlockSpec((N_X, rows, HALF), lambda i: (0, 0, 0)),
-        out_shape=jax.ShapeDtypeStruct((N_X, rows, HALF), jnp.bfloat16),
-        scratch_shapes=[pltpu.VMEM((rows, HALF), jnp.float32)],
-        compiler_params=params(),
-        name="project",
-    )(place, mine, other, weights, hid, hid_pair)
+        out_specs=pl.BlockSpec(shape, lambda i: (0, 0, 0)),
+        out_shape=jax.ShapeDtypeStruct(shape, jnp.bfloat16),
+        compiler_params=params(),
+        name="state",
+    )(place, parts, kept, kept_pair)
 
 
 def qkv_kernel(
@@ -183,8 +197,8 @@
             pl.BlockSpec(memory_space=pltpu.SMEM),
             pl.BlockSpec((1, rows, HALF), lambda i: (i, 0, 0)),
             pl.BlockSpec((1, rows, HALF), lambda i: (i, 0, 0)),
-            pl.BlockSpec((8, STRIP, QW), lambda i: (i, 1, 0)),
-            pl.BlockSpec((8, STRIP // 2, QW), lambda i: (i, 4, 0)),
+            pl.BlockSpec((8, STRIP, QW), lambda i: (i, 0, 0)),
+            pl.BlockSpec((8, STRIP // 2, QW), lambda i: (i, 2, 0)),
             pl.BlockSpec((8, 1, HALF), lambda i: (0, 0, 0)),
         ],
         out_specs=[
@@ -249,6 +263,11 @@
     return mine, lax.ppermute(mine, "head", CORE_SWAP)
 
 
+def gather_seq(shard):
+    some = lax.all_gather(shard, "seq", axis=0, axis_index_groups=PARITY_GROUPS, tiled=True)
+    return lax.all_gather(some, "seq", axis=0, axis_index_groups=Z_GROUPS)
+
+
 def per_device(
     hidden,
     queries,
@@ -269,23 +288,26 @@
     left_count = lax.dynamic_index_in_dim(keep_count, jnp.maximum(seq - 1, 0), keepdims=False)
     place = jnp.stack([core, parity, own_count, left_count]).astype(jnp.int32)
 
-    columns = lax.ppermute(out_weight.T, ("seq", "head"), Z_HEAD_SWAP)
+    out_weights = gather_seq(out_weight.T)
+
+    kept = lower(keep_index.reshape(KMAX, 1), queries, keys_low, values_low, hidden)
+    kept_pair = lax.ppermute(kept, "seq", SIBLING_SWAP)
+
     kv = jnp.concatenate([key_weight, value_weight], axis=1)
     kv = jnp.concatenate([kv[: STRIP // 2], kv[STRIP // 2 :]], axis=1)
-    packed = jnp.concatenate([columns, query_weight, kv], axis=0)
-    weights = lax.all_gather(packed, "seq", axis=0, axis_index_groups=PARITY_GROUPS)
-
-    kept = lower(keep_index.reshape(KMAX, 1), queries, keys_low, values_low, hidden)
-    kept_pair = lax.ppermute(kept, "seq", SIBLING_SWAP)
-    attention = jnp.concatenate([kept[:, :QW], kept_pair[:, :QW]], axis=0)
-    mine, other = gather_head(jnp.broadcast_to(attention[None], (N_X,) + attention.shape))
-
-    state = project(place, mine, other, weights, kept, kept_pair)
-    mine, other = gather_head(state)
+    qkv_weights = gather_seq(jnp.concatenate([query_weight, kv], axis=0))
+    qkv_weights = qkv_weights.reshape(N_Z * N_Y // 2, STRIP + STRIP // 2, QW)
+
+    keep, send = project(place, kept, kept_pair, out_weights)
+    got = lax.ppermute(send, "head", CORE_SWAP)
+    parts = (keep + got.astype(jnp.float32)).astype(jnp.bfloat16)
+    parts = lax.all_to_all(parts, "head", 0, 0, axis_index_groups=X_GROUPS, tiled=True)
+    mine, other = gather_head(add_up(place, parts, kept, kept_pair))
+
     gain = lax.dynamic_index_in_dim(
         norm_gain.reshape(8, N_Y // 2, 2, STRIP), parity, axis=2, keepdims=False
     ).reshape(8, 1, HALF)
-    own, pair_kv, squares, send = qkv(place, mine, other, weights, gain)
+    own, pair_kv, squares, send = qkv(place, mine, other, qkv_weights, gain)
     got = lax.ppermute(send, "seq", SIBLING_SWAP)
     return upper(place, own, pair_kv, squares, got)
 

time: 196 us -> 154 us (0.79)
  waiting for transfers between devices: 74.5 us -> 38.3 us
  starting transfers between devices: 23.1 us -> 16.9 us
  blocking collectives: 60.3 us -> 63.6 us
  local copies, waits for them, and re-layouts: 7.24 us -> 4.94 us
    all_to_all x2 -> x1, blocking collectives: 60.3 us -> 15.8 us  [gather_head(): lax.all_to_all(x, 'head', 0, 0, axis_index_groups=X_GROUPS, tiled=True)]
    all_gather x1 -> x2, waiting for transfers between devices: 46 us -> 15.7 us  [gather_seq(): return lax.all_gather(some, 'seq', axis=0, axis_index_groups=Z_GROUPS)]
    all_gather x0 -> x2, blocking collectives: none -> 29.3 us  [gather_seq(): lax.all_gather(shard, 'seq', axis=0, axis_index_groups=PARITY_GROUPS, til...]
    all_to_all x0 -> x1, blocking collectives: none -> 18.6 us  [per_device(): lax.all_to_all(parts, 'head', 0, 0, axis_index_groups=X_GROUPS, tiled=True)]
    ppermute x1, waiting for transfers between devices: 10.5 us -> 5 us  [per_device(): kept_pair = lax.ppermute(kept, 'seq', SIBLING_SWAP)]
    ppermute x2 -> x1, starting transfers between devices: 8.86 us -> 4.6 us  [gather_head(): return (mine, lax.ppermute(mine, 'head', CORE_SWAP))]
    ppermute x1, starting transfers between devices: 5.63 us -> 3 us  [per_device(): got = lax.ppermute(send, 'seq', SIBLING_SWAP)]
    unnamed x13, local copies, waits for them, and re-layouts: 4.62 us -> 2.54 us
  transfers between devices with their start and end apart: 6 -> 6, of which waited for: 6 -> 6; matrix products, arithmetic and copies ran while one was open for 2% -> 4% of each run, Pallas kernels for 1% -> 4%
where the time goes in v2:
time: 154 us; the launch traced here: 153 us
  blocking collectives  63.6 us (41%)
  waiting for transfers between devices  38.3 us (25%)
  starting transfers between devices  16.9 us (11%)
  Pallas kernels  13.6 us (9%)
  between operations  13.6 us (9%)
  local copies, waits for them, and re-layouts  4.94 us (3%)
  other arithmetic  2.49 us (2%)
    all_gather x2, blocking collectives, gather_seq(): lax.all_gather(shard, 'seq', axis=0, axis_index_groups=PARITY_GROUPS, til...  29.3 us
    all_to_all x1, blocking collectives, per_device(): lax.all_to_all(parts, 'head', 0, 0, axis_index_groups=X_GROUPS, tiled=True)  18.6 us
    all_to_all x1, blocking collectives, gather_head(): lax.all_to_all(x, 'head', 0, 0, axis_index_groups=X_GROUPS, tiled=True)  15.8 us
    all_gather x2, waiting for transfers between devices, gather_seq(): return lax.all_gather(some, 'seq', axis=0, axis_index_groups=Z_GROUPS)  15.7 us
    ppermute x1, waiting for transfers between devices, per_device(): got = lax.ppermute(send, 'seq', SIBLING_SWAP)  13.4 us
    ppermute x1, starting transfers between devices, per_device(): got = lax.ppermute(send, 'head', CORE_SWAP)  5.93 us
    ppermute x1, waiting for transfers between devices, per_device(): kept_pair = lax.ppermute(kept, 'seq', SIBLING_SWAP)  5 us
    ppermute x1, starting transfers between devices, gather_head(): return (mine, lax.ppermute(mine, 'head', CORE_SWAP))  4.6 us
  transfers between devices with their start and end apart: 6, of which 6 were waited for; matrix products, arithmetic and copies ran while one was open for 4% of the time, Pallas kernels for 4%

profile of v2, /device:TPU:1, one launch (start us, length us, event | category | flops | bytes accessed | tf_op | source)
XLA Modules:
  0.0 153.4 jit_solution(17707211480729716367)
XLA Ops:
  6.5 0.0 copy-start.1
  6.5 0.0 copy-start
  6.5 0.0 copy-start.5
  6.5 0.0 all-gather.5.cloned.1.call-start
  6.5 16.2 %all_gather.18 = bf16[256,512]{1,0:T(8,128)(2,1)} all-gather(bf16[64,512]{1,0:T(8,128)(2,1)} %bitcast.9), channel_id=1, replica_groups={{0,16,32,48},{8,24,40,56},{64,80,96,112},{72,88,104,120},{128,144,160,1..., dimensions={0}, use_global_device_ids=true | all-gather | bytes 327680 | tf_op jit(solution)/shard_map/all_gather | solution.py:267
  22.7 0.0 all-gather.5.cloned.1.call-update
  22.7 0.0 all-gather.7.cloned.1.call-start
  22.8 0.7 constant_dynamic-update-slice_fusion.1
  23.5 0.7 constant_dynamic-update-slice_fusion
  24.3 0.8 maximum_maximum_fusion
  25.1 13.1 %all_gather.21 = bf16[384,512]{1,0:T(8,128)(2,1)} all-gather(bf16[96,512]{1,0:T(8,128)(2,1)S(1)} %maximum_maximum_fusion), channel_id=1, replica_groups={{0,16,32,48},{8,24,40,56},{64,80,96,112},{72,88,104,120},{128,144,160,1..., dimensions={0}, use_global_device_ids=true | all-gather | bytes 491520 | tf_op jit(solution)/shard_map/all_gather | solution.py:267
  38.2 0.0 all-gather.7.cloned.1.call-update
  38.2 0.8 copy.12.index_ref
  39.0 0.0 copy-done.1
  39.1 0.0 copy-done
  39.1 0.0 copy-start.2
  39.1 0.9 copy-done.2
  40.0 0.0 copy-start.3
  40.0 0.9 copy-done.3
  40.9 1.8 %lower.1.own_ref.hid_ref = bf16[256,1024]{1,0:T(8,128)(2,1)S(1)} custom-call(s32[256,1]{1,0:T(8,128)S(1)} %copy.12.index_ref, bf16[512,512]{1,0:T(8,128)(2,1)S(1)} %copy-done, bf16[512,128]{1,0:T(8,128)(2,1)S(1)} %copy-done.2, bf16[512,128]{1,0:T(8,128)(2,1)S(1)} %copy-done.3, bf16[512,512]{1,0:T(8,128)(2,1)S(1)} %copy-done.1), custom_call_target="tpu_custom_call" | custom-call | tf_op jit(solution)/shard_map/lower/pallas_call | solution.py:72
  42.6 3.3 %collective-permute-start = (bf16[256,1024]{1,0:T(8,128)(2,1)S(1)}, bf16[256,1024]{1,0:T(8,128)(2,1)S(1)}, u32[]{:S(2)}, u32[]{:S(2)}) collective-permute-start(bf16[256,1024]{1,0:T(8,128)(2,1)S(1)} %lower.1.own_ref.hid_ref), channel_id=1, source_target_pairs={{0,8},{8,0},{16,24},{24,16},{32,40},{40,32},{48,56},{56,48},{64,72... | collective-permute-start | bytes 1572872 | tf_op jit(solution)/shard_map/ppermute | solution.py:294
  46.0 0.0 copy-done.5
  46.0 0.6 fusion.1
  46.6 1.4 pad_add_fusion.place_ref
  48.0 5.0 %collective-permute-done.pair_ref.hid_pair_ref = bf16[256,1024]{1,0:T(8,128)(2,1)S(1)} collective-permute-done((bf16[256,1024]{1,0:T(8,128)(2,1)S(1)}, bf16[256,1024]{1,0:T(8,128)(2,1)S(1)}, u32[]{:S(2)}, u32[]{:S(2)}) %collective-permute-start) | collective-permute-done | bytes 524320 | tf_op jit(solution)/shard_map/ppermute | solution.py:294
  53.0 15.6 %all-gather.5.cloned.1.call-done = bf16[2048,512]{1,0:T(8,128)(2,1)} async-done(((bf16[256,512]{1,0:T(8,128)(2,1)}), bf16[2048,512]{1,0:T(8,128)(2,1)}) %all-gather.5.cloned.1.call-update) | async-done | bytes 2097168 | tf_op jit(solution)/shard_map/all_gather | solution.py:268
  68.6 3.6 %project.1 = (f32[4,512,256]{2,1,0:T(8,128)S(1)}, bf16[4,512,256]{2,1,0:T(8,128)(2,1)S(1)}) custom-call(s32[4]{0:T(128)S(1)} %pad_add_fusion.place_ref, bf16[256,1024]{1,0:T(8,128)(2,1)S(1)} %lower.1.own_ref.hid_ref, bf16[256,1024]{1,0:T(8,128)(2,1)S(1)} %collective-permute-done.pair_ref.hid_pair_ref, bf16[8,256,512]{2,1,0:T(8,128)(2,1)} %bitcast.8), custom_call_target="tpu_custom_call" | custom-call | tf_op jit(solution)/shard_map/project/pallas_call | solution.py:93
  72.2 5.9 %collective-permute-start.1 = (bf16[4,512,256]{2,1,0:T(8,128)(2,1)S(1)}, bf16[4,512,256]{2,1,0:T(8,128)(2,1)S(1)}, u32[]{:S(2)}, u32[]{:S(2)}) collective-permute-start(bf16[4,512,256]{2,1,0:T(8,128)(2,1)S(1)} %get-tuple-element.12), channel_id=1, source_target_pairs={{0,1},{1,0},{2,3},{3,2},{4,5},{5,4},{6,7},{7,6},{8,9},{9,8},{10,11... | collective-permute-start | bytes 3145736 | tf_op jit(solution)/shard_map/ppermute | solution.py:302
  78.1 2.3 %collective-permute-done.1 = bf16[4,512,256]{2,1,0:T(8,128)(2,1)S(1)} collective-permute-done((bf16[4,512,256]{2,1,0:T(8,128)(2,1)S(1)}, bf16[4,512,256]{2,1,0:T(8,128)(2,1)S(1)}, u32[]{:S(2)}, u32[]{:S(2)}) %collective-permute-start.1) | collective-permute-done | bytes 1048608 | tf_op jit(solution)/shard_map/ppermute | solution.py:302
  80.4 0.3 add_convert_fusion
  80.7 18.6 %all_to_all.10.parts_ref = bf16[4,512,256]{2,1,0:T(8,128)(2,1)S(1)} all-to-all(bf16[4,512,256]{2,1,0:T(8,128)(2,1)S(1)} %add_convert_fusion), channel_id=1, replica_groups={{0,2,4,6},{1,3,5,7},{8,10,12,14},{9,11,13,15},{16,18,20,22},{17,19,21,2..., dimensions={0} | all-to-all | bytes 2097152 | tf_op jit(solution)/shard_map/all_to_all | solution.py:304
  99.3 0.0 copy-start.4
  99.3 0.9 state.1
  100.2 15.8 %all_to_all.11.mine_ref = bf16[4,512,256]{2,1,0:T(8,128)(2,1)S(1)} all-to-all(bf16[4,512,256]{2,1,0:T(8,128)(2,1)S(1)} %state.1), channel_id=1, replica_groups={{0,2,4,6},{1,3,5,7},{8,10,12,14},{9,11,13,15},{16,18,20,22},{17,19,21,2..., dimensions={0} | all-to-all | bytes 2097152 | tf_op jit(solution)/shard_map/all_to_all | solution.py:262
  116.0 4.6 %collective-permute-start.2 = (bf16[4,512,256]{2,1,0:T(8,128)(2,1)S(1)}, bf16[4,512,256]{2,1,0:T(8,128)(2,1)S(1)}, u32[]{:S(2)}, u32[]{:S(2)}) collective-permute-start(bf16[4,512,256]{2,1,0:T(8,128)(2,1)S(1)} %all_to_all.11.mine_ref), channel_id=1, source_target_pairs={{0,1},{1,0},{2,3},{3,2},{4,5},{5,4},{6,7},{7,6},{8,9},{9,8},{10,11... | collective-permute-start | bytes 3145736 | tf_op jit(solution)/shard_map/ppermute | solution.py:263
  120.6 0.0 copy-done.4
  120.6 0.1 reshape.15
  120.7 0.1 dynamic-slice_reduce_fusion
  120.8 0.1 reshape.16.gain_ref
  120.9 0.1 all-gather.7.cloned.1.call-done
  121.0 1.9 %collective-permute-done.2.other_ref = bf16[4,512,256]{2,1,0:T(8,128)(2,1)S(1)} collective-permute-done((bf16[4,512,256]{2,1,0:T(8,128)(2,1)S(1)}, bf16[4,512,256]{2,1,0:T(8,128)(2,1)S(1)}, u32[]{:S(2)}, u32[]{:S(2)}) %collective-permute-start.2) | collective-permute-done | bytes 1048608 | tf_op jit(solution)/shard_map/ppermute | solution.py:263
  122.9 4.4 %qkv.1 = (f32[256,768]{1,0:T(8,128)S(1)}, f32[256,256]{1,0:T(8,128)S(1)}, f32[512,128]{1,0:T(8,128)S(1)}, bf16[256,1152]{1,0:T(8,128)(2,1)S(1)}) custom-call(s32[4]{0:T(128)S(1)} %pad_add_fusion.place_ref, bf16[4,512,256]{2,1,0:T(8,128)(2,1)S(1)} %all_to_all.11.mine_ref, bf16[4,512,256]{2,1,0:T(8,128)(2,1)S(1)} %collective-permute-done.2.other_ref, ...), custom_call_target="tpu_custom_call" | custom-call | tf_op jit(solution)/shard_map/qkv/pallas_call | solution.py:193
  127.3 3.0 %collective-permute-start.3 = (bf16[256,1152]{1,0:T(8,128)(2,1)S(1)}, bf16[256,1152]{1,0:T(8,128)(2,1)S(1)}, u32[]{:S(2)}, u32[]{:S(2)}) collective-permute-start(bf16[256,1152]{1,0:T(8,128)(2,1)S(1)} %get-tuple-element.16), channel_id=1, source_target_pairs={{0,8},{8,0},{16,24},{24,16},{32,40},{40,32},{48,56},{56,48},{64,72... | collective-permute-start | bytes 1769480 | tf_op jit(solution)/shard_map/ppermute | solution.py:311
  130.3 13.4 %collective-permute-done.3.got_ref = bf16[256,1152]{1,0:T(8,128)(2,1)S(1)} collective-permute-done((bf16[256,1152]{1,0:T(8,128)(2,1)S(1)}, bf16[256,1152]{1,0:T(8,128)(2,1)S(1)}, u32[]{:S(2)}, u32[]{:S(2)}) %collective-permute-start.3) | collective-permute-done | bytes 589856 | tf_op jit(solution)/shard_map/ppermute | solution.py:311
  143.7 2.8 %upper.1 = bf16[256,512]{1,0:T(8,128)(2,1)} custom-call(s32[4]{0:T(128)S(1)} %pad_add_fusion.place_ref, f32[256,768]{1,0:T(8,128)S(1)} %get-tuple-element.13.own_ref, f32[256,256]{1,0:T(8,128)S(1)} %get-tuple-element.14.pair_kv_ref, f32[512,128]{1,0:T(8,128)S(1)} %get-tuple-element.15.square_ref, bf16[256,1152]{1,0:T(8,128)(2,1)S(1)} %collective-permute-done.3.got_ref), custom_call_target="tpu_custom_call" | custom-call | tf_op jit(solution)/shard_map/upper/pallas_call | solution.py:252
  (1 shorter events, 0.0 us)
Async XLA Ops:
  6.5 32.5 %copy-start.1 = (bf16[512,512]{1,0:T(8,128)(2,1)S(1)}, bf16[512,512]{1,0:T(8,128)(2,1)}, u32[]{:S(2)}) copy-start(bf16[512,512]{1,0:T(8,128)(2,1)} %hidden_ref.1) | copy-start | bytes 1572868
  6.5 32.5 %copy-start = (bf16[512,512]{1,0:T(8,128)(2,1)S(1)}, bf16[512,512]{1,0:T(8,128)(2,1)}, u32[]{:S(2)}) copy-start(bf16[512,512]{1,0:T(8,128)(2,1)} %q_ref.1) | copy-start | bytes 1572868
  6.5 39.5 %copy-start.5 = (s32[64]{0:T(128)S(1)}, s32[64]{0:T(128)}, u32[]{:S(2)}) copy-start(s32[64]{0:T(128)} %param.21) | copy-start | bytes 772
  6.5 62.0 %all-gather.5.cloned.1.call-start = ((), (), s32[]{:S(2)}) async-start(), calls=%async_computation.2 | async-start | bytes 2359296 | tf_op jit(solution)/shard_map/all_gather | solution.py:268
  22.7 98.2 %all-gather.7.cloned.1.call-start = ((), (), s32[]{:S(2)}) async-start(), calls=%async_computation.3 | async-start | bytes 3538944 | tf_op jit(solution)/shard_map/all_gather | solution.py:268
  39.1 0.9 copy-start.2
  40.0 0.9 copy-start.3
  42.6 10.3 %collective-permute-start = (bf16[256,1024]{1,0:T(8,128)(2,1)S(1)}, bf16[256,1024]{1,0:T(8,128)(2,1)S(1)}, u32[]{:S(2)}, u32[]{:S(2)}) collective-permute-start(bf16[256,1024]{1,0:T(8,128)(2,1)S(1)} %lower.1.own_ref.hid_ref), channel_id=1, source_target_pairs={{0,8},{8,0},{16,24},{24,16},{32,40},{40,32},{48,56},{56,48},{64,72... | collective-permute-start | bytes 1572872 | tf_op jit(solution)/shard_map/ppermute | solution.py:294
  72.2 8.2 %collective-permute-start.1 = (bf16[4,512,256]{2,1,0:T(8,128)(2,1)S(1)}, bf16[4,512,256]{2,1,0:T(8,128)(2,1)S(1)}, u32[]{:S(2)}, u32[]{:S(2)}) collective-permute-start(bf16[4,512,256]{2,1,0:T(8,128)(2,1)S(1)} %get-tuple-element.12), channel_id=1, source_target_pairs={{0,1},{1,0},{2,3},{3,2},{4,5},{5,4},{6,7},{7,6},{8,9},{9,8},{10,11... | collective-permute-start | bytes 3145736 | tf_op jit(solution)/shard_map/ppermute | solution.py:302
  99.3 21.3 %copy-start.4 = (f32[4096]{0:T(1024)S(1)}, f32[4096]{0:T(1024)}, u32[]{:S(2)}) copy-start(f32[4096]{0:T(1024)} %param.16) | copy-start | bytes 49156
  116.0 6.9 %collective-permute-start.2 = (bf16[4,512,256]{2,1,0:T(8,128)(2,1)S(1)}, bf16[4,512,256]{2,1,0:T(8,128)(2,1)S(1)}, u32[]{:S(2)}, u32[]{:S(2)}) collective-permute-start(bf16[4,512,256]{2,1,0:T(8,128)(2,1)S(1)} %all_to_all.11.mine_ref), channel_id=1, source_target_pairs={{0,1},{1,0},{2,3},{3,2},{4,5},{5,4},{6,7},{7,6},{8,9},{9,8},{10,11... | collective-permute-start | bytes 3145736 | tf_op jit(solution)/shard_map/ppermute | solution.py:263
  127.3 16.4 %collective-permute-start.3 = (bf16[256,1152]{1,0:T(8,128)(2,1)S(1)}, bf16[256,1152]{1,0:T(8,128)(2,1)S(1)}, u32[]{:S(2)}, u32[]{:S(2)}) collective-permute-start(bf16[256,1152]{1,0:T(8,128)(2,1)S(1)} %get-tuple-element.16), channel_id=1, source_target_pairs={{0,8},{8,0},{16,24},{24,16},{32,40},{40,32},{48,56},{56,48},{64,72... | collective-permute-start | bytes 1769480 | tf_op jit(solution)/shard_map/ppermute | solution.py:311
Sparse Core Ops, SparseCore 0:
  22.9 45.6 all-gather.4
  70.6 50.2 all-gather.6

commit v3 on v2

v3 whole, which is shorter than its diff:
```python
import functools

import jax
import jax.numpy as jnp
from jax import lax
from jax.experimental import pallas as pl
from jax.experimental.pallas import tpu as pltpu
from jax.sharding import PartitionSpec as P

D = 4096
HEADS = 32
KV_HEADS = 8
HD = 128
BLOCK = 512
KMAX = 256
GROUP = HEADS // KV_HEADS
N_Z = 8
N_Y = 8
N_X = 4
STRIP = D // (N_Z * N_Y)
HALF = N_Y // 2 * STRIP
QW = GROUP * HD
KVW = 2 * HD
LOG2E = 1.4426950408889634
SCALE = HD**-0.5 * LOG2E
NEG = -1e30
VMEM_LIMIT = 48 * 1024 * 1024

Z_GROUPS = [[z * N_Y + y for z in range(N_Z)] for y in range(N_Y)]
X_GROUPS = [[2 * x + c for x in range(N_X)] for c in range(2)]
CORE_SWAP = [(i, i ^ 1) for i in range(2 * N_X)]
SIBLING_SWAP = [(i, i ^ 1) for i in range(N_Z * N_Y)]
PARITY_GROUPS = [[z * N_Y + 2 * p + q for p in range(N_Y // 2)] for z in range(N_Z) for q in range(2)]


def params():
    return pltpu.CompilerParams(vmem_limit_bytes=VMEM_LIMIT)


def dot(a, b):
    return jnp.dot(a, b, preferred_element_type=jnp.float32)


def dot_t(a, b):
    return lax.dot_general(a, b, (((1,), (1,)), ((), ())), preferred_element_type=jnp.float32)


def attend(scores, values):
    top = jnp.max(scores, axis=1, keepdims=True)
    unnormed = jnp.exp2(scores - top)
    total = jnp.sum(unnormed, axis=1, keepdims=True)
    return dot(unnormed.astype(jnp.bfloat16), values) / total


def lower_kernel(index_ref, q_ref, k_ref, v_ref, hidden_ref, gain_ref, inverse_ref, out_ref):
    index = index_ref[...]
    column = lax.broadcasted_iota(jnp.int32, (KMAX, BLOCK), 1)
    pick = (column == index).astype(jnp.bfloat16)
    causal = column <= index
    queries = dot(pick, q_ref[...]).astype(jnp.bfloat16)
    keys = k_ref[...]
    values = v_ref[...]
    for g in range(GROUP):
        cols = slice(g * HD, (g + 1) * HD)
        scores = jnp.where(causal, dot_t(queries[:, cols], keys) * SCALE, NEG)
        out_ref[:, cols] = attend(scores, values).astype(jnp.bfloat16)
    out_ref[:, QW:] = dot(pick, hidden_ref[...]).astype(jnp.bfloat16)


def lower(index, queries, keys, values, hidden, gain, inverse):
    return pl.pallas_call(
        lower_kernel,
        in_specs=[pl.BlockSpec(memory_space=pltpu.VMEM)] * 5 + [pl.BlockSpec(memory_space=pl.ANY)] * 2,
        out_shape=jax.ShapeDtypeStruct((KMAX, 2 * QW), jnp.bfloat16),
        compiler_params=params(),
        name="lower",
    )(index, queries, keys, values, hidden, gain, inverse)


def project_kernel(other, place_ref, own_ref, pair_ref, weight_ref, out_ref):
    core = 1 - place_ref[0] if other else place_ref[0]
    own = own_ref[:, :QW]
    pair = pair_ref[:, :QW]
    for x in range(N_X):
        weights = weight_ref[2 * x + core]
        out_ref[x, :KMAX] = dot_t(own, weights).astype(out_ref.dtype)
        out_ref[x, KMAX:] = dot_t(pair, weights).astype(out_ref.dtype)


def project(place, kept, kept_pair, weights, other):
    return pl.pallas_call(
        functools.partial(project_kernel, other),
        in_specs=[pl.BlockSpec(memory_space=pltpu.SMEM)] + [pl.BlockSpec(memory_space=pltpu.VMEM)] * 3,
        out_specs=pl.BlockSpec(memory_space=pltpu.VMEM),
        out_shape=jax.ShapeDtypeStruct(
            (N_X, 2 * KMAX, HALF), jnp.bfloat16 if other else jnp.float32
        ),
        compiler_params=params(),
        cost_estimate=pl.CostEstimate(flops=2**30 // 2, bytes_accessed=2**20, transcendentals=0),
        name="project_other" if other else "project_mine",
    )(place, kept, kept_pair, weights)


def state_kernel(place_ref, parts_ref, hid_ref, hid_pair_ref, gain_ref, out_ref):
    gain = gain_ref[place_ref[4]]
    parity = place_ref[1]
    row = lax.broadcasted_iota(jnp.int32, (QW, HALF), 0)
    col = lax.broadcasted_iota(jnp.int32, (QW, HALF), 1)
    source = (col // STRIP) * (2 * STRIP) + parity * STRIP + col % STRIP
    pick = (row == source).astype(jnp.bfloat16)
    for half, hid in enumerate((hid_ref, hid_pair_ref)):
        rows = slice(half * KMAX, (half + 1) * KMAX)
        total = dot(hid[...], pick)
        for x in range(N_X):
            total += parts_ref[x, rows].astype(jnp.float32)
        state = total.astype(jnp.bfloat16).astype(jnp.float32)
        scaled = (state * gain).astype(jnp.bfloat16)
        for x in range(N_X):
            out_ref[x, rows] = scaled


def add_up(place, parts, kept, kept_pair, gain):
    shape = (N_X, 2 * KMAX, HALF)
    hidden = pl.BlockSpec((KMAX, QW), lambda i: (0, 1))
    return pl.pallas_call(
        state_kernel,
        grid=(1,),
        in_specs=[
            pl.BlockSpec(memory_space=pltpu.SMEM),
            pl.BlockSpec(shape, lambda i: (0, 0, 0)),
            hidden,
            hidden,
            pl.BlockSpec((2 * N_X, 1, HALF), lambda i: (0, 0, 0)),
        ],
        out_specs=pl.BlockSpec(shape, lambda i: (0, 0, 0)),
        out_shape=jax.ShapeDtypeStruct(shape, jnp.bfloat16),
        compiler_params=params(),
        name="state",
    )(place, parts, kept, kept_pair, gain)


def by_core(core):
    return [2 * x + core for x in range(N_X)] + [2 * x + 1 - core for x in range(N_X)]


OWN = slice(0, KMAX)
PAIR = slice(KMAX, 2 * KMAX)


def contract(rows, mine_ref, other_ref, weights):
    state = [ref[x, rows] for ref in (mine_ref, other_ref) for x in range(N_X)]
    return dot(jnp.concatenate(state, axis=1), weights)


def kv_kernel(place_ref, mine_ref, other_ref, weight_ref, keep_ref, send_ref):
    heads = by_core(place_ref[0])
    weights = jnp.concatenate([weight_ref[head, :, QW:] for head in heads], axis=0)
    for half, rows in enumerate((OWN, PAIR)):
        sums = contract(rows, mine_ref, other_ref, weights)
        keep_ref[rows] = sums
        send_ref[:, (1 - half) * KVW : (2 - half) * KVW] = sums.astype(jnp.bfloat16)
    weights = jnp.concatenate([weight_ref[head, :, :HD] for head in heads], axis=0)
    sums = contract(PAIR, mine_ref, other_ref, weights)
    send_ref[:, 2 * KVW :] = sums.astype(jnp.bfloat16)


def project_kv(place, mine, other, weights):
    return pl.pallas_call(
        kv_kernel,
        in_specs=[pl.BlockSpec(memory_space=pltpu.SMEM)] + [pl.BlockSpec(memory_space=pltpu.VMEM)] * 3,
        out_specs=[pl.BlockSpec(memory_space=pltpu.VMEM)] * 2,
        out_shape=[
            jax.ShapeDtypeStruct((2 * KMAX, KVW), jnp.float32),
            jax.ShapeDtypeStruct((KMAX, 2 * KVW + HD), jnp.bfloat16),
        ],
        compiler_params=params(),
        name="project_kv",
    )(place, mine, other, weights)


def q_kernel(
    place_ref, mine_ref, other_ref, weight_ref, inverse_ref, first_ref, keep_ref, square_ref, send_ref
):
    heads = by_core(place_ref[0])
    weights = jnp.concatenate([weight_ref[head, :, HD:QW] for head in heads], axis=0)
    sums = contract(PAIR, mine_ref, other_ref, weights)
    send_ref[:, : QW - HD] = sums.astype(jnp.bfloat16)
    squares = jnp.zeros((2 * KMAX, HD), jnp.float32)
    for i, head in enumerate(heads):
        scaled = (mine_ref if i < N_X else other_ref)[i % N_X].astype(jnp.float32)
        square = scaled * scaled * inverse_ref[head]
        squares += square[:, :HD] + square[:, HD:]
    total = jnp.sum(squares, axis=1, keepdims=True)
    square_ref[...] = jnp.broadcast_to(total, square_ref.shape)
    high = total.astype(jnp.bfloat16).astype(jnp.float32)
    low = total - high
    lane = lax.broadcasted_iota(jnp.int32, (KMAX, HD), 1)
    tail = jnp.where(
        lane == 0,
        high[PAIR],
        jnp.where(lane == 1, low[PAIR], jnp.where(lane == 2, high[OWN], low[OWN])),
    )
    send_ref[:, QW - HD :] = tail.astype(jnp.bfloat16)
    weights = jnp.concatenate([weight_ref[head, :, :QW] for head in heads], axis=0)
    keep_ref[...] = contract(OWN, mine_ref, other_ref, weights)


def project_q(place, mine, other, weights, inverse, first):
    return pl.pallas_call(
        q_kernel,
        in_specs=[pl.BlockSpec(memory_space=pltpu.SMEM)]
        + [pl.BlockSpec(memory_space=pltpu.VMEM)] * 4
        + [pl.BlockSpec(memory_space=pl.ANY)],
        out_specs=[pl.BlockSpec(memory_space=pltpu.VMEM)] * 3,
        out_shape=[
            jax.ShapeDtypeStruct((KMAX, QW), jnp.float32),
            jax.ShapeDtypeStruct((2 * KMAX, HD), jnp.float32),
            jax.ShapeDtypeStruct((KMAX, QW), jnp.bfloat16),
        ],
        compiler_params=params(),
        cost_estimate=pl.CostEstimate(flops=2**30, bytes_accessed=2**22, transcendentals=0),
        name="project_q",
    )(place, mine, other, weights, inverse, first)


def upper_kernel(place_ref, q_ref, kv_ref, square_ref, got_q_ref, got_kv_ref, out_ref):
    parity = place_ref[1]
    own_count = place_ref[2]
    left_count = place_ref[3]
    tail = got_q_ref[:, QW - HD :].astype(jnp.float32)
    own_sum = square_ref[:KMAX, :1] + (tail[:, 0:1] + tail[:, 1:2])
    pair_sum = square_ref[KMAX:, :1] + (tail[:, 2:3] + tail[:, 3:4])
    own_inv = lax.rsqrt(own_sum / D + 1e-05)
    pair_inv = lax.rsqrt(pair_sum / D + 1e-05)
    got = jnp.concatenate([got_kv_ref[:, 2 * KVW :], got_q_ref[:, : QW - HD]], axis=1)
    queries = ((q_ref[...] + got.astype(jnp.float32)) * own_inv).astype(jnp.bfloat16)
    own = (kv_ref[:KMAX] + got_kv_ref[:, :KVW].astype(jnp.float32)) * own_inv
    own = own.astype(jnp.bfloat16)
    pair = (kv_ref[KMAX:] + got_kv_ref[:, KVW : 2 * KVW].astype(jnp.float32)) * pair_inv
    pair = pair.astype(jnp.bfloat16)
    keys = jnp.concatenate([pair[:, :HD], own[:, :HD]], axis=0)
    values = jnp.concatenate([pair[:, HD:], own[:, HD:]], axis=0)
    row = lax.broadcasted_iota(jnp.int32, (KMAX, 2 * KMAX), 0)
    col = lax.broadcasted_iota(jnp.int32, (KMAX, 2 * KMAX), 1)
    from_left = col < left_count * parity
    from_own = (col >= KMAX) & (col - KMAX <= row) & (col - KMAX < own_count)
    allowed = from_left | from_own
    valid = lax.broadcasted_iota(jnp.int32, (KMAX, HD), 0) < own_count
    for g in range(GROUP):
        cols = slice(g * HD, (g + 1) * HD)
        scores = jnp.where(allowed, dot_t(queries[:, cols], keys) * SCALE, NEG)
        out_ref[:, cols] = jnp.where(valid, attend(scores, values), 0.0).astype(jnp.bfloat16)


def upper(place, q, kv, squares, got_q, got_kv):
    return pl.pallas_call(
        upper_kernel,
        in_specs=[pl.BlockSpec(memory_space=pltpu.SMEM)] + [pl.BlockSpec(memory_space=pltpu.VMEM)] * 5,
        out_shape=jax.ShapeDtypeStruct((KMAX, QW), jnp.bfloat16),
        compiler_params=params(),
        name="upper",
    )(place, q, kv, squares, got_q, got_kv)


def gather_head(x):
    mine = lax.all_to_all(x, "head", 0, 0, axis_index_groups=X_GROUPS, tiled=True)
    return mine, lax.ppermute(mine, "head", CORE_SWAP)


def per_device(
    hidden,
    queries,
    keys_low,
    values_low,
    out_weight,
    norm_gain,
    query_weight,
    key_weight,
    value_weight,
    keep_index,
    keep_count,
):
    seq = lax.axis_index("seq")
    parity = seq % 2
    head = lax.axis_index("head")
    core = head % 2
    own_count = lax.dynamic_index_in_dim(keep_count, seq, keepdims=False)
    left_count = lax.dynamic_index_in_dim(keep_count, jnp.maximum(seq - 1, 0), keepdims=False)
    place = jnp.stack([core, parity, own_count, left_count, head]).astype(jnp.int32)

    shard = out_weight.T
    shards = lax.all_to_all(
        jnp.broadcast_to(shard, (N_Y // 2,) + shard.shape),
        "seq",
        0,
        0,
        axis_index_groups=PARITY_GROUPS,
        tiled=True,
    )
    out_weights = lax.all_gather(
        shards.reshape(HALF, QW), "seq", axis=0, axis_index_groups=Z_GROUPS
    )

    gain = lax.dynamic_index_in_dim(
        norm_gain.reshape(8, N_Y // 2, 2, STRIP), parity, axis=2, keepdims=False
    ).reshape(8, 1, HALF)
    inverse = 1.0 / (gain * gain)
    index = keep_index.reshape(KMAX, 1)
    kept = lower(index, queries, keys_low, values_low, hidden, gain, inverse)
    kept_pair = lax.ppermute(kept, "seq", SIBLING_SWAP)

    shard = jnp.concatenate([query_weight, key_weight, value_weight], axis=1)
    shards = lax.all_gather(shard, "seq", axis=0, axis_index_groups=PARITY_GROUPS, tiled=True)
    qkv_weights = lax.all_gather(shards, "seq", axis=0, axis_index_groups=Z_GROUPS)

    send = project(place, kept, kept_pair, out_weights, True)
    got = lax.ppermute(send, "head", CORE_SWAP)
    keep = project(place, kept, kept_pair, out_weights, False)
    parts = (keep + got.astype(jnp.float32)).astype(jnp.bfloat16)
    parts = lax.all_to_all(parts, "head", 0, 0, axis_index_groups=X_GROUPS, tiled=True)
    mine, other = gather_head(add_up(place, parts, kept, kept_pair, gain))

    kv, send = project_kv(place, mine, other, qkv_weights)
    got_kv = lax.ppermute(send, "seq", SIBLING_SWAP)
    q, squares, send = project_q(place, mine, other, qkv_weights, inverse, kv)
    got_q = lax.ppermute(send, "seq", SIBLING_SWAP)
    return upper(place, q, kv, squares, got_q, got_kv)


def solution(mesh):
    in_specs = (
        P("seq", "head"),
        P("seq", "head"),
        P("seq", "head"),
        P("seq", "head"),
        P("head", "seq"),
        P(),
        P("seq", "head"),
        P("seq", "head"),
        P("seq", "head"),
        P("seq", None),
        P(),
    )
    out_specs = P("seq", "head")
    return jax.shard_map(
        per_device, mesh=mesh, in_specs=in_specs, out_specs=out_specs, check_vma=False
    )
```

time: 154 us -> 151 us (0.981)
  waiting for transfers between devices: 38.3 us -> 32.7 us
  local copies, waits for them, and re-layouts: 4.94 us -> 6.77 us
  blocking collectives: 63.6 us -> 65.4 us
    all_to_all x0 -> x1, blocking collectives: none -> 16.5 us  [per_device(): lax.all_to_all(jnp.broadcast_to(shard, (N_Y // 2,) + shard.shape), 'seq',...]
    all_gather x2 -> x1, blocking collectives: 29.3 us -> 14.5 us  [per_device(): lax.all_gather(shard, 'seq', axis=0, axis_index_groups=PARITY_GROUPS, til...]
    ppermute x1 -> x2, waiting for transfers between devices: 13.4 us -> 7.73 us  [the longest x1 7.72 us: per_device(): got_q = lax.ppermute(send, 'seq', SIBLING_SWAP)]
    ppermute x1 -> x2, starting transfers between devices: 3 us -> 5.28 us  [the longest x1 3.09 us: per_device(): got_kv = lax.ppermute(send, 'seq', SIBLING_SWAP)]
    unnamed x13 -> x18, local copies, waits for them, and re-layouts: 2.54 us -> 3.51 us
    pallas_call x3 -> x5, Pallas kernels: 9.8 us -> 9.4 us  [the longest x1 3.51 us: project_q(): pl.pallas_call(q_kernel, in_specs=[pl.BlockSpec(memory_space=pltpu.SMEM)]...]
  transfers between devices with their start and end apart: 6 -> 7, of which waited for: 6 -> 6; matrix products, arithmetic and copies ran while one was open for 4% -> 2% of each run, Pallas kernels for 4% -> 6%
where the time goes in v3:
time: 151 us
  blocking collectives  65.4 us (43%)
  waiting for transfers between devices  32.7 us (22%)
  starting transfers between devices  18 us (12%)
  between operations  13.6 us (9%)
  Pallas kernels  13.2 us (9%)
  local copies, waits for them, and re-layouts  6.77 us (4%)
    all_to_all x1, blocking collectives, per_device(): lax.all_to_all(parts, 'head', 0, 0, axis_index_groups=X_GROUPS, tiled=True)  18.6 us
    all_to_all x1, blocking collectives, per_device(): lax.all_to_all(jnp.broadcast_to(shard, (N_Y // 2,) + shard.shape), 'seq',...  16.5 us
    all_to_all x1, blocking collectives, gather_head(): lax.all_to_all(x, 'head', 0, 0, axis_index_groups=X_GROUPS, tiled=True)  15.8 us
    all_gather x1, waiting for transfers between devices, per_device(): lax.all_gather(shards.reshape(HALF, QW), 'seq', axis=0, axis_index_groups...  15.2 us
    all_gather x1, blocking collectives, per_device(): lax.all_gather(shard, 'seq', axis=0, axis_index_groups=PARITY_GROUPS, til...  14.5 us
    ppermute x1, waiting for transfers between devices, per_device(): got_q = lax.ppermute(send, 'seq', SIBLING_SWAP)  7.72 us
    ppermute x1, waiting for transfers between devices, per_device(): kept_pair = lax.ppermute(kept, 'seq', SIBLING_SWAP)  6.54 us
    ppermute x1, starting transfers between devices, per_device(): got = lax.ppermute(send, 'head', CORE_SWAP)  6.13 us
  transfers between devices with their start and end apart: 7, of which 6 were waited for; matrix products, arithmetic and copies ran while one was open for 2% of the time, Pallas kernels for 6%

profile of v3, /device:TPU:1, one launch (start us, length us, event | category | flops | bytes accessed | tf_op | source)
XLA Modules:
  0.0 150.9 jit_solution(9008075093536018060)
XLA Ops:
  6.5 0.0 copy-start.6
  6.5 0.0 copy-start.5
  6.6 0.0 all-gather.4.cloned.1.call-start
  6.6 1.0 broadcast_in_dim.3
  7.6 0.0 copy-start.7
  7.6 16.5 %all_to_all.15 = bf16[4,64,512]{2,1,0:T(8,128)(2,1)} all-to-all(bf16[4,64,512]{2,1,0:T(8,128)(2,1)S(1)} %broadcast_in_dim.3), channel_id=1, replica_groups={{0,16,32,48},{8,24,40,56},{64,80,96,112},{72,88,104,120},{128,144,160,1..., dimensions={0} | all-to-all | bytes 524288 | tf_op jit(solution)/shard_map/all_to_all | solution.py:292
  24.1 0.0 all-gather.4.cloned.1.call-update
  24.1 0.0 all-gather.6.cloned.1.call-start
  24.2 0.9 pad_maximum_fusion
  25.1 14.5 %all_gather.13 = bf16[256,768]{1,0:T(8,128)(2,1)} all-gather(bf16[64,768]{1,0:T(8,128)(2,1)S(1)} %pad_maximum_fusion), channel_id=1, replica_groups={{0,16,32,48},{8,24,40,56},{64,80,96,112},{72,88,104,120},{128,144,160,1..., dimensions={0}, use_global_device_ids=true | all-gather | bytes 491520 | tf_op jit(solution)/shard_map/all_gather | solution.py:313
  39.6 0.0 all-gather.6.cloned.1.call-update
  39.6 0.0 copy-done.6
  39.6 0.1 reshape.27
  39.7 0.1 dynamic-slice_reduce_fusion
  39.8 0.1 reshape.28.gain_ref
  39.9 0.0 copy-done.8
  39.9 0.1 copy.13.index_ref
  40.1 0.0 copy-done.3
  40.1 0.0 copy-done.2
  40.1 0.0 copy-done.4
  40.1 0.0 copy-done.5
  40.1 1.8 %lower.1.own_ref.hid_ref = bf16[256,1024]{1,0:T(8,128)(2,1)S(1)} custom-call(s32[256,1]{1,0:T(8,128)S(1)} %copy.13.index_ref, bf16[512,512]{1,0:T(8,128)(2,1)S(1)} %copy-done.2, bf16[512,128]{1,0:T(8,128)(2,1)S(1)} %copy-done.4, bf16[512,128]{1,0:T(8,128)(2,1)S(1)} %copy-done.5, bf16[512,512]{1,0:T(8,128)(2,1)S(1)} %copy-done.3, ...), custom_call_target="tpu_custom_call" | custom-call | tf_op jit(solution)/shard_map/lower/pallas_call | solution.py:71
  41.9 1.9 %collective-permute-start = (bf16[256,1024]{1,0:T(8,128)(2,1)S(1)}, bf16[256,1024]{1,0:T(8,128)(2,1)S(1)}, u32[]{:S(2)}, u32[]{:S(2)}) collective-permute-start(bf16[256,1024]{1,0:T(8,128)(2,1)S(1)} %lower.1.own_ref.hid_ref), channel_id=1, source_target_pairs={{0,8},{8,0},{16,24},{24,16},{32,40},{40,32},{48,56},{56,48},{64,72... | collective-permute-start | bytes 1572872 | tf_op jit(solution)/shard_map/ppermute | solution.py:310
  43.8 0.0 copy-done.7
  43.8 0.7 fusion
  44.5 1.3 stack.17.place_ref
  45.8 6.5 %collective-permute-done.pair_ref.hid_pair_ref = bf16[256,1024]{1,0:T(8,128)(2,1)S(1)} collective-permute-done((bf16[256,1024]{1,0:T(8,128)(2,1)S(1)}, bf16[256,1024]{1,0:T(8,128)(2,1)S(1)}, u32[]{:S(2)}, u32[]{:S(2)}) %collective-permute-start) | collective-permute-done | bytes 524320 | tf_op jit(solution)/shard_map/ppermute | solution.py:310
  52.3 15.2 %all-gather.4.cloned.1.call-done.weight_ref = bf16[8,256,512]{2,1,0:T(8,128)(2,1)} async-done(((bf16[1,256,512]{2,1,0:T(8,128)(2,1)}), bf16[8,256,512]{2,1,0:T(8,128)(2,1)}) %all-gather.4.cloned.1.call-update) | async-done | bytes 2097168 | tf_op jit(solution)/shard_map/all_gather | solution.py:300
  67.5 1.6 %copy-done.1 = bf16[8,256,512]{2,1,0:T(8,128)(2,1)S(1)} copy-done((bf16[8,256,512]{2,1,0:T(8,128)(2,1)S(1)}, bf16[8,256,512]{2,1,0:T(8,128)(2,1)}, u32[]{:S(2)}) %copy-start.1) | copy-done | bytes 2097176
  69.1 1.3 project_other.1
  70.4 6.1 %collective-permute-start.1 = (bf16[4,512,256]{2,1,0:T(8,128)(2,1)S(1)}, bf16[4,512,256]{2,1,0:T(8,128)(2,1)S(1)}, u32[]{:S(2)}, u32[]{:S(2)}) collective-permute-start(bf16[4,512,256]{2,1,0:T(8,128)(2,1)S(1)} %project_other.1), channel_id=1, source_target_pairs={{0,1},{1,0},{2,3},{3,2},{4,5},{5,4},{6,7},{7,6},{8,9},{9,8},{10,11... | collective-permute-start | bytes 3145736 | tf_op jit(solution)/shard_map/ppermute | solution.py:317
  76.5 1.3 project_mine.1
  77.8 1.0 collective-permute-done.1
  78.8 0.3 add_convert_fusion
  79.1 18.6 %all_to_all.16.parts_ref = bf16[4,512,256]{2,1,0:T(8,128)(2,1)S(1)} all-to-all(bf16[4,512,256]{2,1,0:T(8,128)(2,1)S(1)} %add_convert_fusion), channel_id=1, replica_groups={{0,2,4,6},{1,3,5,7},{8,10,12,14},{9,11,13,15},{16,18,20,22},{17,19,21,2..., dimensions={0} | all-to-all | bytes 2097152 | tf_op jit(solution)/shard_map/all_to_all | solution.py:320
  97.7 1.0 state.1
  98.6 15.8 %all_to_all.17.mine_ref = bf16[4,512,256]{2,1,0:T(8,128)(2,1)S(1)} all-to-all(bf16[4,512,256]{2,1,0:T(8,128)(2,1)S(1)} %state.1), channel_id=1, replica_groups={{0,2,4,6},{1,3,5,7},{8,10,12,14},{9,11,13,15},{16,18,20,22},{17,19,21,2..., dimensions={0} | all-to-all | bytes 2097152 | tf_op jit(solution)/shard_map/all_to_all | solution.py:266
  114.4 4.6 %collective-permute-start.2 = (bf16[4,512,256]{2,1,0:T(8,128)(2,1)S(1)}, bf16[4,512,256]{2,1,0:T(8,128)(2,1)S(1)}, u32[]{:S(2)}, u32[]{:S(2)}) collective-permute-start(bf16[4,512,256]{2,1,0:T(8,128)(2,1)S(1)} %all_to_all.17.mine_ref), channel_id=1, source_target_pairs={{0,1},{1,0},{2,3},{3,2},{4,5},{5,4},{6,7},{7,6},{8,9},{9,8},{10,11... | collective-permute-start | bytes 3145736 | tf_op jit(solution)/shard_map/ppermute | solution.py:267
  119.0 1.1 all-gather.6.cloned.1.call-done
  120.1 1.1 collective-permute-done.2.other_ref
  121.3 1.9 %copy-done = bf16[2048,768]{1,0:T(8,128)(2,1)S(1)} copy-done((bf16[2048,768]{1,0:T(8,128)(2,1)S(1)}, bf16[2048,768]{1,0:T(8,128)(2,1)}, u32[]{:S(2)}) %copy-start) | copy-done | bytes 3145752
  123.2 1.5 %project_kv.1 = (f32[512,256]{1,0:T(8,128)S(1)}, bf16[256,640]{1,0:T(8,128)(2,1)S(1)}) custom-call(s32[5]{0:T(128)S(1)} %stack.17.place_ref, bf16[4,512,256]{2,1,0:T(8,128)(2,1)S(1)} %all_to_all.17.mine_ref, bf16[4,512,256]{2,1,0:T(8,128)(2,1)S(1)} %collective-permute-done.2.other_ref, bf16[8,256,768]{2,1,0:T(8,128)(2,1)S(1)} %bitcast.8), custom_call_target="tpu_custom_call" | custom-call | tf_op jit(solution)/shard_map/project_kv/pallas_call | solution.py:168
  124.7 3.1 %collective-permute-start.4 = (bf16[256,640]{1,0:T(8,128)(2,1)S(1)}, bf16[256,640]{1,0:T(8,128)(2,1)S(1)}, u32[]{:S(2)}, u32[]{:S(2)}) collective-permute-start(bf16[256,640]{1,0:T(8,128)(2,1)S(1)} %get-tuple-element.14), channel_id=1, source_target_pairs={{0,8},{8,0},{16,24},{24,16},{32,40},{40,32},{48,56},{56,48},{64,72... | collective-permute-start | bytes 983048 | tf_op jit(solution)/shard_map/ppermute | solution.py:324
  127.8 3.5 %project_q.1 = (f32[256,512]{1,0:T(8,128)S(1)}, f32[512,128]{1,0:T(8,128)S(1)}, bf16[256,512]{1,0:T(8,128)(2,1)S(1)}) custom-call(s32[5]{0:T(128)S(1)} %stack.17.place_ref, bf16[4,512,256]{2,1,0:T(8,128)(2,1)S(1)} %all_to_all.17.mine_ref, bf16[4,512,256]{2,1,0:T(8,128)(2,1)S(1)} %collective-permute-done.2.other_ref, bf16[8,256,768]{2,1,0:T(8,128)(2,1)} %bitcast.7, ...), custom_call_target="tpu_custom_call" | custom-call | flops 1073741824 | bytes 4194304 | tf_op jit(solution)/shard_map/project_q/pallas_call | solution.py:209
  131.3 2.2 %collective-permute-start.3 = (bf16[256,512]{1,0:T(8,128)(2,1)S(1)}, bf16[256,512]{1,0:T(8,128)(2,1)S(1)}, u32[]{:S(2)}, u32[]{:S(2)}) collective-permute-start(bf16[256,512]{1,0:T(8,128)(2,1)S(1)} %get-tuple-element.13), channel_id=1, source_target_pairs={{0,8},{8,0},{16,24},{24,16},{32,40},{40,32},{48,56},{56,48},{64,72... | collective-permute-start | bytes 786440 | tf_op jit(solution)/shard_map/ppermute | solution.py:326
  133.5 7.7 %collective-permute-done.3.got_q_ref = bf16[256,512]{1,0:T(8,128)(2,1)S(1)} collective-permute-done((bf16[256,512]{1,0:T(8,128)(2,1)S(1)}, bf16[256,512]{1,0:T(8,128)(2,1)S(1)}, u32[]{:S(2)}, u32[]{:S(2)}) %collective-permute-start.3) | collective-permute-done | bytes 262176 | tf_op jit(solution)/shard_map/ppermute | solution.py:326
  141.2 0.0 collective-permute-done.4.got_kv_ref
  141.2 2.8 %upper.1 = bf16[256,512]{1,0:T(8,128)(2,1)} custom-call(s32[5]{0:T(128)S(1)} %stack.17.place_ref, f32[256,512]{1,0:T(8,128)S(1)} %get-tuple-element.11.q_ref, f32[512,256]{1,0:T(8,128)S(1)} %get-tuple-element.10.first_ref.kv_ref, f32[512,128]{1,0:T(8,128)S(1)} %get-tuple-element.12.square_ref, bf16[256,512]{1,0:T(8,128)(2,1)S(1)} %collective-permute-done.3.got_q_ref, ...), custom_call_target="tpu_custom_call" | custom-call | tf_op jit(solution)/shard_map/upper/pallas_call | solution.py:256
  (7 shorter events, 0.0 us)
Async XLA Ops:
  6.5 33.1 %copy-start.6 = (f32[4096]{0:T(1024)S(1)}, f32[4096]{0:T(1024)}, u32[]{:S(2)}) copy-start(f32[4096]{0:T(1024)} %param.16) | copy-start | bytes 49156
  6.5 33.4 %copy-start.8 = (s32[1,256]{1,0:T(1,128)S(1)}, s32[1,256]{1,0:T(1,128)}, u32[]{:S(2)}) copy-start(s32[1,256]{1,0:T(1,128)} %param.20) | copy-start | bytes 3076
  6.5 33.5 %copy-start.3 = (bf16[512,512]{1,0:T(8,128)(2,1)S(1)}, bf16[512,512]{1,0:T(8,128)(2,1)}, u32[]{:S(2)}) copy-start(bf16[512,512]{1,0:T(8,128)(2,1)} %hidden_ref.1) | copy-start | bytes 1572868
  6.5 33.5 %copy-start.2 = (bf16[512,512]{1,0:T(8,128)(2,1)S(1)}, bf16[512,512]{1,0:T(8,128)(2,1)}, u32[]{:S(2)}) copy-start(bf16[512,512]{1,0:T(8,128)(2,1)} %q_ref.1) | copy-start | bytes 1572868
  6.5 33.5 %copy-start.4 = (bf16[512,128]{1,0:T(8,128)(2,1)S(1)}, bf16[512,128]{1,0:T(8,128)(2,1)}, u32[]{:S(2)}) copy-start(bf16[512,128]{1,0:T(8,128)(2,1)} %k_ref.1) | copy-start | bytes 393220
  6.5 33.6 %copy-start.5 = (bf16[512,128]{1,0:T(8,128)(2,1)S(1)}, bf16[512,128]{1,0:T(8,128)(2,1)}, u32[]{:S(2)}) copy-start(bf16[512,128]{1,0:T(8,128)(2,1)} %v_ref.1) | copy-start | bytes 393220
  6.6 60.9 %all-gather.4.cloned.1.call-start = ((), (), s32[]{:S(2)}) async-start(), calls=%async_computation.3 | async-start | bytes 2359296 | tf_op jit(solution)/shard_map/all_gather | solution.py:300
  7.6 36.3 %copy-start.7 = (s32[64]{0:T(128)S(1)}, s32[64]{0:T(128)}, u32[]{:S(2)}) copy-start(s32[64]{0:T(128)} %param.21) | copy-start | bytes 772
  24.1 96.0 %all-gather.6.cloned.1.call-start = ((), (), s32[]{:S(2)}) async-start(), calls=%async_computation.4 | async-start | bytes 3538944 | tf_op jit(solution)/shard_map/all_gather | solution.py:314
  41.9 10.4 %collective-permute-start = (bf16[256,1024]{1,0:T(8,128)(2,1)S(1)}, bf16[256,1024]{1,0:T(8,128)(2,1)S(1)}, u32[]{:S(2)}, u32[]{:S(2)}) collective-permute-start(bf16[256,1024]{1,0:T(8,128)(2,1)S(1)} %lower.1.own_ref.hid_ref), channel_id=1, source_target_pairs={{0,8},{8,0},{16,24},{24,16},{32,40},{40,32},{48,56},{56,48},{64,72... | collective-permute-start | bytes 1572872 | tf_op jit(solution)/shard_map/ppermute | solution.py:310
  67.5 1.6 %copy-start.1 = (bf16[8,256,512]{2,1,0:T(8,128)(2,1)S(1)}, bf16[8,256,512]{2,1,0:T(8,128)(2,1)}, u32[]{:S(2)}) copy-start(bf16[8,256,512]{2,1,0:T(8,128)(2,1)} %all-gather.4.cloned.1.call-done.weight_ref) | copy-start | bytes 6291460
  70.4 8.4 %collective-permute-start.1 = (bf16[4,512,256]{2,1,0:T(8,128)(2,1)S(1)}, bf16[4,512,256]{2,1,0:T(8,128)(2,1)S(1)}, u32[]{:S(2)}, u32[]{:S(2)}) collective-permute-start(bf16[4,512,256]{2,1,0:T(8,128)(2,1)S(1)} %project_other.1), channel_id=1, source_target_pairs={{0,1},{1,0},{2,3},{3,2},{4,5},{5,4},{6,7},{7,6},{8,9},{9,8},{10,11... | collective-permute-start | bytes 3145736 | tf_op jit(solution)/shard_map/ppermute | solution.py:317
  114.4 6.9 %collective-permute-start.2 = (bf16[4,512,256]{2,1,0:T(8,128)(2,1)S(1)}, bf16[4,512,256]{2,1,0:T(8,128)(2,1)S(1)}, u32[]{:S(2)}, u32[]{:S(2)}) collective-permute-start(bf16[4,512,256]{2,1,0:T(8,128)(2,1)S(1)} %all_to_all.17.mine_ref), channel_id=1, source_target_pairs={{0,1},{1,0},{2,3},{3,2},{4,5},{5,4},{6,7},{7,6},{8,9},{9,8},{10,11... | collective-permute-start | bytes 3145736 | tf_op jit(solution)/shard_map/ppermute | solution.py:267
  121.3 1.9 %copy-start = (bf16[2048,768]{1,0:T(8,128)(2,1)S(1)}, bf16[2048,768]{1,0:T(8,128)(2,1)}, u32[]{:S(2)}) copy-start(bf16[2048,768]{1,0:T(8,128)(2,1)} %all-gather.6.cloned.1.call-done) | copy-start | bytes 9437188
  124.7 16.5 %collective-permute-start.4 = (bf16[256,640]{1,0:T(8,128)(2,1)S(1)}, bf16[256,640]{1,0:T(8,128)(2,1)S(1)}, u32[]{:S(2)}, u32[]{:S(2)}) collective-permute-start(bf16[256,640]{1,0:T(8,128)(2,1)S(1)} %get-tuple-element.14), channel_id=1, source_target_pairs={{0,8},{8,0},{16,24},{24,16},{32,40},{40,32},{48,56},{56,48},{64,72... | collective-permute-start | bytes 983048 | tf_op jit(solution)/shard_map/ppermute | solution.py:324
  131.3 9.9 %collective-permute-start.3 = (bf16[256,512]{1,0:T(8,128)(2,1)S(1)}, bf16[256,512]{1,0:T(8,128)(2,1)S(1)}, u32[]{:S(2)}, u32[]{:S(2)}) collective-permute-start(bf16[256,512]{1,0:T(8,128)(2,1)S(1)} %get-tuple-element.13), channel_id=1, source_target_pairs={{0,8},{8,0},{16,24},{24,16},{32,40},{40,32},{48,56},{56,48},{64,72... | collective-permute-start | bytes 786440 | tf_op jit(solution)/shard_map/ppermute | solution.py:326
Sparse Core Ops, SparseCore 0:
  24.3 43.1 all-gather.3
  69.5 50.5 all-gather.5

commit v4 on v3

--- a/solution.py
+++ b/solution.py
@@ -17,6 +17,7 @@
 N_Z = 8
 N_Y = 8
 N_X = 4
+TAIL = 16
 STRIP = D // (N_Z * N_Y)
 HALF = N_Y // 2 * STRIP
 QW = GROUP * HD
@@ -178,13 +179,13 @@
     )(place, mine, other, weights)
 
 
-def q_kernel(
-    place_ref, mine_ref, other_ref, weight_ref, inverse_ref, first_ref, keep_ref, square_ref, send_ref
+def sibling_kernel(
+    place_ref, mine_ref, other_ref, weight_ref, inverse_ref, first_ref, square_ref, send_ref
 ):
     heads = by_core(place_ref[0])
     weights = jnp.concatenate([weight_ref[head, :, HD:QW] for head in heads], axis=0)
     sums = contract(PAIR, mine_ref, other_ref, weights)
-    send_ref[:, : QW - HD] = sums.astype(jnp.bfloat16)
+    send_ref[:KMAX] = sums.astype(jnp.bfloat16)
     squares = jnp.zeros((2 * KMAX, HD), jnp.float32)
     for i, head in enumerate(heads):
         scaled = (mine_ref if i < N_X else other_ref)[i % N_X].astype(jnp.float32)
@@ -192,47 +193,78 @@
         squares += square[:, :HD] + square[:, HD:]
     total = jnp.sum(squares, axis=1, keepdims=True)
     square_ref[...] = jnp.broadcast_to(total, square_ref.shape)
-    high = total.astype(jnp.bfloat16).astype(jnp.float32)
-    low = total - high
-    lane = lax.broadcasted_iota(jnp.int32, (KMAX, HD), 1)
+    across = lax.dot_general(
+        jnp.ones((TAIL, HD), jnp.float32),
+        squares,
+        (((1,), (1,)), ((), ())),
+        precision=lax.Precision.HIGHEST,
+        preferred_element_type=jnp.float32,
+    )
+    high = across.astype(jnp.bfloat16).astype(jnp.float32)
+    low = across - high
+    row = lax.broadcasted_iota(jnp.int32, (TAIL, KMAX), 0)
     tail = jnp.where(
-        lane == 0,
-        high[PAIR],
-        jnp.where(lane == 1, low[PAIR], jnp.where(lane == 2, high[OWN], low[OWN])),
-    )
-    send_ref[:, QW - HD :] = tail.astype(jnp.bfloat16)
-    weights = jnp.concatenate([weight_ref[head, :, :QW] for head in heads], axis=0)
-    keep_ref[...] = contract(OWN, mine_ref, other_ref, weights)
-
-
-def project_q(place, mine, other, weights, inverse, first):
-    return pl.pallas_call(
-        q_kernel,
+        row == 0,
+        high[:, PAIR],
+        jnp.where(row == 1, low[:, PAIR], jnp.where(row == 2, high[:, OWN], low[:, OWN])),
+    )
+    send_ref[KMAX:] = jnp.concatenate([tail, tail[:, :HD]], axis=1).astype(jnp.bfloat16)
+
+
+def project_sibling(place, mine, other, weights, inverse, first):
+    return pl.pallas_call(
+        sibling_kernel,
         in_specs=[pl.BlockSpec(memory_space=pltpu.SMEM)]
         + [pl.BlockSpec(memory_space=pltpu.VMEM)] * 4
         + [pl.BlockSpec(memory_space=pl.ANY)],
-        out_specs=[pl.BlockSpec(memory_space=pltpu.VMEM)] * 3,
+        out_specs=[pl.BlockSpec(memory_space=pltpu.VMEM)] * 2,
         out_shape=[
-            jax.ShapeDtypeStruct((KMAX, QW), jnp.float32),
             jax.ShapeDtypeStruct((2 * KMAX, HD), jnp.float32),
-            jax.ShapeDtypeStruct((KMAX, QW), jnp.bfloat16),
+            jax.ShapeDtypeStruct((KMAX + TAIL, QW - HD), jnp.bfloat16),
         ],
         compiler_params=params(),
-        cost_estimate=pl.CostEstimate(flops=2**30, bytes_accessed=2**22, transcendentals=0),
+        cost_estimate=pl.CostEstimate(flops=2**29, bytes_accessed=2**22, transcendentals=0),
+        name="project_sibling",
+    )(place, mine, other, weights, inverse, first)
+
+
+def q_kernel(place_ref, mine_ref, other_ref, weight_ref, first_ref, out_ref):
+    heads = by_core(place_ref[0])
+    weights = jnp.concatenate([weight_ref[head, :, :QW] for head in heads], axis=0)
+    out_ref[...] = contract(OWN, mine_ref, other_ref, weights)
+
+
+def project_q(place, mine, other, weights, first):
+    return pl.pallas_call(
+        q_kernel,
+        in_specs=[pl.BlockSpec(memory_space=pltpu.SMEM)]
+        + [pl.BlockSpec(memory_space=pltpu.VMEM)] * 3
+        + [pl.BlockSpec(memory_space=pl.ANY)],
+        out_specs=pl.BlockSpec(memory_space=pltpu.VMEM),
+        out_shape=jax.ShapeDtypeStruct((KMAX, QW), jnp.float32),
+        compiler_params=params(),
+        cost_estimate=pl.CostEstimate(flops=2**29, bytes_accessed=2**22, transcendentals=0),
         name="project_q",
-    )(place, mine, other, weights, inverse, first)
+    )(place, mine, other, weights, first)
 
 
 def upper_kernel(place_ref, q_ref, kv_ref, square_ref, got_q_ref, got_kv_ref, out_ref):
     parity = place_ref[1]
     own_count = place_ref[2]
     left_count = place_ref[3]
-    tail = got_q_ref[:, QW - HD :].astype(jnp.float32)
-    own_sum = square_ref[:KMAX, :1] + (tail[:, 0:1] + tail[:, 1:2])
-    pair_sum = square_ref[KMAX:, :1] + (tail[:, 2:3] + tail[:, 3:4])
+    tail = got_q_ref[KMAX:, :KMAX].astype(jnp.float32)
+    same = lax.broadcasted_iota(jnp.int32, (KMAX, KMAX), 0) == lax.broadcasted_iota(
+        jnp.int32, (KMAX, KMAX), 1
+    )
+
+    def down(across):
+        return jnp.sum(jnp.where(same, across, 0.0), axis=1, keepdims=True)
+
+    own_sum = square_ref[:KMAX, :1] + down(tail[0:1] + tail[1:2])
+    pair_sum = square_ref[KMAX:, :1] + down(tail[2:3] + tail[3:4])
     own_inv = lax.rsqrt(own_sum / D + 1e-05)
     pair_inv = lax.rsqrt(pair_sum / D + 1e-05)
-    got = jnp.concatenate([got_kv_ref[:, 2 * KVW :], got_q_ref[:, : QW - HD]], axis=1)
+    got = jnp.concatenate([got_kv_ref[:, 2 * KVW :], got_q_ref[:KMAX]], axis=1)
     queries = ((q_ref[...] + got.astype(jnp.float32)) * own_inv).astype(jnp.bfloat16)
     own = (kv_ref[:KMAX] + got_kv_ref[:, :KVW].astype(jnp.float32)) * own_inv
     own = own.astype(jnp.bfloat16)
@@ -322,8 +354,9 @@
 
     kv, send = project_kv(place, mine, other, qkv_weights)
     got_kv = lax.ppermute(send, "seq", SIBLING_SWAP)
-    q, squares, send = project_q(place, mine, other, qkv_weights, inverse, kv)
+    squares, send = project_sibling(place, mine, other, qkv_weights, inverse, kv)
     got_q = lax.ppermute(send, "seq", SIBLING_SWAP)
+    q = project_q(place, mine, other, qkv_weights, send)
     return upper(place, q, kv, squares, got_q, got_kv)
 
 

time: 151 us -> 150 us (level)
  waiting for transfers between devices: 32.7 us -> 30.5 us
    pallas_call x0 -> x1, Pallas kernels: none -> 3.4 us  [project_sibling(): pl.pallas_call(sibling_kernel, in_specs=[pl.BlockSpec(memory_space=pltpu....]
    pallas_call x1, Pallas kernels: 3.51 us -> 1.25 us  [project_q(): pl.pallas_call(q_kernel, in_specs=[pl.BlockSpec(memory_space=pltpu.SMEM)]...]
    ppermute x1, waiting for transfers between devices: 7.72 us -> 5.5 us  [per_device(): got_q = lax.ppermute(send, 'seq', SIBLING_SWAP)]
    unnamed x18 -> x20, local copies, waits for them, and re-layouts: 3.51 us -> 3.51 us
  transfers between devices with their start and end apart: 7 -> 7, of which waited for: 6 -> 6; matrix products, arithmetic and copies ran while one was open for 2% -> 2% of each run, Pallas kernels for 6% -> 7%
where the time goes in v4:
time: 150 us
  blocking collectives  65.4 us (44%)
  waiting for transfers between devices  30.5 us (20%)
  starting transfers between devices  18 us (12%)
  Pallas kernels  14.4 us (10%)
  between operations  13.6 us (9%)
  local copies, waits for them, and re-layouts  6.76 us (5%)
    all_to_all x1, blocking collectives, per_device(): lax.all_to_all(parts, 'head', 0, 0, axis_index_groups=X_GROUPS, tiled=True)  18.6 us
    all_to_all x1, blocking collectives, per_device(): lax.all_to_all(jnp.broadcast_to(shard, (N_Y // 2,) + shard.shape), 'seq',...  16.5 us
    all_to_all x1, blocking collectives, gather_head(): lax.all_to_all(x, 'head', 0, 0, axis_index_groups=X_GROUPS, tiled=True)  15.8 us
    all_gather x1, waiting for transfers between devices, per_device(): lax.all_gather(shards.reshape(HALF, QW), 'seq', axis=0, axis_index_groups...  15.2 us
    all_gather x1, blocking collectives, per_device(): lax.all_gather(shard, 'seq', axis=0, axis_index_groups=PARITY_GROUPS, til...  14.5 us
    ppermute x1, waiting for transfers between devices, per_device(): kept_pair = lax.ppermute(kept, 'seq', SIBLING_SWAP)  6.56 us
    ppermute x1, starting transfers between devices, per_device(): got = lax.ppermute(send, 'head', CORE_SWAP)  6.13 us
    ppermute x1, waiting for transfers between devices, per_device(): got_q = lax.ppermute(send, 'seq', SIBLING_SWAP)  5.5 us
  transfers between devices with their start and end apart: 7, of which 6 were waited for; matrix products, arithmetic and copies ran while one was open for 2% of the time, Pallas kernels for 7%

profile of v4, /device:TPU:1, one launch (start us, length us, event | category | flops | bytes accessed | tf_op | source)
XLA Modules:
  0.0 149.9 jit_solution(18415361387362357057)
XLA Ops:
  6.5 0.0 copy-start.6
  6.6 0.0 all-gather.4.cloned.1.call-start
  6.6 1.0 broadcast_in_dim.3
  7.6 0.0 copy-start.8
  7.6 16.5 %all_to_all.15 = bf16[4,64,512]{2,1,0:T(8,128)(2,1)} all-to-all(bf16[4,64,512]{2,1,0:T(8,128)(2,1)S(1)} %broadcast_in_dim.3), channel_id=1, replica_groups={{0,16,32,48},{8,24,40,56},{64,80,96,112},{72,88,104,120},{128,144,160,1..., dimensions={0} | all-to-all | bytes 524288 | tf_op jit(solution)/shard_map/all_to_all | solution.py:324
  24.1 0.0 all-gather.4.cloned.1.call-update
  24.1 0.0 all-gather.6.cloned.1.call-start
  24.2 0.9 pad_maximum_fusion
  25.1 14.5 %all_gather.13 = bf16[256,768]{1,0:T(8,128)(2,1)} all-gather(bf16[64,768]{1,0:T(8,128)(2,1)S(1)} %pad_maximum_fusion), channel_id=1, replica_groups={{0,16,32,48},{8,24,40,56},{64,80,96,112},{72,88,104,120},{128,144,160,1..., dimensions={0}, use_global_device_ids=true | all-gather | bytes 491520 | tf_op jit(solution)/shard_map/all_gather | solution.py:345
  39.6 0.0 all-gather.6.cloned.1.call-update
  39.6 0.0 copy-done.7
  39.6 0.1 reshape.27
  39.7 0.1 dynamic-slice_reduce_fusion
  39.8 0.1 reshape.28.gain_ref
  39.9 0.0 copy-done.9
  39.9 0.1 copy.13.index_ref
  40.1 0.0 copy-done.4
  40.1 0.0 copy-done.3
  40.1 0.0 copy-done.5
  40.1 0.0 copy-done.6
  40.1 1.8 %lower.1.own_ref.hid_ref = bf16[256,1024]{1,0:T(8,128)(2,1)S(1)} custom-call(s32[256,1]{1,0:T(8,128)S(1)} %copy.13.index_ref, bf16[512,512]{1,0:T(8,128)(2,1)S(1)} %copy-done.3, bf16[512,128]{1,0:T(8,128)(2,1)S(1)} %copy-done.5, bf16[512,128]{1,0:T(8,128)(2,1)S(1)} %copy-done.6, bf16[512,512]{1,0:T(8,128)(2,1)S(1)} %copy-done.4, ...), custom_call_target="tpu_custom_call" | custom-call | tf_op jit(solution)/shard_map/lower/pallas_call | solution.py:72
  41.9 1.9 %collective-permute-start = (bf16[256,1024]{1,0:T(8,128)(2,1)S(1)}, bf16[256,1024]{1,0:T(8,128)(2,1)S(1)}, u32[]{:S(2)}, u32[]{:S(2)}) collective-permute-start(bf16[256,1024]{1,0:T(8,128)(2,1)S(1)} %lower.1.own_ref.hid_ref), channel_id=1, source_target_pairs={{0,8},{8,0},{16,24},{24,16},{32,40},{40,32},{48,56},{56,48},{64,72... | collective-permute-start | bytes 1572872 | tf_op jit(solution)/shard_map/ppermute | solution.py:342
  43.8 0.0 copy-done.8
  43.8 0.6 fusion
  44.5 1.3 stack.17.place_ref
  45.7 6.6 %collective-permute-done.pair_ref.hid_pair_ref = bf16[256,1024]{1,0:T(8,128)(2,1)S(1)} collective-permute-done((bf16[256,1024]{1,0:T(8,128)(2,1)S(1)}, bf16[256,1024]{1,0:T(8,128)(2,1)S(1)}, u32[]{:S(2)}, u32[]{:S(2)}) %collective-permute-start) | collective-permute-done | bytes 524320 | tf_op jit(solution)/shard_map/ppermute | solution.py:342
  52.3 15.2 %all-gather.4.cloned.1.call-done.weight_ref = bf16[8,256,512]{2,1,0:T(8,128)(2,1)} async-done(((bf16[1,256,512]{2,1,0:T(8,128)(2,1)}), bf16[8,256,512]{2,1,0:T(8,128)(2,1)}) %all-gather.4.cloned.1.call-update) | async-done | bytes 2097168 | tf_op jit(solution)/shard_map/all_gather | solution.py:332
  67.5 1.6 %copy-done.2 = bf16[8,256,512]{2,1,0:T(8,128)(2,1)S(1)} copy-done((bf16[8,256,512]{2,1,0:T(8,128)(2,1)S(1)}, bf16[8,256,512]{2,1,0:T(8,128)(2,1)}, u32[]{:S(2)}) %copy-start.2) | copy-done | bytes 2097176
  69.1 1.3 project_other.1
  70.4 6.1 %collective-permute-start.1 = (bf16[4,512,256]{2,1,0:T(8,128)(2,1)S(1)}, bf16[4,512,256]{2,1,0:T(8,128)(2,1)S(1)}, u32[]{:S(2)}, u32[]{:S(2)}) collective-permute-start(bf16[4,512,256]{2,1,0:T(8,128)(2,1)S(1)} %project_other.1), channel_id=1, source_target_pairs={{0,1},{1,0},{2,3},{3,2},{4,5},{5,4},{6,7},{7,6},{8,9},{9,8},{10,11... | collective-permute-start | bytes 3145736 | tf_op jit(solution)/shard_map/ppermute | solution.py:349
  76.5 1.3 project_mine.1
  77.8 1.0 collective-permute-done.1
  78.8 0.3 add_convert_fusion
  79.1 18.6 %all_to_all.16.parts_ref = bf16[4,512,256]{2,1,0:T(8,128)(2,1)S(1)} all-to-all(bf16[4,512,256]{2,1,0:T(8,128)(2,1)S(1)} %add_convert_fusion), channel_id=1, replica_groups={{0,2,4,6},{1,3,5,7},{8,10,12,14},{9,11,13,15},{16,18,20,22},{17,19,21,2..., dimensions={0} | all-to-all | bytes 2097152 | tf_op jit(solution)/shard_map/all_to_all | solution.py:352
  97.7 1.0 state.1
  98.6 15.8 %all_to_all.17.mine_ref = bf16[4,512,256]{2,1,0:T(8,128)(2,1)S(1)} all-to-all(bf16[4,512,256]{2,1,0:T(8,128)(2,1)S(1)} %state.1), channel_id=1, replica_groups={{0,2,4,6},{1,3,5,7},{8,10,12,14},{9,11,13,15},{16,18,20,22},{17,19,21,2..., dimensions={0} | all-to-all | bytes 2097152 | tf_op jit(solution)/shard_map/all_to_all | solution.py:298
  114.4 4.6 %collective-permute-start.2 = (bf16[4,512,256]{2,1,0:T(8,128)(2,1)S(1)}, bf16[4,512,256]{2,1,0:T(8,128)(2,1)S(1)}, u32[]{:S(2)}, u32[]{:S(2)}) collective-permute-start(bf16[4,512,256]{2,1,0:T(8,128)(2,1)S(1)} %all_to_all.17.mine_ref), channel_id=1, source_target_pairs={{0,1},{1,0},{2,3},{3,2},{4,5},{5,4},{6,7},{7,6},{8,9},{9,8},{10,11... | collective-permute-start | bytes 3145736 | tf_op jit(solution)/shard_map/ppermute | solution.py:299
  119.0 1.1 all-gather.6.cloned.1.call-done
  120.1 1.1 collective-permute-done.2.other_ref
  121.3 1.9 %copy-done = bf16[2048,768]{1,0:T(8,128)(2,1)S(1)} copy-done((bf16[2048,768]{1,0:T(8,128)(2,1)S(1)}, bf16[2048,768]{1,0:T(8,128)(2,1)}, u32[]{:S(2)}) %copy-start) | copy-done | bytes 3145752
  123.2 1.5 %project_kv.1 = (f32[512,256]{1,0:T(8,128)S(1)}, bf16[256,640]{1,0:T(8,128)(2,1)S(1)}) custom-call(s32[5]{0:T(128)S(1)} %stack.17.place_ref, bf16[4,512,256]{2,1,0:T(8,128)(2,1)S(1)} %all_to_all.17.mine_ref, bf16[4,512,256]{2,1,0:T(8,128)(2,1)S(1)} %collective-permute-done.2.other_ref, bf16[8,256,768]{2,1,0:T(8,128)(2,1)S(1)} %bitcast.8), custom_call_target="tpu_custom_call" | custom-call | tf_op jit(solution)/shard_map/project_kv/pallas_call | solution.py:169
  124.7 3.1 %collective-permute-start.4 = (bf16[256,640]{1,0:T(8,128)(2,1)S(1)}, bf16[256,640]{1,0:T(8,128)(2,1)S(1)}, u32[]{:S(2)}, u32[]{:S(2)}) collective-permute-start(bf16[256,640]{1,0:T(8,128)(2,1)S(1)} %get-tuple-element.12), channel_id=1, source_target_pairs={{0,8},{8,0},{16,24},{24,16},{32,40},{40,32},{48,56},{56,48},{64,72... | collective-permute-start | bytes 983048 | tf_op jit(solution)/shard_map/ppermute | solution.py:356
  127.8 3.4 %project_sibling.1 = (f32[512,128]{1,0:T(8,128)S(1)}, bf16[272,384]{1,0:T(8,128)(2,1)S(1)}) custom-call(s32[5]{0:T(128)S(1)} %stack.17.place_ref, bf16[4,512,256]{2,1,0:T(8,128)(2,1)S(1)} %all_to_all.17.mine_ref, bf16[4,512,256]{2,1,0:T(8,128)(2,1)S(1)} %collective-permute-done.2.other_ref, bf16[8,256,768]{2,1,0:T(8,128)(2,1)} %bitcast.7, ...), custom_call_target="tpu_custom_call" | custom-call | flops 536870912 | bytes 4194304 | tf_op jit(solution)/shard_map/project_sibling/pallas_call | solution.py:215
  131.2 2.2 %collective-permute-start.3 = (bf16[272,384]{1,0:T(8,128)(2,1)S(1)}, bf16[272,384]{1,0:T(8,128)(2,1)S(1)}, u32[]{:S(2)}, u32[]{:S(2)}) collective-permute-start(bf16[272,384]{1,0:T(8,128)(2,1)S(1)} %get-tuple-element.10.first_ref), channel_id=1, source_target_pairs={{0,8},{8,0},{16,24},{24,16},{32,40},{40,32},{48,56},{56,48},{64,72... | collective-permute-start | bytes 626696 | tf_op jit(solution)/shard_map/ppermute | solution.py:358
  133.4 1.2 project_q.1.q_ref
  134.7 5.5 %collective-permute-done.3.got_q_ref = bf16[272,384]{1,0:T(8,128)(2,1)S(1)} collective-permute-done((bf16[272,384]{1,0:T(8,128)(2,1)S(1)}, bf16[272,384]{1,0:T(8,128)(2,1)S(1)}, u32[]{:S(2)}, u32[]{:S(2)}) %collective-permute-start.3) | collective-permute-done | bytes 208928 | tf_op jit(solution)/shard_map/ppermute | solution.py:358
  140.2 0.0 collective-permute-done.4.got_kv_ref
  140.2 2.8 %upper.1 = bf16[256,512]{1,0:T(8,128)(2,1)} custom-call(s32[5]{0:T(128)S(1)} %stack.17.place_ref, f32[256,512]{1,0:T(8,128)S(1)} %project_q.1.q_ref, f32[512,256]{1,0:T(8,128)S(1)} %get-tuple-element.9.first_ref.kv_ref, f32[512,128]{1,0:T(8,128)S(1)} %get-tuple-element.11.square_ref, bf16[272,384]{1,0:T(8,128)(2,1)S(1)} %collective-permute-done.3.got_q_ref, ...), custom_call_target="tpu_custom_call" | custom-call | tf_op jit(solution)/shard_map/upper/pallas_call | solution.py:288
  (10 shorter events, 0.0 us)
Async XLA Ops:
  6.5 33.1 %copy-start.7 = (f32[4096]{0:T(1024)S(1)}, f32[4096]{0:T(1024)}, u32[]{:S(2)}) copy-start(f32[4096]{0:T(1024)} %param.16) | copy-start | bytes 49156
  6.5 33.4 %copy-start.9 = (s32[1,256]{1,0:T(1,128)S(1)}, s32[1,256]{1,0:T(1,128)}, u32[]{:S(2)}) copy-start(s32[1,256]{1,0:T(1,128)} %param.20) | copy-start | bytes 3076
  6.5 33.5 %copy-start.4 = (bf16[512,512]{1,0:T(8,128)(2,1)S(1)}, bf16[512,512]{1,0:T(8,128)(2,1)}, u32[]{:S(2)}) copy-start(bf16[512,512]{1,0:T(8,128)(2,1)} %hidden_ref.1) | copy-start | bytes 1572868
  6.5 33.5 %copy-start.3 = (bf16[512,512]{1,0:T(8,128)(2,1)S(1)}, bf16[512,512]{1,0:T(8,128)(2,1)}, u32[]{:S(2)}) copy-start(bf16[512,512]{1,0:T(8,128)(2,1)} %q_ref.1) | copy-start | bytes 1572868
  6.5 33.5 %copy-start.5 = (bf16[512,128]{1,0:T(8,128)(2,1)S(1)}, bf16[512,128]{1,0:T(8,128)(2,1)}, u32[]{:S(2)}) copy-start(bf16[512,128]{1,0:T(8,128)(2,1)} %k_ref.1) | copy-start | bytes 393220
  6.5 33.6 %copy-start.6 = (bf16[512,128]{1,0:T(8,128)(2,1)S(1)}, bf16[512,128]{1,0:T(8,128)(2,1)}, u32[]{:S(2)}) copy-start(bf16[512,128]{1,0:T(8,128)(2,1)} %v_ref.1) | copy-start | bytes 393220
  6.6 60.9 %all-gather.4.cloned.1.call-start = ((), (), s32[]{:S(2)}) async-start(), calls=%async_computation.3 | async-start | bytes 2359296 | tf_op jit(solution)/shard_map/all_gather | solution.py:332
  7.6 36.3 %copy-start.8 = (s32[64]{0:T(128)S(1)}, s32[64]{0:T(128)}, u32[]{:S(2)}) copy-start(s32[64]{0:T(128)} %param.21) | copy-start | bytes 772
  24.1 96.0 %all-gather.6.cloned.1.call-start = ((), (), s32[]{:S(2)}) async-start(), calls=%async_computation.4 | async-start | bytes 3538944 | tf_op jit(solution)/shard_map/all_gather | solution.py:346
  41.9 10.4 %collective-permute-start = (bf16[256,1024]{1,0:T(8,128)(2,1)S(1)}, bf16[256,1024]{1,0:T(8,128)(2,1)S(1)}, u32[]{:S(2)}, u32[]{:S(2)}) collective-permute-start(bf16[256,1024]{1,0:T(8,128)(2,1)S(1)} %lower.1.own_ref.hid_ref), channel_id=1, source_target_pairs={{0,8},{8,0},{16,24},{24,16},{32,40},{40,32},{48,56},{56,48},{64,72... | collective-permute-start | bytes 1572872 | tf_op jit(solution)/shard_map/ppermute | solution.py:342
  67.5 1.6 %copy-start.2 = (bf16[8,256,512]{2,1,0:T(8,128)(2,1)S(1)}, bf16[8,256,512]{2,1,0:T(8,128)(2,1)}, u32[]{:S(2)}) copy-start(bf16[8,256,512]{2,1,0:T(8,128)(2,1)} %all-gather.4.cloned.1.call-done.weight_ref) | copy-start | bytes 6291460
  70.4 8.4 %collective-permute-start.1 = (bf16[4,512,256]{2,1,0:T(8,128)(2,1)S(1)}, bf16[4,512,256]{2,1,0:T(8,128)(2,1)S(1)}, u32[]{:S(2)}, u32[]{:S(2)}) collective-permute-start(bf16[4,512,256]{2,1,0:T(8,128)(2,1)S(1)} %project_other.1), channel_id=1, source_target_pairs={{0,1},{1,0},{2,3},{3,2},{4,5},{5,4},{6,7},{7,6},{8,9},{9,8},{10,11... | collective-permute-start | bytes 3145736 | tf_op jit(solution)/shard_map/ppermute | solution.py:349
  114.4 6.9 %collective-permute-start.2 = (bf16[4,512,256]{2,1,0:T(8,128)(2,1)S(1)}, bf16[4,512,256]{2,1,0:T(8,128)(2,1)S(1)}, u32[]{:S(2)}, u32[]{:S(2)}) collective-permute-start(bf16[4,512,256]{2,1,0:T(8,128)(2,1)S(1)} %all_to_all.17.mine_ref), channel_id=1, source_target_pairs={{0,1},{1,0},{2,3},{3,2},{4,5},{5,4},{6,7},{7,6},{8,9},{9,8},{10,11... | collective-permute-start | bytes 3145736 | tf_op jit(solution)/shard_map/ppermute | solution.py:299
  121.3 1.9 %copy-start = (bf16[2048,768]{1,0:T(8,128)(2,1)S(1)}, bf16[2048,768]{1,0:T(8,128)(2,1)}, u32[]{:S(2)}) copy-start(bf16[2048,768]{1,0:T(8,128)(2,1)} %all-gather.6.cloned.1.call-done) | copy-start | bytes 9437188
  124.7 15.5 %collective-permute-start.4 = (bf16[256,640]{1,0:T(8,128)(2,1)S(1)}, bf16[256,640]{1,0:T(8,128)(2,1)S(1)}, u32[]{:S(2)}, u32[]{:S(2)}) collective-permute-start(bf16[256,640]{1,0:T(8,128)(2,1)S(1)} %get-tuple-element.12), channel_id=1, source_target_pairs={{0,8},{8,0},{16,24},{24,16},{32,40},{40,32},{48,56},{56,48},{64,72... | collective-permute-start | bytes 983048 | tf_op jit(solution)/shard_map/ppermute | solution.py:356
  127.8 5.6 %copy-start.1 = (bf16[2048,768]{1,0:T(8,128)(2,1)S(1)}, bf16[2048,768]{1,0:T(8,128)(2,1)}, u32[]{:S(2)}) copy-start(bf16[2048,768]{1,0:T(8,128)(2,1)} %all-gather.6.cloned.1.call-done) | copy-start | bytes 9437188
  131.2 9.0 %collective-permute-start.3 = (bf16[272,384]{1,0:T(8,128)(2,1)S(1)}, bf16[272,384]{1,0:T(8,128)(2,1)S(1)}, u32[]{:S(2)}, u32[]{:S(2)}) collective-permute-start(bf16[272,384]{1,0:T(8,128)(2,1)S(1)} %get-tuple-element.10.first_ref), channel_id=1, source_target_pairs={{0,8},{8,0},{16,24},{24,16},{32,40},{40,32},{48,56},{56,48},{64,72... | collective-permute-start | bytes 626696 | tf_op jit(solution)/shard_map/ppermute | solution.py:358
Sparse Core Ops, SparseCore 0:
  24.3 43.1 all-gather.3
  69.5 50.5 all-gather.5

commit v5 on v4

--- a/solution.py
+++ b/solution.py
@@ -46,11 +46,15 @@
     return lax.dot_general(a, b, (((1,), (1,)), ((), ())), preferred_element_type=jnp.float32)
 
 
+def with_ones(values):
+    return jnp.concatenate([values, jnp.ones_like(values)], axis=1)
+
+
 def attend(scores, values):
     top = jnp.max(scores, axis=1, keepdims=True)
-    unnormed = jnp.exp2(scores - top)
-    total = jnp.sum(unnormed, axis=1, keepdims=True)
-    return dot(unnormed.astype(jnp.bfloat16), values) / total
+    unnormed = jnp.exp2(scores - top).astype(jnp.bfloat16)
+    sums = dot(unnormed, values)
+    return sums[:, :HD] / sums[:, HD : HD + 1]
 
 
 def lower_kernel(index_ref, q_ref, k_ref, v_ref, hidden_ref, gain_ref, inverse_ref, out_ref):
@@ -60,7 +64,7 @@
     causal = column <= index
     queries = dot(pick, q_ref[...]).astype(jnp.bfloat16)
     keys = k_ref[...]
-    values = v_ref[...]
+    values = with_ones(v_ref[...])
     for g in range(GROUP):
         cols = slice(g * HD, (g + 1) * HD)
         scores = jnp.where(causal, dot_t(queries[:, cols], keys) * SCALE, NEG)
@@ -153,28 +157,47 @@
     return dot(jnp.concatenate(state, axis=1), weights)
 
 
-def kv_kernel(place_ref, mine_ref, other_ref, weight_ref, keep_ref, send_ref):
+def kv_kernel(place_ref, mine_ref, other_ref, weight_ref, keep_ref, send_ref, kv_ref, first_ref, sems):
     heads = by_core(place_ref[0])
-    weights = jnp.concatenate([weight_ref[head, :, QW:] for head in heads], axis=0)
+    copies = []
+    for cols, buffer in ((pl.ds(QW, KVW), kv_ref), (pl.ds(0, HD), first_ref)):
+        for i, head in enumerate(heads):
+            source = weight_ref.at[head, :, cols]
+            copies.append(pltpu.make_async_copy(source, buffer.at[i], sems.at[len(copies)]))
+            copies[-1].start()
+    for copy in copies[: 2 * N_X]:
+        copy.wait()
+    weights = kv_ref[...].reshape(2 * N_X * HALF, KVW)
     for half, rows in enumerate((OWN, PAIR)):
         sums = contract(rows, mine_ref, other_ref, weights)
         keep_ref[rows] = sums
         send_ref[:, (1 - half) * KVW : (2 - half) * KVW] = sums.astype(jnp.bfloat16)
-    weights = jnp.concatenate([weight_ref[head, :, :HD] for head in heads], axis=0)
-    sums = contract(PAIR, mine_ref, other_ref, weights)
+    for copy in copies[2 * N_X :]:
+        copy.wait()
+    sums = contract(PAIR, mine_ref, other_ref, first_ref[...].reshape(2 * N_X * HALF, HD))
     send_ref[:, 2 * KVW :] = sums.astype(jnp.bfloat16)
 
 
 def project_kv(place, mine, other, weights):
     return pl.pallas_call(
         kv_kernel,
-        in_specs=[pl.BlockSpec(memory_space=pltpu.SMEM)] + [pl.BlockSpec(memory_space=pltpu.VMEM)] * 3,
+        in_specs=[
+            pl.BlockSpec(memory_space=pltpu.SMEM),
+            pl.BlockSpec(memory_space=pltpu.VMEM),
+            pl.BlockSpec(memory_space=pltpu.VMEM),
+            pl.BlockSpec(memory_space=pl.ANY),
+        ],
         out_specs=[pl.BlockSpec(memory_space=pltpu.VMEM)] * 2,
         out_shape=[
             jax.ShapeDtypeStruct((2 * KMAX, KVW), jnp.float32),
             jax.ShapeDtypeStruct((KMAX, 2 * KVW + HD), jnp.bfloat16),
         ],
-        compiler_params=params(),
+        scratch_shapes=[
+            pltpu.VMEM((2 * N_X, HALF, KVW), jnp.bfloat16),
+            pltpu.VMEM((2 * N_X, HALF, HD), jnp.bfloat16),
+            pltpu.SemaphoreType.DMA((4 * N_X,)),
+        ],
+        compiler_params=pltpu.CompilerParams(vmem_limit_bytes=50 * 1024 * 1024),
         name="project_kv",
     )(place, mine, other, weights)
 
@@ -271,7 +294,7 @@
     pair = (kv_ref[KMAX:] + got_kv_ref[:, KVW : 2 * KVW].astype(jnp.float32)) * pair_inv
     pair = pair.astype(jnp.bfloat16)
     keys = jnp.concatenate([pair[:, :HD], own[:, :HD]], axis=0)
-    values = jnp.concatenate([pair[:, HD:], own[:, HD:]], axis=0)
+    values = with_ones(jnp.concatenate([pair[:, HD:], own[:, HD:]], axis=0))
     row = lax.broadcasted_iota(jnp.int32, (KMAX, 2 * KMAX), 0)
     col = lax.broadcasted_iota(jnp.int32, (KMAX, 2 * KMAX), 1)
     from_left = col < left_count * parity

time: 150 us -> 150 us (level)
  local copies, waits for them, and re-layouts: 6.76 us -> 4.89 us
    unnamed x20 -> x18, local copies, waits for them, and re-layouts: 3.51 us -> 1.62 us
    pallas_call x1, Pallas kernels: 1.52 us -> 3.12 us  [project_kv(): pl.pallas_call(kv_kernel, in_specs=[pl.BlockSpec(memory_space=pltpu.SMEM)...]
  transfers between devices with their start and end apart: 7 -> 7, of which waited for: 6 -> 6; matrix products, arithmetic and copies ran while one was open for 2% -> 2% of each run, Pallas kernels for 7% -> 6%
where the time goes in v5:
time: 150 us; the launch traced here: 149 us
  blocking collectives  65.5 us (44%)
  waiting for transfers between devices  31.2 us (21%)
  starting transfers between devices  17.7 us (12%)
  Pallas kernels  15.4 us (10%)
  between operations  13.6 us (9%)
  local copies, waits for them, and re-layouts  4.89 us (3%)
    all_to_all x1, blocking collectives, per_device(): lax.all_to_all(parts, 'head', 0, 0, axis_index_groups=X_GROUPS, tiled=True)  18.7 us
    all_to_all x1, blocking collectives, per_device(): lax.all_to_all(jnp.broadcast_to(shard, (N_Y // 2,) + shard.shape), 'seq',...  16.5 us
    all_to_all x1, blocking collectives, gather_head(): lax.all_to_all(x, 'head', 0, 0, axis_index_groups=X_GROUPS, tiled=True)  15.8 us
    all_gather x1, waiting for transfers between devices, per_device(): lax.all_gather(shards.reshape(HALF, QW), 'seq', axis=0, axis_index_groups...  15.7 us
    all_gather x1, blocking collectives, per_device(): lax.all_gather(shard, 'seq', axis=0, axis_index_groups=PARITY_GROUPS, til...  14.5 us
    ppermute x1, waiting for transfers between devices, per_device(): kept_pair = lax.ppermute(kept, 'seq', SIBLING_SWAP)  6.64 us
    ppermute x1, starting transfers between devices, per_device(): got = lax.ppermute(send, 'head', CORE_SWAP)  5.83 us
    ppermute x1, waiting for transfers between devices, per_device(): got_q = lax.ppermute(send, 'seq', SIBLING_SWAP)  5.57 us
  transfers between devices with their start and end apart: 7, of which 6 were waited for; matrix products, arithmetic and copies ran while one was open for 2% of the time, Pallas kernels for 6%

profile of v5, /device:TPU:1, one launch (start us, length us, event | category | flops | bytes accessed | tf_op | source)
XLA Modules:
  0.0 149.5 jit_solution(13178843620216475195)
XLA Ops:
  6.5 0.0 copy-start.5
  6.6 0.0 all-gather.4.cloned.1.call-start
  6.6 1.0 broadcast_in_dim.3
  7.6 0.0 copy-start.7
  7.6 16.5 %all_to_all.15 = bf16[4,64,512]{2,1,0:T(8,128)(2,1)} all-to-all(bf16[4,64,512]{2,1,0:T(8,128)(2,1)S(1)} %broadcast_in_dim.3), channel_id=1, replica_groups={{0,16,32,48},{8,24,40,56},{64,80,96,112},{72,88,104,120},{128,144,160,1..., dimensions={0} | all-to-all | bytes 524288 | tf_op jit(solution)/shard_map/all_to_all | solution.py:347
  24.1 0.0 all-gather.4.cloned.1.call-update
  24.1 0.0 all-gather.6.cloned.1.call-start
  24.2 0.9 pad_maximum_fusion
  25.1 14.5 %all_gather.13 = bf16[256,768]{1,0:T(8,128)(2,1)} all-gather(bf16[64,768]{1,0:T(8,128)(2,1)S(1)} %pad_maximum_fusion), channel_id=1, replica_groups={{0,16,32,48},{8,24,40,56},{64,80,96,112},{72,88,104,120},{128,144,160,1..., dimensions={0}, use_global_device_ids=true | all-gather | bytes 491520 | tf_op jit(solution)/shard_map/all_gather | solution.py:368
  39.6 0.0 all-gather.6.cloned.1.call-update
  39.6 0.0 copy-done.6
  39.6 0.1 reshape.27
  39.7 0.1 dynamic-slice_reduce_fusion
  39.8 0.1 reshape.28.gain_ref
  39.9 0.0 copy-done.8
  39.9 0.1 copy.13.index_ref
  40.1 0.0 copy-done.3
  40.1 0.0 copy-done.2
  40.1 0.0 copy-done.4
  40.1 0.0 copy-done.5
  40.1 1.4 lower.1.own_ref.hid_ref
  41.5 1.9 %collective-permute-start = (bf16[256,1024]{1,0:T(8,128)(2,1)S(1)}, bf16[256,1024]{1,0:T(8,128)(2,1)S(1)}, u32[]{:S(2)}, u32[]{:S(2)}) collective-permute-start(bf16[256,1024]{1,0:T(8,128)(2,1)S(1)} %lower.1.own_ref.hid_ref), channel_id=1, source_target_pairs={{0,8},{8,0},{16,24},{24,16},{32,40},{40,32},{48,56},{56,48},{64,72... | collective-permute-start | bytes 1572872 | tf_op jit(solution)/shard_map/ppermute | solution.py:365
  43.5 0.0 copy-done.7
  43.5 0.7 fusion
  44.1 1.3 stack.17.place_ref
  45.4 6.6 %collective-permute-done.pair_ref.hid_pair_ref = bf16[256,1024]{1,0:T(8,128)(2,1)S(1)} collective-permute-done((bf16[256,1024]{1,0:T(8,128)(2,1)S(1)}, bf16[256,1024]{1,0:T(8,128)(2,1)S(1)}, u32[]{:S(2)}, u32[]{:S(2)}) %collective-permute-start) | collective-permute-done | bytes 524320 | tf_op jit(solution)/shard_map/ppermute | solution.py:365
  52.1 15.7 %all-gather.4.cloned.1.call-done.weight_ref = bf16[8,256,512]{2,1,0:T(8,128)(2,1)} async-done(((bf16[1,256,512]{2,1,0:T(8,128)(2,1)}), bf16[8,256,512]{2,1,0:T(8,128)(2,1)}) %all-gather.4.cloned.1.call-update) | async-done | bytes 2097168 | tf_op jit(solution)/shard_map/all_gather | solution.py:355
  67.8 1.6 %copy-done.1 = bf16[8,256,512]{2,1,0:T(8,128)(2,1)S(1)} copy-done((bf16[8,256,512]{2,1,0:T(8,128)(2,1)S(1)}, bf16[8,256,512]{2,1,0:T(8,128)(2,1)}, u32[]{:S(2)}) %copy-start.1) | copy-done | bytes 2097176
  69.4 1.3 project_other.1
  70.7 5.8 %collective-permute-start.1 = (bf16[4,512,256]{2,1,0:T(8,128)(2,1)S(1)}, bf16[4,512,256]{2,1,0:T(8,128)(2,1)S(1)}, u32[]{:S(2)}, u32[]{:S(2)}) collective-permute-start(bf16[4,512,256]{2,1,0:T(8,128)(2,1)S(1)} %project_other.1), channel_id=1, source_target_pairs={{0,1},{1,0},{2,3},{3,2},{4,5},{5,4},{6,7},{7,6},{8,9},{9,8},{10,11... | collective-permute-start | bytes 3145736 | tf_op jit(solution)/shard_map/ppermute | solution.py:372
  76.5 1.3 project_mine.1
  77.8 1.0 collective-permute-done.1
  78.8 0.3 add_convert_fusion
  79.1 18.7 %all_to_all.16.parts_ref = bf16[4,512,256]{2,1,0:T(8,128)(2,1)S(1)} all-to-all(bf16[4,512,256]{2,1,0:T(8,128)(2,1)S(1)} %add_convert_fusion), channel_id=1, replica_groups={{0,2,4,6},{1,3,5,7},{8,10,12,14},{9,11,13,15},{16,18,20,22},{17,19,21,2..., dimensions={0} | all-to-all | bytes 2097152 | tf_op jit(solution)/shard_map/all_to_all | solution.py:375
  97.7 1.0 state.1
  98.7 15.8 %all_to_all.17.mine_ref = bf16[4,512,256]{2,1,0:T(8,128)(2,1)S(1)} all-to-all(bf16[4,512,256]{2,1,0:T(8,128)(2,1)S(1)} %state.1), channel_id=1, replica_groups={{0,2,4,6},{1,3,5,7},{8,10,12,14},{9,11,13,15},{16,18,20,22},{17,19,21,2..., dimensions={0} | all-to-all | bytes 2097152 | tf_op jit(solution)/shard_map/all_to_all | solution.py:321
  114.5 4.6 %collective-permute-start.2 = (bf16[4,512,256]{2,1,0:T(8,128)(2,1)S(1)}, bf16[4,512,256]{2,1,0:T(8,128)(2,1)S(1)}, u32[]{:S(2)}, u32[]{:S(2)}) collective-permute-start(bf16[4,512,256]{2,1,0:T(8,128)(2,1)S(1)} %all_to_all.17.mine_ref), channel_id=1, source_target_pairs={{0,1},{1,0},{2,3},{3,2},{4,5},{5,4},{6,7},{7,6},{8,9},{9,8},{10,11... | collective-permute-start | bytes 3145736 | tf_op jit(solution)/shard_map/ppermute | solution.py:322
  119.1 1.1 all-gather.6.cloned.1.call-done
  120.1 1.2 collective-permute-done.2.other_ref
  121.3 3.1 %project_kv.1 = (f32[512,256]{1,0:T(8,128)S(1)}, bf16[256,640]{1,0:T(8,128)(2,1)S(1)}) custom-call(s32[5]{0:T(128)S(1)} %stack.17.place_ref, bf16[4,512,256]{2,1,0:T(8,128)(2,1)S(1)} %all_to_all.17.mine_ref, bf16[4,512,256]{2,1,0:T(8,128)(2,1)S(1)} %collective-permute-done.2.other_ref, bf16[8,256,768]{2,1,0:T(8,128)(2,1)} %bitcast.7), custom_call_target="tpu_custom_call" | custom-call | tf_op jit(solution)/shard_map/project_kv/pallas_call | solution.py:182
  124.5 3.0 %collective-permute-start.4 = (bf16[256,640]{1,0:T(8,128)(2,1)S(1)}, bf16[256,640]{1,0:T(8,128)(2,1)S(1)}, u32[]{:S(2)}, u32[]{:S(2)}) collective-permute-start(bf16[256,640]{1,0:T(8,128)(2,1)S(1)} %get-tuple-element.12), channel_id=1, source_target_pairs={{0,8},{8,0},{16,24},{24,16},{32,40},{40,32},{48,56},{56,48},{64,72... | collective-permute-start | bytes 983048 | tf_op jit(solution)/shard_map/ppermute | solution.py:379
  127.5 0.0 copy-start
  127.5 3.4 %project_sibling.1 = (f32[512,128]{1,0:T(8,128)S(1)}, bf16[272,384]{1,0:T(8,128)(2,1)S(1)}) custom-call(s32[5]{0:T(128)S(1)} %stack.17.place_ref, bf16[4,512,256]{2,1,0:T(8,128)(2,1)S(1)} %all_to_all.17.mine_ref, bf16[4,512,256]{2,1,0:T(8,128)(2,1)S(1)} %collective-permute-done.2.other_ref, bf16[8,256,768]{2,1,0:T(8,128)(2,1)} %bitcast.8, ...), custom_call_target="tpu_custom_call" | custom-call | flops 536870912 | bytes 4194304 | tf_op jit(solution)/shard_map/project_sibling/pallas_call | solution.py:238
  130.9 2.3 %collective-permute-start.3 = (bf16[272,384]{1,0:T(8,128)(2,1)S(1)}, bf16[272,384]{1,0:T(8,128)(2,1)S(1)}, u32[]{:S(2)}, u32[]{:S(2)}) collective-permute-start(bf16[272,384]{1,0:T(8,128)(2,1)S(1)} %get-tuple-element.10.first_ref), channel_id=1, source_target_pairs={{0,8},{8,0},{16,24},{24,16},{32,40},{40,32},{48,56},{56,48},{64,72... | collective-permute-start | bytes 626696 | tf_op jit(solution)/shard_map/ppermute | solution.py:381
  133.2 1.2 project_q.1.q_ref
  134.5 5.6 %collective-permute-done.3.got_q_ref = bf16[272,384]{1,0:T(8,128)(2,1)S(1)} collective-permute-done((bf16[272,384]{1,0:T(8,128)(2,1)S(1)}, bf16[272,384]{1,0:T(8,128)(2,1)S(1)}, u32[]{:S(2)}, u32[]{:S(2)}) %collective-permute-start.3) | collective-permute-done | bytes 208928 | tf_op jit(solution)/shard_map/ppermute | solution.py:381
  140.0 0.0 collective-permute-done.4.got_kv_ref
  140.0 2.6 %upper.1 = bf16[256,512]{1,0:T(8,128)(2,1)} custom-call(s32[5]{0:T(128)S(1)} %stack.17.place_ref, f32[256,512]{1,0:T(8,128)S(1)} %project_q.1.q_ref, f32[512,256]{1,0:T(8,128)S(1)} %get-tuple-element.9.first_ref.kv_ref, f32[512,128]{1,0:T(8,128)S(1)} %get-tuple-element.11.square_ref, bf16[272,384]{1,0:T(8,128)(2,1)S(1)} %collective-permute-done.3.got_q_ref, ...), custom_call_target="tpu_custom_call" | custom-call | tf_op jit(solution)/shard_map/upper/pallas_call | solution.py:311
  (8 shorter events, 0.0 us)
Async XLA Ops:
  6.5 33.1 %copy-start.6 = (f32[4096]{0:T(1024)S(1)}, f32[4096]{0:T(1024)}, u32[]{:S(2)}) copy-start(f32[4096]{0:T(1024)} %param.16) | copy-start | bytes 49156
  6.5 33.4 %copy-start.8 = (s32[1,256]{1,0:T(1,128)S(1)}, s32[1,256]{1,0:T(1,128)}, u32[]{:S(2)}) copy-start(s32[1,256]{1,0:T(1,128)} %param.20) | copy-start | bytes 3076
  6.5 33.5 %copy-start.3 = (bf16[512,512]{1,0:T(8,128)(2,1)S(1)}, bf16[512,512]{1,0:T(8,128)(2,1)}, u32[]{:S(2)}) copy-start(bf16[512,512]{1,0:T(8,128)(2,1)} %hidden_ref.1) | copy-start | bytes 1572868
  6.5 33.5 %copy-start.2 = (bf16[512,512]{1,0:T(8,128)(2,1)S(1)}, bf16[512,512]{1,0:T(8,128)(2,1)}, u32[]{:S(2)}) copy-start(bf16[512,512]{1,0:T(8,128)(2,1)} %q_ref.1) | copy-start | bytes 1572868
  6.5 33.5 %copy-start.4 = (bf16[512,128]{1,0:T(8,128)(2,1)S(1)}, bf16[512,128]{1,0:T(8,128)(2,1)}, u32[]{:S(2)}) copy-start(bf16[512,128]{1,0:T(8,128)(2,1)} %k_ref.1) | copy-start | bytes 393220
  6.5 33.6 %copy-start.5 = (bf16[512,128]{1,0:T(8,128)(2,1)S(1)}, bf16[512,128]{1,0:T(8,128)(2,1)}, u32[]{:S(2)}) copy-start(bf16[512,128]{1,0:T(8,128)(2,1)} %v_ref.1) | copy-start | bytes 393220
  6.6 61.2 %all-gather.4.cloned.1.call-start = ((), (), s32[]{:S(2)}) async-start(), calls=%async_computation.3 | async-start | bytes 2359296 | tf_op jit(solution)/shard_map/all_gather | solution.py:355
  7.6 35.9 %copy-start.7 = (s32[64]{0:T(128)S(1)}, s32[64]{0:T(128)}, u32[]{:S(2)}) copy-start(s32[64]{0:T(128)} %param.21) | copy-start | bytes 772
  24.1 96.0 %all-gather.6.cloned.1.call-start = ((), (), s32[]{:S(2)}) async-start(), calls=%async_computation.4 | async-start | bytes 3538944 | tf_op jit(solution)/shard_map/all_gather | solution.py:369
  41.5 10.5 %collective-permute-start = (bf16[256,1024]{1,0:T(8,128)(2,1)S(1)}, bf16[256,1024]{1,0:T(8,128)(2,1)S(1)}, u32[]{:S(2)}, u32[]{:S(2)}) collective-permute-start(bf16[256,1024]{1,0:T(8,128)(2,1)S(1)} %lower.1.own_ref.hid_ref), channel_id=1, source_target_pairs={{0,8},{8,0},{16,24},{24,16},{32,40},{40,32},{48,56},{56,48},{64,72... | collective-permute-start | bytes 1572872 | tf_op jit(solution)/shard_map/ppermute | solution.py:365
  67.8 1.6 %copy-start.1 = (bf16[8,256,512]{2,1,0:T(8,128)(2,1)S(1)}, bf16[8,256,512]{2,1,0:T(8,128)(2,1)}, u32[]{:S(2)}) copy-start(bf16[8,256,512]{2,1,0:T(8,128)(2,1)} %all-gather.4.cloned.1.call-done.weight_ref) | copy-start | bytes 6291460
  70.7 8.1 %collective-permute-start.1 = (bf16[4,512,256]{2,1,0:T(8,128)(2,1)S(1)}, bf16[4,512,256]{2,1,0:T(8,128)(2,1)S(1)}, u32[]{:S(2)}, u32[]{:S(2)}) collective-permute-start(bf16[4,512,256]{2,1,0:T(8,128)(2,1)S(1)} %project_other.1), channel_id=1, source_target_pairs={{0,1},{1,0},{2,3},{3,2},{4,5},{5,4},{6,7},{7,6},{8,9},{9,8},{10,11... | collective-permute-start | bytes 3145736 | tf_op jit(solution)/shard_map/ppermute | solution.py:372
  114.5 6.9 %collective-permute-start.2 = (bf16[4,512,256]{2,1,0:T(8,128)(2,1)S(1)}, bf16[4,512,256]{2,1,0:T(8,128)(2,1)S(1)}, u32[]{:S(2)}, u32[]{:S(2)}) collective-permute-start(bf16[4,512,256]{2,1,0:T(8,128)(2,1)S(1)} %all_to_all.17.mine_ref), channel_id=1, source_target_pairs={{0,1},{1,0},{2,3},{3,2},{4,5},{5,4},{6,7},{7,6},{8,9},{9,8},{10,11... | collective-permute-start | bytes 3145736 | tf_op jit(solution)/shard_map/ppermute | solution.py:322
  124.5 15.6 %collective-permute-start.4 = (bf16[256,640]{1,0:T(8,128)(2,1)S(1)}, bf16[256,640]{1,0:T(8,128)(2,1)S(1)}, u32[]{:S(2)}, u32[]{:S(2)}) collective-permute-start(bf16[256,640]{1,0:T(8,128)(2,1)S(1)} %get-tuple-element.12), channel_id=1, source_target_pairs={{0,8},{8,0},{16,24},{24,16},{32,40},{40,32},{48,56},{56,48},{64,72... | collective-permute-start | bytes 983048 | tf_op jit(solution)/shard_map/ppermute | solution.py:379
  127.5 5.7 %copy-start = (bf16[2048,768]{1,0:T(8,128)(2,1)S(1)}, bf16[2048,768]{1,0:T(8,128)(2,1)}, u32[]{:S(2)}) copy-start(bf16[2048,768]{1,0:T(8,128)(2,1)} %all-gather.6.cloned.1.call-done) | copy-start | bytes 9437188
  130.9 9.1 %collective-permute-start.3 = (bf16[272,384]{1,0:T(8,128)(2,1)S(1)}, bf16[272,384]{1,0:T(8,128)(2,1)S(1)}, u32[]{:S(2)}, u32[]{:S(2)}) collective-permute-start(bf16[272,384]{1,0:T(8,128)(2,1)S(1)} %get-tuple-element.10.first_ref), channel_id=1, source_target_pairs={{0,8},{8,0},{16,24},{24,16},{32,40},{40,32},{48,56},{56,48},{64,72... | collective-permute-start | bytes 626696 | tf_op jit(solution)/shard_map/ppermute | solution.py:381
Sparse Core Ops, SparseCore 0:
  24.3 43.4 all-gather.3
  69.8 50.2 all-gather.5

commit v6 on v5

--- a/solution.py
+++ b/solution.py
@@ -57,7 +57,9 @@
     return sums[:, :HD] / sums[:, HD : HD + 1]
 
 
-def lower_kernel(index_ref, q_ref, k_ref, v_ref, hidden_ref, gain_ref, inverse_ref, out_ref):
+def lower_kernel(
+    place_ref, index_ref, q_ref, k_ref, v_ref, hidden_ref, gain_ref, inverse_ref, out_ref, hid_ref
+):
     index = index_ref[...]
     column = lax.broadcasted_iota(jnp.int32, (KMAX, BLOCK), 1)
     pick = (column == index).astype(jnp.bfloat16)
@@ -69,17 +71,27 @@
         cols = slice(g * HD, (g + 1) * HD)
         scores = jnp.where(causal, dot_t(queries[:, cols], keys) * SCALE, NEG)
         out_ref[:, cols] = attend(scores, values).astype(jnp.bfloat16)
-    out_ref[:, QW:] = dot(pick, hidden_ref[...]).astype(jnp.bfloat16)
-
-
-def lower(index, queries, keys, values, hidden, gain, inverse):
+    kept = dot(pick, hidden_ref[...]).astype(jnp.bfloat16)
+    row = lax.broadcasted_iota(jnp.int32, (QW, HALF), 0)
+    col = lax.broadcasted_iota(jnp.int32, (QW, HALF), 1)
+    for ref, parity in ((hid_ref, place_ref[1]), (out_ref.at[:, QW:], 1 - place_ref[1])):
+        source = (col // STRIP) * (2 * STRIP) + parity * STRIP + col % STRIP
+        ref[...] = dot(kept, (row == source).astype(jnp.bfloat16)).astype(jnp.bfloat16)
+
+
+def lower(place, index, queries, keys, values, hidden, gain, inverse):
     return pl.pallas_call(
         lower_kernel,
-        in_specs=[pl.BlockSpec(memory_space=pltpu.VMEM)] * 5 + [pl.BlockSpec(memory_space=pl.ANY)] * 2,
-        out_shape=jax.ShapeDtypeStruct((KMAX, 2 * QW), jnp.bfloat16),
+        in_specs=[pl.BlockSpec(memory_space=pltpu.SMEM)]
+        + [pl.BlockSpec(memory_space=pltpu.VMEM)] * 5
+        + [pl.BlockSpec(memory_space=pl.ANY)] * 2,
+        out_shape=[
+            jax.ShapeDtypeStruct((KMAX, QW + HALF), jnp.bfloat16),
+            jax.ShapeDtypeStruct((KMAX, HALF), jnp.bfloat16),
+        ],
         compiler_params=params(),
         name="lower",
-    )(index, queries, keys, values, hidden, gain, inverse)
+    )(place, index, queries, keys, values, hidden, gain, inverse)
 
 
 def project_kernel(other, place_ref, own_ref, pair_ref, weight_ref, out_ref):
@@ -106,16 +118,11 @@
     )(place, kept, kept_pair, weights)
 
 
-def state_kernel(place_ref, parts_ref, hid_ref, hid_pair_ref, gain_ref, out_ref):
+def state_kernel(place_ref, parts_ref, hid_ref, pair_ref, gain_ref, out_ref):
     gain = gain_ref[place_ref[4]]
-    parity = place_ref[1]
-    row = lax.broadcasted_iota(jnp.int32, (QW, HALF), 0)
-    col = lax.broadcasted_iota(jnp.int32, (QW, HALF), 1)
-    source = (col // STRIP) * (2 * STRIP) + parity * STRIP + col % STRIP
-    pick = (row == source).astype(jnp.bfloat16)
-    for half, hid in enumerate((hid_ref, hid_pair_ref)):
+    for half, hid in enumerate((hid_ref, pair_ref.at[:, QW:])):
         rows = slice(half * KMAX, (half + 1) * KMAX)
-        total = dot(hid[...], pick)
+        total = hid[...].astype(jnp.float32)
         for x in range(N_X):
             total += parts_ref[x, rows].astype(jnp.float32)
         state = total.astype(jnp.bfloat16).astype(jnp.float32)
@@ -124,24 +131,14 @@
             out_ref[x, rows] = scaled
 
 
-def add_up(place, parts, kept, kept_pair, gain):
-    shape = (N_X, 2 * KMAX, HALF)
-    hidden = pl.BlockSpec((KMAX, QW), lambda i: (0, 1))
+def add_up(place, parts, hid, kept_pair, gain):
     return pl.pallas_call(
         state_kernel,
-        grid=(1,),
-        in_specs=[
-            pl.BlockSpec(memory_space=pltpu.SMEM),
-            pl.BlockSpec(shape, lambda i: (0, 0, 0)),
-            hidden,
-            hidden,
-            pl.BlockSpec((2 * N_X, 1, HALF), lambda i: (0, 0, 0)),
-        ],
-        out_specs=pl.BlockSpec(shape, lambda i: (0, 0, 0)),
-        out_shape=jax.ShapeDtypeStruct(shape, jnp.bfloat16),
+        in_specs=[pl.BlockSpec(memory_space=pltpu.SMEM)] + [pl.BlockSpec(memory_space=pltpu.VMEM)] * 4,
+        out_shape=jax.ShapeDtypeStruct((N_X, 2 * KMAX, HALF), jnp.bfloat16),
         compiler_params=params(),
         name="state",
-    )(place, parts, kept, kept_pair, gain)
+    )(place, parts, hid, kept_pair, gain)
 
 
 def by_core(core):
@@ -361,7 +358,7 @@
     ).reshape(8, 1, HALF)
     inverse = 1.0 / (gain * gain)
     index = keep_index.reshape(KMAX, 1)
-    kept = lower(index, queries, keys_low, values_low, hidden, gain, inverse)
+    kept, hid = lower(place, index, queries, keys_low, values_low, hidden, gain, inverse)
     kept_pair = lax.ppermute(kept, "seq", SIBLING_SWAP)
 
     shard = jnp.concatenate([query_weight, key_weight, value_weight], axis=1)
@@ -373,7 +370,7 @@
     keep = project(place, kept, kept_pair, out_weights, False)
     parts = (keep + got.astype(jnp.float32)).astype(jnp.bfloat16)
     parts = lax.all_to_all(parts, "head", 0, 0, axis_index_groups=X_GROUPS, tiled=True)
-    mine, other = gather_head(add_up(place, parts, kept, kept_pair, gain))
+    mine, other = gather_head(add_up(place, parts, hid, kept_pair, gain))
 
     kv, send = project_kv(place, mine, other, qkv_weights)
     got_kv = lax.ppermute(send, "seq", SIBLING_SWAP)

time: 150 us -> 150 us (level)
  transfers between devices with their start and end apart: 7 -> 7, of which waited for: 6 -> 6; matrix products, arithmetic and copies ran while one was open for 2% -> 2% of each run, Pallas kernels for 6% -> 7%
where the time goes in v6:
time: 150 us; the launch traced here: 149 us
  blocking collectives  65.5 us (44%)
  waiting for transfers between devices  30.2 us (20%)
  starting transfers between devices  18 us (12%)
  Pallas kernels  15.8 us (11%)
  between operations  13.6 us (9%)
  local copies, waits for them, and re-layouts  4.87 us (3%)
    all_to_all x1, blocking collectives, per_device(): lax.all_to_all(parts, 'head', 0, 0, axis_index_groups=X_GROUPS, tiled=True)  18.6 us
    all_to_all x1, blocking collectives, per_device(): lax.all_to_all(jnp.broadcast_to(shard, (N_Y // 2,) + shard.shape), 'seq',...  16.5 us
    all_to_all x1, blocking collectives, gather_head(): lax.all_to_all(x, 'head', 0, 0, axis_index_groups=X_GROUPS, tiled=True)  15.8 us
    all_gather x1, blocking collectives, per_device(): lax.all_gather(shard, 'seq', axis=0, axis_index_groups=PARITY_GROUPS, til...  14.5 us
    all_gather x1, waiting for transfers between devices, per_device(): lax.all_gather(shards.reshape(HALF, QW), 'seq', axis=0, axis_index_groups...  14.4 us
    ppermute x1, waiting for transfers between devices, per_device(): kept_pair = lax.ppermute(kept, 'seq', SIBLING_SWAP)  6.99 us
    ppermute x1, starting transfers between devices, per_device(): got = lax.ppermute(send, 'head', CORE_SWAP)  6.11 us
    ppermute x1, waiting for transfers between devices, per_device(): got_q = lax.ppermute(send, 'seq', SIBLING_SWAP)  5.49 us
  transfers between devices with their start and end apart: 7, of which 6 were waited for; matrix products, arithmetic and copies ran while one was open for 2% of the time, Pallas kernels for 7%

profile of v6, /device:TPU:1, one launch (start us, length us, event | category | flops | bytes accessed | tf_op | source)
XLA Modules:
  0.0 149.1 jit_solution(13434251404773410466)
XLA Ops:
  6.5 0.0 copy-start.4
  6.6 0.0 copy-start.5
  6.6 0.0 all-gather.4.cloned.1.call-start
  6.6 1.0 broadcast_in_dim.3
  7.6 16.5 %all_to_all.15 = bf16[4,64,512]{2,1,0:T(8,128)(2,1)} all-to-all(bf16[4,64,512]{2,1,0:T(8,128)(2,1)S(1)} %broadcast_in_dim.3), channel_id=1, replica_groups={{0,16,32,48},{8,24,40,56},{64,80,96,112},{72,88,104,120},{128,144,160,1..., dimensions={0} | all-to-all | bytes 524288 | tf_op jit(solution)/shard_map/all_to_all | solution.py:344
  24.1 0.0 all-gather.4.cloned.1.call-update
  24.1 0.0 all-gather.6.cloned.1.call-start
  24.2 0.9 pad_maximum_fusion
  25.1 14.5 %all_gather.13 = bf16[256,768]{1,0:T(8,128)(2,1)} all-gather(bf16[64,768]{1,0:T(8,128)(2,1)S(1)} %pad_maximum_fusion), channel_id=1, replica_groups={{0,16,32,48},{8,24,40,56},{64,80,96,112},{72,88,104,120},{128,144,160,1..., dimensions={0}, use_global_device_ids=true | all-gather | bytes 491520 | tf_op jit(solution)/shard_map/all_gather | solution.py:365
  39.6 0.0 all-gather.6.cloned.1.call-update
  39.6 0.0 copy-done.6
  39.7 0.1 reshape.27
  39.7 0.1 dynamic-slice_reduce_fusion
  39.8 0.1 reshape.28.gain_ref
  39.9 0.0 copy-done.8
  39.9 0.1 copy.13.index_ref
  40.1 0.0 copy-done.7
  40.1 0.6 fusion
  40.7 1.3 stack.17.place_ref
  42.0 0.0 copy-done.3
  42.0 0.0 copy-done.2
  42.0 0.0 copy-done.4
  42.0 2.1 %lower.1 = (bf16[256,768]{1,0:T(8,128)(2,1)S(1)}, bf16[256,256]{1,0:T(8,128)(2,1)S(1)}) custom-call(s32[5]{0:T(128)S(1)} %stack.17.place_ref, s32[256,1]{1,0:T(8,128)S(1)} %copy.13.index_ref, bf16[512,512]{1,0:T(8,128)(2,1)S(1)} %copy-done.2, bf16[512,128]{1,0:T(8,128)(2,1)S(1)} %copy-done.4, bf16[512,128]{1,0:T(8,128)(2,1)S(1)} %copy-done.5, ...), custom_call_target="tpu_custom_call" | custom-call | tf_op jit(solution)/shard_map/lower/pallas_call | solution.py:83
  44.1 1.9 %collective-permute-start = (bf16[256,768]{1,0:T(8,128)(2,1)S(1)}, bf16[256,768]{1,0:T(8,128)(2,1)S(1)}, u32[]{:S(2)}, u32[]{:S(2)}) collective-permute-start(bf16[256,768]{1,0:T(8,128)(2,1)S(1)} %get-tuple-element.11.own_ref), channel_id=1, source_target_pairs={{0,8},{8,0},{16,24},{24,16},{32,40},{40,32},{48,56},{56,48},{64,72... | collective-permute-start | bytes 1179656 | tf_op jit(solution)/shard_map/ppermute | solution.py:362
  46.1 7.0 %collective-permute-done.pair_ref = bf16[256,768]{1,0:T(8,128)(2,1)S(1)} collective-permute-done((bf16[256,768]{1,0:T(8,128)(2,1)S(1)}, bf16[256,768]{1,0:T(8,128)(2,1)S(1)}, u32[]{:S(2)}, u32[]{:S(2)}) %collective-permute-start) | collective-permute-done | bytes 393248 | tf_op jit(solution)/shard_map/ppermute | solution.py:362
  53.1 14.4 %all-gather.4.cloned.1.call-done.weight_ref = bf16[8,256,512]{2,1,0:T(8,128)(2,1)} async-done(((bf16[1,256,512]{2,1,0:T(8,128)(2,1)}), bf16[8,256,512]{2,1,0:T(8,128)(2,1)}) %all-gather.4.cloned.1.call-update) | async-done | bytes 2097168 | tf_op jit(solution)/shard_map/all_gather | solution.py:352
  67.5 1.6 %copy-done.1 = bf16[8,256,512]{2,1,0:T(8,128)(2,1)S(1)} copy-done((bf16[8,256,512]{2,1,0:T(8,128)(2,1)S(1)}, bf16[8,256,512]{2,1,0:T(8,128)(2,1)}, u32[]{:S(2)}) %copy-start.1) | copy-done | bytes 2097176
  69.1 1.3 project_other.1
  70.4 6.1 %collective-permute-start.1 = (bf16[4,512,256]{2,1,0:T(8,128)(2,1)S(1)}, bf16[4,512,256]{2,1,0:T(8,128)(2,1)S(1)}, u32[]{:S(2)}, u32[]{:S(2)}) collective-permute-start(bf16[4,512,256]{2,1,0:T(8,128)(2,1)S(1)} %project_other.1), channel_id=1, source_target_pairs={{0,1},{1,0},{2,3},{3,2},{4,5},{5,4},{6,7},{7,6},{8,9},{9,8},{10,11... | collective-permute-start | bytes 3145736 | tf_op jit(solution)/shard_map/ppermute | solution.py:369
  76.5 1.3 project_mine.1
  77.8 1.0 collective-permute-done.1
  78.7 0.3 add_convert_fusion
  79.1 18.6 %all_to_all.16.parts_ref = bf16[4,512,256]{2,1,0:T(8,128)(2,1)S(1)} all-to-all(bf16[4,512,256]{2,1,0:T(8,128)(2,1)S(1)} %add_convert_fusion), channel_id=1, replica_groups={{0,2,4,6},{1,3,5,7},{8,10,12,14},{9,11,13,15},{16,18,20,22},{17,19,21,2..., dimensions={0} | all-to-all | bytes 2097152 | tf_op jit(solution)/shard_map/all_to_all | solution.py:372
  97.7 0.7 state.1
  98.5 15.8 %all_to_all.17.mine_ref = bf16[4,512,256]{2,1,0:T(8,128)(2,1)S(1)} all-to-all(bf16[4,512,256]{2,1,0:T(8,128)(2,1)S(1)} %state.1), channel_id=1, replica_groups={{0,2,4,6},{1,3,5,7},{8,10,12,14},{9,11,13,15},{16,18,20,22},{17,19,21,2..., dimensions={0} | all-to-all | bytes 2097152 | tf_op jit(solution)/shard_map/all_to_all | solution.py:318
  114.2 4.6 %collective-permute-start.2 = (bf16[4,512,256]{2,1,0:T(8,128)(2,1)S(1)}, bf16[4,512,256]{2,1,0:T(8,128)(2,1)S(1)}, u32[]{:S(2)}, u32[]{:S(2)}) collective-permute-start(bf16[4,512,256]{2,1,0:T(8,128)(2,1)S(1)} %all_to_all.17.mine_ref), channel_id=1, source_target_pairs={{0,1},{1,0},{2,3},{3,2},{4,5},{5,4},{6,7},{7,6},{8,9},{9,8},{10,11... | collective-permute-start | bytes 3145736 | tf_op jit(solution)/shard_map/ppermute | solution.py:319
  118.8 1.3 all-gather.6.cloned.1.call-done
  120.2 0.9 collective-permute-done.2.other_ref
  121.1 3.1 %project_kv.1 = (f32[512,256]{1,0:T(8,128)S(1)}, bf16[256,640]{1,0:T(8,128)(2,1)S(1)}) custom-call(s32[5]{0:T(128)S(1)} %stack.17.place_ref, bf16[4,512,256]{2,1,0:T(8,128)(2,1)S(1)} %all_to_all.17.mine_ref, bf16[4,512,256]{2,1,0:T(8,128)(2,1)S(1)} %collective-permute-done.2.other_ref, bf16[8,256,768]{2,1,0:T(8,128)(2,1)} %bitcast.7), custom_call_target="tpu_custom_call" | custom-call | tf_op jit(solution)/shard_map/project_kv/pallas_call | solution.py:179
  124.2 3.1 %collective-permute-start.4 = (bf16[256,640]{1,0:T(8,128)(2,1)S(1)}, bf16[256,640]{1,0:T(8,128)(2,1)S(1)}, u32[]{:S(2)}, u32[]{:S(2)}) collective-permute-start(bf16[256,640]{1,0:T(8,128)(2,1)S(1)} %get-tuple-element.16), channel_id=1, source_target_pairs={{0,8},{8,0},{16,24},{24,16},{32,40},{40,32},{48,56},{56,48},{64,72... | collective-permute-start | bytes 983048 | tf_op jit(solution)/shard_map/ppermute | solution.py:376
  127.3 0.0 copy-start
  127.3 3.4 %project_sibling.1 = (f32[512,128]{1,0:T(8,128)S(1)}, bf16[272,384]{1,0:T(8,128)(2,1)S(1)}) custom-call(s32[5]{0:T(128)S(1)} %stack.17.place_ref, bf16[4,512,256]{2,1,0:T(8,128)(2,1)S(1)} %all_to_all.17.mine_ref, bf16[4,512,256]{2,1,0:T(8,128)(2,1)S(1)} %collective-permute-done.2.other_ref, bf16[8,256,768]{2,1,0:T(8,128)(2,1)} %bitcast.8, ...), custom_call_target="tpu_custom_call" | custom-call | flops 536870912 | bytes 4194304 | tf_op jit(solution)/shard_map/project_sibling/pallas_call | solution.py:235
  130.8 2.2 %collective-permute-start.3 = (bf16[272,384]{1,0:T(8,128)(2,1)S(1)}, bf16[272,384]{1,0:T(8,128)(2,1)S(1)}, u32[]{:S(2)}, u32[]{:S(2)}) collective-permute-start(bf16[272,384]{1,0:T(8,128)(2,1)S(1)} %get-tuple-element.14.first_ref), channel_id=1, source_target_pairs={{0,8},{8,0},{16,24},{24,16},{32,40},{40,32},{48,56},{56,48},{64,72... | collective-permute-start | bytes 626696 | tf_op jit(solution)/shard_map/ppermute | solution.py:378
  132.9 0.0 copy-done
  133.0 1.2 project_q.1.q_ref
  134.2 5.5 %collective-permute-done.3.got_q_ref = bf16[272,384]{1,0:T(8,128)(2,1)S(1)} collective-permute-done((bf16[272,384]{1,0:T(8,128)(2,1)S(1)}, bf16[272,384]{1,0:T(8,128)(2,1)S(1)}, u32[]{:S(2)}, u32[]{:S(2)}) %collective-permute-start.3) | collective-permute-done | bytes 208928 | tf_op jit(solution)/shard_map/ppermute | solution.py:378
  139.7 0.0 collective-permute-done.4.got_kv_ref
  139.7 2.6 %upper.1 = bf16[256,512]{1,0:T(8,128)(2,1)} custom-call(s32[5]{0:T(128)S(1)} %stack.17.place_ref, f32[256,512]{1,0:T(8,128)S(1)} %project_q.1.q_ref, f32[512,256]{1,0:T(8,128)S(1)} %get-tuple-element.13.first_ref.kv_ref, f32[512,128]{1,0:T(8,128)S(1)} %get-tuple-element.15.square_ref, bf16[272,384]{1,0:T(8,128)(2,1)S(1)} %collective-permute-done.3.got_q_ref, ...), custom_call_target="tpu_custom_call" | custom-call | tf_op jit(solution)/shard_map/upper/pallas_call | solution.py:308
  (8 shorter events, 0.0 us)
Async XLA Ops:
  6.5 33.1 %copy-start.6 = (f32[4096]{0:T(1024)S(1)}, f32[4096]{0:T(1024)}, u32[]{:S(2)}) copy-start(f32[4096]{0:T(1024)} %param.16) | copy-start | bytes 49156
  6.5 33.4 %copy-start.8 = (s32[1,256]{1,0:T(1,128)S(1)}, s32[1,256]{1,0:T(1,128)}, u32[]{:S(2)}) copy-start(s32[1,256]{1,0:T(1,128)} %param.20) | copy-start | bytes 3076
  6.5 33.5 %copy-start.7 = (s32[64]{0:T(128)S(1)}, s32[64]{0:T(128)}, u32[]{:S(2)}) copy-start(s32[64]{0:T(128)} %param.21) | copy-start | bytes 772
  6.5 35.5 %copy-start.3 = (bf16[512,512]{1,0:T(8,128)(2,1)S(1)}, bf16[512,512]{1,0:T(8,128)(2,1)}, u32[]{:S(2)}) copy-start(bf16[512,512]{1,0:T(8,128)(2,1)} %hidden_ref.1) | copy-start | bytes 1572868
  6.5 35.5 %copy-start.2 = (bf16[512,512]{1,0:T(8,128)(2,1)S(1)}, bf16[512,512]{1,0:T(8,128)(2,1)}, u32[]{:S(2)}) copy-start(bf16[512,512]{1,0:T(8,128)(2,1)} %q_ref.1) | copy-start | bytes 1572868
  6.5 35.5 %copy-start.4 = (bf16[512,128]{1,0:T(8,128)(2,1)S(1)}, bf16[512,128]{1,0:T(8,128)(2,1)}, u32[]{:S(2)}) copy-start(bf16[512,128]{1,0:T(8,128)(2,1)} %k_ref.1) | copy-start | bytes 393220
  6.6 35.5 %copy-start.5 = (bf16[512,128]{1,0:T(8,128)(2,1)S(1)}, bf16[512,128]{1,0:T(8,128)(2,1)}, u32[]{:S(2)}) copy-start(bf16[512,128]{1,0:T(8,128)(2,1)} %v_ref.1) | copy-start | bytes 393220
  6.6 60.9 %all-gather.4.cloned.1.call-start = ((), (), s32[]{:S(2)}) async-start(), calls=%async_computation.3 | async-start | bytes 2359296 | tf_op jit(solution)/shard_map/all_gather | solution.py:352
  24.1 96.0 %all-gather.6.cloned.1.call-start = ((), (), s32[]{:S(2)}) async-start(), calls=%async_computation.4 | async-start | bytes 3538944 | tf_op jit(solution)/shard_map/all_gather | solution.py:366
  44.1 8.9 %collective-permute-start = (bf16[256,768]{1,0:T(8,128)(2,1)S(1)}, bf16[256,768]{1,0:T(8,128)(2,1)S(1)}, u32[]{:S(2)}, u32[]{:S(2)}) collective-permute-start(bf16[256,768]{1,0:T(8,128)(2,1)S(1)} %get-tuple-element.11.own_ref), channel_id=1, source_target_pairs={{0,8},{8,0},{16,24},{24,16},{32,40},{40,32},{48,56},{56,48},{64,72... | collective-permute-start | bytes 1179656 | tf_op jit(solution)/shard_map/ppermute | solution.py:362
  67.5 1.6 %copy-start.1 = (bf16[8,256,512]{2,1,0:T(8,128)(2,1)S(1)}, bf16[8,256,512]{2,1,0:T(8,128)(2,1)}, u32[]{:S(2)}) copy-start(bf16[8,256,512]{2,1,0:T(8,128)(2,1)} %all-gather.4.cloned.1.call-done.weight_ref) | copy-start | bytes 6291460
  70.4 8.4 %collective-permute-start.1 = (bf16[4,512,256]{2,1,0:T(8,128)(2,1)S(1)}, bf16[4,512,256]{2,1,0:T(8,128)(2,1)S(1)}, u32[]{:S(2)}, u32[]{:S(2)}) collective-permute-start(bf16[4,512,256]{2,1,0:T(8,128)(2,1)S(1)} %project_other.1), channel_id=1, source_target_pairs={{0,1},{1,0},{2,3},{3,2},{4,5},{5,4},{6,7},{7,6},{8,9},{9,8},{10,11... | collective-permute-start | bytes 3145736 | tf_op jit(solution)/shard_map/ppermute | solution.py:369
  114.2 6.9 %collective-permute-start.2 = (bf16[4,512,256]{2,1,0:T(8,128)(2,1)S(1)}, bf16[4,512,256]{2,1,0:T(8,128)(2,1)S(1)}, u32[]{:S(2)}, u32[]{:S(2)}) collective-permute-start(bf16[4,512,256]{2,1,0:T(8,128)(2,1)S(1)} %all_to_all.17.mine_ref), channel_id=1, source_target_pairs={{0,1},{1,0},{2,3},{3,2},{4,5},{5,4},{6,7},{7,6},{8,9},{9,8},{10,11... | collective-permute-start | bytes 3145736 | tf_op jit(solution)/shard_map/ppermute | solution.py:319
  124.2 15.5 %collective-permute-start.4 = (bf16[256,640]{1,0:T(8,128)(2,1)S(1)}, bf16[256,640]{1,0:T(8,128)(2,1)S(1)}, u32[]{:S(2)}, u32[]{:S(2)}) collective-permute-start(bf16[256,640]{1,0:T(8,128)(2,1)S(1)} %get-tuple-element.16), channel_id=1, source_target_pairs={{0,8},{8,0},{16,24},{24,16},{32,40},{40,32},{48,56},{56,48},{64,72... | collective-permute-start | bytes 983048 | tf_op jit(solution)/shard_map/ppermute | solution.py:376
  127.3 5.6 %copy-start = (bf16[2048,768]{1,0:T(8,128)(2,1)S(1)}, bf16[2048,768]{1,0:T(8,128)(2,1)}, u32[]{:S(2)}) copy-start(bf16[2048,768]{1,0:T(8,128)(2,1)} %all-gather.6.cloned.1.call-done) | copy-start | bytes 9437188
  130.8 9.0 %collective-permute-start.3 = (bf16[272,384]{1,0:T(8,128)(2,1)S(1)}, bf16[272,384]{1,0:T(8,128)(2,1)S(1)}, u32[]{:S(2)}, u32[]{:S(2)}) collective-permute-start(bf16[272,384]{1,0:T(8,128)(2,1)S(1)} %get-tuple-element.14.first_ref), channel_id=1, source_target_pairs={{0,8},{8,0},{16,24},{24,16},{32,40},{40,32},{48,56},{56,48},{64,72... | collective-permute-start | bytes 626696 | tf_op jit(solution)/shard_map/ppermute | solution.py:378
Sparse Core Ops, SparseCore 0:
  24.3 43.1 all-gather.3
  69.6 50.5 all-gather.5

commit v7 on v6

--- a/solution.py
+++ b/solution.py
@@ -154,25 +154,21 @@
     return dot(jnp.concatenate(state, axis=1), weights)
 
 
-def kv_kernel(place_ref, mine_ref, other_ref, weight_ref, keep_ref, send_ref, kv_ref, first_ref, sems):
+def kv_kernel(place_ref, mine_ref, other_ref, weight_ref, keep_ref, send_ref, kv_ref, sems):
     heads = by_core(place_ref[0])
-    copies = []
-    for cols, buffer in ((pl.ds(QW, KVW), kv_ref), (pl.ds(0, HD), first_ref)):
-        for i, head in enumerate(heads):
-            source = weight_ref.at[head, :, cols]
-            copies.append(pltpu.make_async_copy(source, buffer.at[i], sems.at[len(copies)]))
-            copies[-1].start()
-    for copy in copies[: 2 * N_X]:
+    copies = [
+        pltpu.make_async_copy(weight_ref.at[head, :, pl.ds(QW, KVW)], kv_ref.at[i], sems.at[i])
+        for i, head in enumerate(heads)
+    ]
+    for copy in copies:
+        copy.start()
+    for copy in copies:
         copy.wait()
     weights = kv_ref[...].reshape(2 * N_X * HALF, KVW)
     for half, rows in enumerate((OWN, PAIR)):
         sums = contract(rows, mine_ref, other_ref, weights)
         keep_ref[rows] = sums
         send_ref[:, (1 - half) * KVW : (2 - half) * KVW] = sums.astype(jnp.bfloat16)
-    for copy in copies[2 * N_X :]:
-        copy.wait()
-    sums = contract(PAIR, mine_ref, other_ref, first_ref[...].reshape(2 * N_X * HALF, HD))
-    send_ref[:, 2 * KVW :] = sums.astype(jnp.bfloat16)
 
 
 def project_kv(place, mine, other, weights):
@@ -187,12 +183,11 @@
         out_specs=[pl.BlockSpec(memory_space=pltpu.VMEM)] * 2,
         out_shape=[
             jax.ShapeDtypeStruct((2 * KMAX, KVW), jnp.float32),
-            jax.ShapeDtypeStruct((KMAX, 2 * KVW + HD), jnp.bfloat16),
+            jax.ShapeDtypeStruct((KMAX, 2 * KVW), jnp.bfloat16),
         ],
         scratch_shapes=[
             pltpu.VMEM((2 * N_X, HALF, KVW), jnp.bfloat16),
-            pltpu.VMEM((2 * N_X, HALF, HD), jnp.bfloat16),
-            pltpu.SemaphoreType.DMA((4 * N_X,)),
+            pltpu.SemaphoreType.DMA((2 * N_X,)),
         ],
         compiler_params=pltpu.CompilerParams(vmem_limit_bytes=50 * 1024 * 1024),
         name="project_kv",
@@ -200,12 +195,13 @@
 
 
 def sibling_kernel(
-    place_ref, mine_ref, other_ref, weight_ref, inverse_ref, first_ref, square_ref, send_ref
+    place_ref, mine_ref, other_ref, weight_ref, inverse_ref, first_ref, square_ref, send_ref, last_ref
 ):
     heads = by_core(place_ref[0])
-    weights = jnp.concatenate([weight_ref[head, :, HD:QW] for head in heads], axis=0)
+    weights = jnp.concatenate([weight_ref[head, :, :QW] for head in heads], axis=0)
     sums = contract(PAIR, mine_ref, other_ref, weights)
-    send_ref[:KMAX] = sums.astype(jnp.bfloat16)
+    send_ref[...] = sums[:, :KMAX].astype(jnp.bfloat16)
+    last_ref[:KMAX] = sums[:, KMAX:].astype(jnp.bfloat16)
     squares = jnp.zeros((2 * KMAX, HD), jnp.float32)
     for i, head in enumerate(heads):
         scaled = (mine_ref if i < N_X else other_ref)[i % N_X].astype(jnp.float32)
@@ -228,7 +224,7 @@
         high[:, PAIR],
         jnp.where(row == 1, low[:, PAIR], jnp.where(row == 2, high[:, OWN], low[:, OWN])),
     )
-    send_ref[KMAX:] = jnp.concatenate([tail, tail[:, :HD]], axis=1).astype(jnp.bfloat16)
+    last_ref[KMAX:] = tail.astype(jnp.bfloat16)
 
 
 def project_sibling(place, mine, other, weights, inverse, first):
@@ -237,10 +233,11 @@
         in_specs=[pl.BlockSpec(memory_space=pltpu.SMEM)]
         + [pl.BlockSpec(memory_space=pltpu.VMEM)] * 4
         + [pl.BlockSpec(memory_space=pl.ANY)],
-        out_specs=[pl.BlockSpec(memory_space=pltpu.VMEM)] * 2,
+        out_specs=[pl.BlockSpec(memory_space=pltpu.VMEM)] * 3,
         out_shape=[
             jax.ShapeDtypeStruct((2 * KMAX, HD), jnp.float32),
-            jax.ShapeDtypeStruct((KMAX + TAIL, QW - HD), jnp.bfloat16),
+            jax.ShapeDtypeStruct((KMAX, KMAX), jnp.bfloat16),
+            jax.ShapeDtypeStruct((KMAX + TAIL, KMAX), jnp.bfloat16),
         ],
         compiler_params=params(),
         cost_estimate=pl.CostEstimate(flops=2**29, bytes_accessed=2**22, transcendentals=0),
@@ -268,11 +265,11 @@
     )(place, mine, other, weights, first)
 
 
-def upper_kernel(place_ref, q_ref, kv_ref, square_ref, got_q_ref, got_kv_ref, out_ref):
+def upper_kernel(place_ref, q_ref, kv_ref, square_ref, got_q_ref, got_last_ref, got_kv_ref, out_ref):
     parity = place_ref[1]
     own_count = place_ref[2]
     left_count = place_ref[3]
-    tail = got_q_ref[KMAX:, :KMAX].astype(jnp.float32)
+    tail = got_last_ref[KMAX:].astype(jnp.float32)
     same = lax.broadcasted_iota(jnp.int32, (KMAX, KMAX), 0) == lax.broadcasted_iota(
         jnp.int32, (KMAX, KMAX), 1
     )
@@ -284,7 +281,7 @@
     pair_sum = square_ref[KMAX:, :1] + down(tail[2:3] + tail[3:4])
     own_inv = lax.rsqrt(own_sum / D + 1e-05)
     pair_inv = lax.rsqrt(pair_sum / D + 1e-05)
-    got = jnp.concatenate([got_kv_ref[:, 2 * KVW :], got_q_ref[:KMAX]], axis=1)
+    got = jnp.concatenate([got_q_ref[...], got_last_ref[:KMAX]], axis=1)
     queries = ((q_ref[...] + got.astype(jnp.float32)) * own_inv).astype(jnp.bfloat16)
     own = (kv_ref[:KMAX] + got_kv_ref[:, :KVW].astype(jnp.float32)) * own_inv
     own = own.astype(jnp.bfloat16)
@@ -304,14 +301,14 @@
         out_ref[:, cols] = jnp.where(valid, attend(scores, values), 0.0).astype(jnp.bfloat16)
 
 
-def upper(place, q, kv, squares, got_q, got_kv):
+def upper(place, q, kv, squares, got_q, got_last, got_kv):
     return pl.pallas_call(
         upper_kernel,
-        in_specs=[pl.BlockSpec(memory_space=pltpu.SMEM)] + [pl.BlockSpec(memory_space=pltpu.VMEM)] * 5,
+        in_specs=[pl.BlockSpec(memory_space=pltpu.SMEM)] + [pl.BlockSpec(memory_space=pltpu.VMEM)] * 6,
         out_shape=jax.ShapeDtypeStruct((KMAX, QW), jnp.bfloat16),
         compiler_params=params(),
         name="upper",
-    )(place, q, kv, squares, got_q, got_kv)
+    )(place, q, kv, squares, got_q, got_last, got_kv)
 
 
 def gather_head(x):
@@ -374,10 +371,11 @@
 
     kv, send = project_kv(place, mine, other, qkv_weights)
     got_kv = lax.ppermute(send, "seq", SIBLING_SWAP)
-    squares, send = project_sibling(place, mine, other, qkv_weights, inverse, kv)
+    squares, send, last = project_sibling(place, mine, other, qkv_weights, inverse, kv)
     got_q = lax.ppermute(send, "seq", SIBLING_SWAP)
+    got_last = lax.ppermute(last, "seq", SIBLING_SWAP)
     q = project_q(place, mine, other, qkv_weights, send)
-    return upper(place, q, kv, squares, got_q, got_kv)
+    return upper(place, q, kv, squares, got_q, got_last, got_kv)
 
 
 def solution(mesh):

time: 150 us -> 150 us (level)
  starting transfers between devices: 18 us -> 21 us
  waiting for transfers between devices: 30.2 us -> 27.7 us
    ppermute x1, waiting for transfers between devices: 5.49 us -> 3.11 us  [per_device(): got_q = lax.ppermute(send, 'seq', SIBLING_SWAP)]
    ppermute x0 -> x1, starting transfers between devices: none -> 2.25 us  [per_device(): got_last = lax.ppermute(last, 'seq', SIBLING_SWAP)]
  transfers between devices with their start and end apart: 7 -> 8, of which waited for: 6 -> 6; matrix products, arithmetic and copies ran while one was open for 2% -> 2% of each run, Pallas kernels for 7% -> 7%
where the time goes in v7:
time: 150 us; the launch traced here: 149 us
  blocking collectives  65.5 us (44%)
  waiting for transfers between devices  27.7 us (18%)
  starting transfers between devices  21 us (14%)
  Pallas kernels  15.3 us (10%)
  between operations  13.6 us (9%)
  local copies, waits for them, and re-layouts  4.97 us (3%)
    all_to_all x1, blocking collectives, per_device(): lax.all_to_all(parts, 'head', 0, 0, axis_index_groups=X_GROUPS, tiled=True)  18.6 us
    all_to_all x1, blocking collectives, per_device(): lax.all_to_all(jnp.broadcast_to(shard, (N_Y // 2,) + shard.shape), 'seq',...  16.5 us
    all_to_all x1, blocking collectives, gather_head(): lax.all_to_all(x, 'head', 0, 0, axis_index_groups=X_GROUPS, tiled=True)  15.8 us
    all_gather x1, blocking collectives, per_device(): lax.all_gather(shard, 'seq', axis=0, axis_index_groups=PARITY_GROUPS, til...  14.5 us
    all_gather x1, waiting for transfers between devices, per_device(): lax.all_gather(shards.reshape(HALF, QW), 'seq', axis=0, axis_index_groups...  14.3 us
    ppermute x1, waiting for transfers between devices, per_device(): kept_pair = lax.ppermute(kept, 'seq', SIBLING_SWAP)  6.99 us
    ppermute x1, starting transfers between devices, per_device(): got = lax.ppermute(send, 'head', CORE_SWAP)  6.13 us
    ppermute x1, starting transfers between devices, gather_head(): return (mine, lax.ppermute(mine, 'head', CORE_SWAP))  4.6 us
  transfers between devices with their start and end apart: 8, of which 6 were waited for; matrix products, arithmetic and copies ran while one was open for 2% of the time, Pallas kernels for 7%

profile of v7, /device:TPU:1, one launch (start us, length us, event | category | flops | bytes accessed | tf_op | source)
XLA Modules:
  0.0 149.3 jit_solution(10908197025461914531)
XLA Ops:
  6.5 0.0 copy-start.4
  6.6 0.0 copy-start.5
  6.6 0.0 all-gather.4.cloned.1.call-start
  6.6 1.0 broadcast_in_dim.3
  7.6 16.5 %all_to_all.15 = bf16[4,64,512]{2,1,0:T(8,128)(2,1)} all-to-all(bf16[4,64,512]{2,1,0:T(8,128)(2,1)S(1)} %broadcast_in_dim.3), channel_id=1, replica_groups={{0,16,32,48},{8,24,40,56},{64,80,96,112},{72,88,104,120},{128,144,160,1..., dimensions={0} | all-to-all | bytes 524288 | tf_op jit(solution)/shard_map/all_to_all | solution.py:341
  24.1 0.0 all-gather.4.cloned.1.call-update
  24.1 0.0 all-gather.6.cloned.1.call-start
  24.2 0.9 pad_maximum_fusion
  25.1 14.5 %all_gather.13 = bf16[256,768]{1,0:T(8,128)(2,1)} all-gather(bf16[64,768]{1,0:T(8,128)(2,1)S(1)} %pad_maximum_fusion), channel_id=1, replica_groups={{0,16,32,48},{8,24,40,56},{64,80,96,112},{72,88,104,120},{128,144,160,1..., dimensions={0}, use_global_device_ids=true | all-gather | bytes 491520 | tf_op jit(solution)/shard_map/all_gather | solution.py:362
  39.6 0.0 all-gather.6.cloned.1.call-update
  39.6 0.0 copy-done.6
  39.7 0.1 reshape.27
  39.7 0.1 dynamic-slice_reduce_fusion
  39.8 0.1 reshape.28.gain_ref
  39.9 0.0 copy-done.8
  39.9 0.1 copy.13.index_ref
  40.1 0.0 copy-done.7
  40.1 0.7 fusion
  40.7 1.3 stack.17.place_ref
  42.1 0.0 copy-done.3
  42.1 0.0 copy-done.2
  42.1 0.0 copy-done.4
  42.1 2.1 %lower.1 = (bf16[256,768]{1,0:T(8,128)(2,1)S(1)}, bf16[256,256]{1,0:T(8,128)(2,1)S(1)}) custom-call(s32[5]{0:T(128)S(1)} %stack.17.place_ref, s32[256,1]{1,0:T(8,128)S(1)} %copy.13.index_ref, bf16[512,512]{1,0:T(8,128)(2,1)S(1)} %copy-done.2, bf16[512,128]{1,0:T(8,128)(2,1)S(1)} %copy-done.4, bf16[512,128]{1,0:T(8,128)(2,1)S(1)} %copy-done.5, ...), custom_call_target="tpu_custom_call" | custom-call | tf_op jit(solution)/shard_map/lower/pallas_call | solution.py:83
  44.2 1.9 %collective-permute-start = (bf16[256,768]{1,0:T(8,128)(2,1)S(1)}, bf16[256,768]{1,0:T(8,128)(2,1)S(1)}, u32[]{:S(2)}, u32[]{:S(2)}) collective-permute-start(bf16[256,768]{1,0:T(8,128)(2,1)S(1)} %get-tuple-element.12.own_ref), channel_id=1, source_target_pairs={{0,8},{8,0},{16,24},{24,16},{32,40},{40,32},{48,56},{56,48},{64,72... | collective-permute-start | bytes 1179656 | tf_op jit(solution)/shard_map/ppermute | solution.py:359
  46.2 7.0 %collective-permute-done.pair_ref = bf16[256,768]{1,0:T(8,128)(2,1)S(1)} collective-permute-done((bf16[256,768]{1,0:T(8,128)(2,1)S(1)}, bf16[256,768]{1,0:T(8,128)(2,1)S(1)}, u32[]{:S(2)}, u32[]{:S(2)}) %collective-permute-start) | collective-permute-done | bytes 393248 | tf_op jit(solution)/shard_map/ppermute | solution.py:359
  53.2 14.3 %all-gather.4.cloned.1.call-done.weight_ref = bf16[8,256,512]{2,1,0:T(8,128)(2,1)} async-done(((bf16[1,256,512]{2,1,0:T(8,128)(2,1)}), bf16[8,256,512]{2,1,0:T(8,128)(2,1)}) %all-gather.4.cloned.1.call-update) | async-done | bytes 2097168 | tf_op jit(solution)/shard_map/all_gather | solution.py:349
  67.5 1.6 %copy-done.1 = bf16[8,256,512]{2,1,0:T(8,128)(2,1)S(1)} copy-done((bf16[8,256,512]{2,1,0:T(8,128)(2,1)S(1)}, bf16[8,256,512]{2,1,0:T(8,128)(2,1)}, u32[]{:S(2)}) %copy-start.1) | copy-done | bytes 2097176
  69.1 1.3 project_other.1
  70.3 6.1 %collective-permute-start.1 = (bf16[4,512,256]{2,1,0:T(8,128)(2,1)S(1)}, bf16[4,512,256]{2,1,0:T(8,128)(2,1)S(1)}, u32[]{:S(2)}, u32[]{:S(2)}) collective-permute-start(bf16[4,512,256]{2,1,0:T(8,128)(2,1)S(1)} %project_other.1), channel_id=1, source_target_pairs={{0,1},{1,0},{2,3},{3,2},{4,5},{5,4},{6,7},{7,6},{8,9},{9,8},{10,11... | collective-permute-start | bytes 3145736 | tf_op jit(solution)/shard_map/ppermute | solution.py:366
  76.5 1.3 project_mine.1
  77.8 1.0 collective-permute-done.1
  78.7 0.3 add_convert_fusion
  79.1 18.6 %all_to_all.16.parts_ref = bf16[4,512,256]{2,1,0:T(8,128)(2,1)S(1)} all-to-all(bf16[4,512,256]{2,1,0:T(8,128)(2,1)S(1)} %add_convert_fusion), channel_id=1, replica_groups={{0,2,4,6},{1,3,5,7},{8,10,12,14},{9,11,13,15},{16,18,20,22},{17,19,21,2..., dimensions={0} | all-to-all | bytes 2097152 | tf_op jit(solution)/shard_map/all_to_all | solution.py:369
  97.7 0.7 state.1
  98.5 15.8 %all_to_all.17.mine_ref = bf16[4,512,256]{2,1,0:T(8,128)(2,1)S(1)} all-to-all(bf16[4,512,256]{2,1,0:T(8,128)(2,1)S(1)} %state.1), channel_id=1, replica_groups={{0,2,4,6},{1,3,5,7},{8,10,12,14},{9,11,13,15},{16,18,20,22},{17,19,21,2..., dimensions={0} | all-to-all | bytes 2097152 | tf_op jit(solution)/shard_map/all_to_all | solution.py:315
  114.2 4.6 %collective-permute-start.2 = (bf16[4,512,256]{2,1,0:T(8,128)(2,1)S(1)}, bf16[4,512,256]{2,1,0:T(8,128)(2,1)S(1)}, u32[]{:S(2)}, u32[]{:S(2)}) collective-permute-start(bf16[4,512,256]{2,1,0:T(8,128)(2,1)S(1)} %all_to_all.17.mine_ref), channel_id=1, source_target_pairs={{0,1},{1,0},{2,3},{3,2},{4,5},{5,4},{6,7},{7,6},{8,9},{9,8},{10,11... | collective-permute-start | bytes 3145736 | tf_op jit(solution)/shard_map/ppermute | solution.py:316
  118.8 1.3 all-gather.6.cloned.1.call-done
  120.2 0.9 collective-permute-done.2.other_ref
  121.1 2.6 %project_kv.1 = (f32[512,256]{1,0:T(8,128)S(1)}, bf16[256,512]{1,0:T(8,128)(2,1)S(1)}) custom-call(s32[5]{0:T(128)S(1)} %stack.17.place_ref, bf16[4,512,256]{2,1,0:T(8,128)(2,1)S(1)} %all_to_all.17.mine_ref, bf16[4,512,256]{2,1,0:T(8,128)(2,1)S(1)} %collective-permute-done.2.other_ref, bf16[8,256,768]{2,1,0:T(8,128)(2,1)} %bitcast.7), custom_call_target="tpu_custom_call" | custom-call | tf_op jit(solution)/shard_map/project_kv/pallas_call | solution.py:175
  123.7 3.0 %collective-permute-start.5 = (bf16[256,512]{1,0:T(8,128)(2,1)S(1)}, bf16[256,512]{1,0:T(8,128)(2,1)S(1)}, u32[]{:S(2)}, u32[]{:S(2)}) collective-permute-start(bf16[256,512]{1,0:T(8,128)(2,1)S(1)} %get-tuple-element.18), channel_id=1, source_target_pairs={{0,8},{8,0},{16,24},{24,16},{32,40},{40,32},{48,56},{56,48},{64,72... | collective-permute-start | bytes 786440 | tf_op jit(solution)/shard_map/ppermute | solution.py:373
  126.8 3.4 %project_sibling.1 = (f32[512,128]{1,0:T(8,128)S(1)}, bf16[256,256]{1,0:T(8,128)(2,1)S(1)}, bf16[272,256]{1,0:T(8,128)(2,1)S(1)}) custom-call(s32[5]{0:T(128)S(1)} %stack.17.place_ref, bf16[4,512,256]{2,1,0:T(8,128)(2,1)S(1)} %all_to_all.17.mine_ref, bf16[4,512,256]{2,1,0:T(8,128)(2,1)S(1)} %collective-permute-done.2.other_ref, ...), custom_call_target="tpu_custom_call" | custom-call | flops 536870912 | bytes 4194304 | tf_op jit(solution)/shard_map/project_sibling/pallas_call | solution.py:231
  130.2 2.2 %collective-permute-start.4 = (bf16[272,256]{1,0:T(8,128)(2,1)S(1)}, bf16[272,256]{1,0:T(8,128)(2,1)S(1)}, u32[]{:S(2)}, u32[]{:S(2)}) collective-permute-start(bf16[272,256]{1,0:T(8,128)(2,1)S(1)} %get-tuple-element.17), channel_id=1, source_target_pairs={{0,8},{8,0},{16,24},{24,16},{32,40},{40,32},{48,56},{56,48},{64,72... | collective-permute-start | bytes 417800 | tf_op jit(solution)/shard_map/ppermute | solution.py:376
  132.5 3.0 %collective-permute-start.3 = (bf16[256,256]{1,0:T(8,128)(2,1)S(1)}, bf16[256,256]{1,0:T(8,128)(2,1)S(1)}, u32[]{:S(2)}, u32[]{:S(2)}) collective-permute-start(bf16[256,256]{1,0:T(8,128)(2,1)S(1)} %get-tuple-element.15.first_ref), channel_id=1, source_target_pairs={{0,8},{8,0},{16,24},{24,16},{32,40},{40,32},{48,56},{56,48},{64,72... | collective-permute-start | bytes 393224 | tf_op jit(solution)/shard_map/ppermute | solution.py:375
  135.5 1.2 project_q.1.q_ref
  136.8 3.1 %collective-permute-done.3.got_q_ref = bf16[256,256]{1,0:T(8,128)(2,1)S(1)} collective-permute-done((bf16[256,256]{1,0:T(8,128)(2,1)S(1)}, bf16[256,256]{1,0:T(8,128)(2,1)S(1)}, u32[]{:S(2)}, u32[]{:S(2)}) %collective-permute-start.3) | collective-permute-done | bytes 131104 | tf_op jit(solution)/shard_map/ppermute | solution.py:375
  139.9 0.0 collective-permute-done.4.got_last_ref
  139.9 0.0 collective-permute-done.5.got_kv_ref
  139.9 2.6 %upper.1 = bf16[256,512]{1,0:T(8,128)(2,1)} custom-call(s32[5]{0:T(128)S(1)} %stack.17.place_ref, f32[256,512]{1,0:T(8,128)S(1)} %project_q.1.q_ref, f32[512,256]{1,0:T(8,128)S(1)} %get-tuple-element.14.first_ref.kv_ref, f32[512,128]{1,0:T(8,128)S(1)} %get-tuple-element.16.square_ref, bf16[256,256]{1,0:T(8,128)(2,1)S(1)} %collective-permute-done.3.got_q_ref, ...), custom_call_target="tpu_custom_call" | custom-call | tf_op jit(solution)/shard_map/upper/pallas_call | solution.py:305
  (10 shorter events, 0.0 us)
Async XLA Ops:
  6.5 33.1 %copy-start.6 = (f32[4096]{0:T(1024)S(1)}, f32[4096]{0:T(1024)}, u32[]{:S(2)}) copy-start(f32[4096]{0:T(1024)} %param.16) | copy-start | bytes 49156
  6.5 33.4 %copy-start.8 = (s32[1,256]{1,0:T(1,128)S(1)}, s32[1,256]{1,0:T(1,128)}, u32[]{:S(2)}) copy-start(s32[1,256]{1,0:T(1,128)} %param.20) | copy-start | bytes 3076
  6.5 33.5 %copy-start.7 = (s32[64]{0:T(128)S(1)}, s32[64]{0:T(128)}, u32[]{:S(2)}) copy-start(s32[64]{0:T(128)} %param.21) | copy-start | bytes 772
  6.5 35.5 %copy-start.3 = (bf16[512,512]{1,0:T(8,128)(2,1)S(1)}, bf16[512,512]{1,0:T(8,128)(2,1)}, u32[]{:S(2)}) copy-start(bf16[512,512]{1,0:T(8,128)(2,1)} %hidden_ref.1) | copy-start | bytes 1572868
  6.5 35.6 %copy-start.2 = (bf16[512,512]{1,0:T(8,128)(2,1)S(1)}, bf16[512,512]{1,0:T(8,128)(2,1)}, u32[]{:S(2)}) copy-start(bf16[512,512]{1,0:T(8,128)(2,1)} %q_ref.1) | copy-start | bytes 1572868
  6.5 35.6 %copy-start.4 = (bf16[512,128]{1,0:T(8,128)(2,1)S(1)}, bf16[512,128]{1,0:T(8,128)(2,1)}, u32[]{:S(2)}) copy-start(bf16[512,128]{1,0:T(8,128)(2,1)} %k_ref.1) | copy-start | bytes 393220
  6.6 35.6 %copy-start.5 = (bf16[512,128]{1,0:T(8,128)(2,1)S(1)}, bf16[512,128]{1,0:T(8,128)(2,1)}, u32[]{:S(2)}) copy-start(bf16[512,128]{1,0:T(8,128)(2,1)} %v_ref.1) | copy-start | bytes 393220
  6.6 60.9 %all-gather.4.cloned.1.call-start = ((), (), s32[]{:S(2)}) async-start(), calls=%async_computation.3 | async-start | bytes 2359296 | tf_op jit(solution)/shard_map/all_gather | solution.py:349
  24.1 96.0 %all-gather.6.cloned.1.call-start = ((), (), s32[]{:S(2)}) async-start(), calls=%async_computation.4 | async-start | bytes 3538944 | tf_op jit(solution)/shard_map/all_gather | solution.py:363
  44.2 8.9 %collective-permute-start = (bf16[256,768]{1,0:T(8,128)(2,1)S(1)}, bf16[256,768]{1,0:T(8,128)(2,1)S(1)}, u32[]{:S(2)}, u32[]{:S(2)}) collective-permute-start(bf16[256,768]{1,0:T(8,128)(2,1)S(1)} %get-tuple-element.12.own_ref), channel_id=1, source_target_pairs={{0,8},{8,0},{16,24},{24,16},{32,40},{40,32},{48,56},{56,48},{64,72... | collective-permute-start | bytes 1179656 | tf_op jit(solution)/shard_map/ppermute | solution.py:359
  67.5 1.6 %copy-start.1 = (bf16[8,256,512]{2,1,0:T(8,128)(2,1)S(1)}, bf16[8,256,512]{2,1,0:T(8,128)(2,1)}, u32[]{:S(2)}) copy-start(bf16[8,256,512]{2,1,0:T(8,128)(2,1)} %all-gather.4.cloned.1.call-done.weight_ref) | copy-start | bytes 6291460
  70.3 8.4 %collective-permute-start.1 = (bf16[4,512,256]{2,1,0:T(8,128)(2,1)S(1)}, bf16[4,512,256]{2,1,0:T(8,128)(2,1)S(1)}, u32[]{:S(2)}, u32[]{:S(2)}) collective-permute-start(bf16[4,512,256]{2,1,0:T(8,128)(2,1)S(1)} %project_other.1), channel_id=1, source_target_pairs={{0,1},{1,0},{2,3},{3,2},{4,5},{5,4},{6,7},{7,6},{8,9},{9,8},{10,11... | collective-permute-start | bytes 3145736 | tf_op jit(solution)/shard_map/ppermute | solution.py:366
  114.2 6.9 %collective-permute-start.2 = (bf16[4,512,256]{2,1,0:T(8,128)(2,1)S(1)}, bf16[4,512,256]{2,1,0:T(8,128)(2,1)S(1)}, u32[]{:S(2)}, u32[]{:S(2)}) collective-permute-start(bf16[4,512,256]{2,1,0:T(8,128)(2,1)S(1)} %all_to_all.17.mine_ref), channel_id=1, source_target_pairs={{0,1},{1,0},{2,3},{3,2},{4,5},{5,4},{6,7},{7,6},{8,9},{9,8},{10,11... | collective-permute-start | bytes 3145736 | tf_op jit(solution)/shard_map/ppermute | solution.py:316
  123.7 16.2 %collective-permute-start.5 = (bf16[256,512]{1,0:T(8,128)(2,1)S(1)}, bf16[256,512]{1,0:T(8,128)(2,1)S(1)}, u32[]{:S(2)}, u32[]{:S(2)}) collective-permute-start(bf16[256,512]{1,0:T(8,128)(2,1)S(1)} %get-tuple-element.18), channel_id=1, source_target_pairs={{0,8},{8,0},{16,24},{24,16},{32,40},{40,32},{48,56},{56,48},{64,72... | collective-permute-start | bytes 786440 | tf_op jit(solution)/shard_map/ppermute | solution.py:373
  126.8 8.7 %copy-start = (bf16[2048,768]{1,0:T(8,128)(2,1)S(1)}, bf16[2048,768]{1,0:T(8,128)(2,1)}, u32[]{:S(2)}) copy-start(bf16[2048,768]{1,0:T(8,128)(2,1)} %all-gather.6.cloned.1.call-done) | copy-start | bytes 9437188
  130.2 9.7 %collective-permute-start.4 = (bf16[272,256]{1,0:T(8,128)(2,1)S(1)}, bf16[272,256]{1,0:T(8,128)(2,1)S(1)}, u32[]{:S(2)}, u32[]{:S(2)}) collective-permute-start(bf16[272,256]{1,0:T(8,128)(2,1)S(1)} %get-tuple-element.17), channel_id=1, source_target_pairs={{0,8},{8,0},{16,24},{24,16},{32,40},{40,32},{48,56},{56,48},{64,72... | collective-permute-start | bytes 417800 | tf_op jit(solution)/shard_map/ppermute | solution.py:376
  132.5 7.4 %collective-permute-start.3 = (bf16[256,256]{1,0:T(8,128)(2,1)S(1)}, bf16[256,256]{1,0:T(8,128)(2,1)S(1)}, u32[]{:S(2)}, u32[]{:S(2)}) collective-permute-start(bf16[256,256]{1,0:T(8,128)(2,1)S(1)} %get-tuple-element.15.first_ref), channel_id=1, source_target_pairs={{0,8},{8,0},{16,24},{24,16},{32,40},{40,32},{48,56},{56,48},{64,72... | collective-permute-start | bytes 393224 | tf_op jit(solution)/shard_map/ppermute | solution.py:375
Sparse Core Ops, SparseCore 0:
  24.3 43.1 all-gather.3
  69.5 50.5 all-gather.5

commit v8 on v7

--- a/solution.py
+++ b/solution.py
@@ -94,6 +94,21 @@
     )(place, index, queries, keys, values, hidden, gain, inverse)
 
 
+def copies_kernel(shard_ref, out_ref):
+    shard = shard_ref[...]
+    for place in range(N_Y // 2):
+        out_ref[place] = shard
+
+
+def copies_of(shard):
+    return pl.pallas_call(
+        copies_kernel,
+        out_shape=jax.ShapeDtypeStruct((N_Y // 2,) + shard.shape, shard.dtype),
+        compiler_params=params(),
+        name="copies",
+    )(shard)
+
+
 def project_kernel(other, place_ref, own_ref, pair_ref, weight_ref, out_ref):
     core = 1 - place_ref[0] if other else place_ref[0]
     own = own_ref[:, :QW]
@@ -165,10 +180,12 @@
     for copy in copies:
         copy.wait()
     weights = kv_ref[...].reshape(2 * N_X * HALF, KVW)
-    for half, rows in enumerate((OWN, PAIR)):
+    for at in range(0, 2 * KMAX, HD):
+        rows = slice(at, at + HD)
         sums = contract(rows, mine_ref, other_ref, weights)
         keep_ref[rows] = sums
-        send_ref[:, (1 - half) * KVW : (2 - half) * KVW] = sums.astype(jnp.bfloat16)
+        half, at = divmod(at, KMAX)
+        send_ref[at : at + HD, (1 - half) * KVW : (2 - half) * KVW] = sums.astype(jnp.bfloat16)
 
 
 def project_kv(place, mine, other, weights):
@@ -339,7 +356,7 @@
 
     shard = out_weight.T
     shards = lax.all_to_all(
-        jnp.broadcast_to(shard, (N_Y // 2,) + shard.shape),
+        copies_of(shard),
         "seq",
         0,
         0,

time: 150 us -> 150 us (level)
  no operation moved by 1% of the time
where the time goes in v8:
time: 150 us; the launch traced here: 149 us
  blocking collectives  65.6 us (44%)
  waiting for transfers between devices  27.7 us (18%)
  starting transfers between devices  21 us (14%)
  Pallas kernels  15.3 us (10%)
  between operations  13.6 us (9%)
  local copies, waits for them, and re-layouts  4.94 us (3%)
    all_to_all x1, blocking collectives, per_device(): lax.all_to_all(parts, 'head', 0, 0, axis_index_groups=X_GROUPS, tiled=True)  18.6 us
    all_to_all x1, blocking collectives, per_device(): lax.all_to_all(copies_of(shard), 'seq', 0, 0, axis_index_groups=PARITY_GR...  16.7 us
    all_to_all x1, blocking collectives, gather_head(): lax.all_to_all(x, 'head', 0, 0, axis_index_groups=X_GROUPS, tiled=True)  15.8 us
    all_gather x1, blocking collectives, per_device(): lax.all_gather(shard, 'seq', axis=0, axis_index_groups=PARITY_GROUPS, til...  14.5 us
    all_gather x1, waiting for transfers between devices, per_device(): lax.all_gather(shards.reshape(HALF, QW), 'seq', axis=0, axis_index_groups...  14.3 us
    ppermute x1, waiting for transfers between devices, per_device(): kept_pair = lax.ppermute(kept, 'seq', SIBLING_SWAP)  6.99 us
    ppermute x1, starting transfers between devices, per_device(): got = lax.ppermute(send, 'head', CORE_SWAP)  6.13 us
    ppermute x1, starting transfers between devices, gather_head(): return (mine, lax.ppermute(mine, 'head', CORE_SWAP))  4.6 us
  transfers between devices with their start and end apart: 8, of which 6 were waited for; matrix products, arithmetic and copies ran while one was open for 2% of the time, Pallas kernels for 7%

profile of v8, /device:TPU:1, one launch (start us, length us, event | category | flops | bytes accessed | tf_op | source)
XLA Modules:
  0.0 149.4 jit_solution(2678219448168197240)
XLA Ops:
  6.5 0.0 all-gather.4.cloned.1.call-start
  6.6 0.0 copy-start.6
  6.6 0.9 copy-done.6
  7.5 16.7 %all_to_all.15 = bf16[4,64,512]{2,1,0:T(8,128)(2,1)} all-to-all(bf16[4,64,512]{2,1,0:T(8,128)(2,1)S(1)} %copies.1), channel_id=1, replica_groups={{0,16,32,48},{8,24,40,56},{64,80,96,112},{72,88,104,120},{128,144,160,1..., dimensions={0} | all-to-all | bytes 524288 | tf_op jit(solution)/shard_map/all_to_all | solution.py:358
  24.2 0.0 all-gather.4.cloned.1.call-update
  24.2 0.0 all-gather.6.cloned.1.call-start
  24.3 0.9 pad_maximum_fusion
  25.2 14.5 %all_gather.13 = bf16[256,768]{1,0:T(8,128)(2,1)} all-gather(bf16[64,768]{1,0:T(8,128)(2,1)S(1)} %pad_maximum_fusion), channel_id=1, replica_groups={{0,16,32,48},{8,24,40,56},{64,80,96,112},{72,88,104,120},{128,144,160,1..., dimensions={0}, use_global_device_ids=true | all-gather | bytes 491520 | tf_op jit(solution)/shard_map/all_gather | solution.py:379
  39.7 0.0 all-gather.6.cloned.1.call-update
  39.7 0.0 copy-done.7
  39.8 0.1 reshape.27
  39.9 0.1 dynamic-slice_reduce_fusion
  39.9 0.1 reshape.28.gain_ref
  40.0 0.0 copy-done.9
  40.0 0.1 copy.13.index_ref
  40.2 0.0 copy-done.8
  40.2 0.7 fusion
  40.8 1.3 stack.17.place_ref
  42.2 0.0 copy-done.3
  42.2 0.0 copy-done.2
  42.2 0.0 copy-done.4
  42.2 2.1 %lower.1 = (bf16[256,768]{1,0:T(8,128)(2,1)S(1)}, bf16[256,256]{1,0:T(8,128)(2,1)S(1)}) custom-call(s32[5]{0:T(128)S(1)} %stack.17.place_ref, s32[256,1]{1,0:T(8,128)S(1)} %copy.13.index_ref, bf16[512,512]{1,0:T(8,128)(2,1)S(1)} %copy-done.2, bf16[512,128]{1,0:T(8,128)(2,1)S(1)} %copy-done.4, bf16[512,128]{1,0:T(8,128)(2,1)S(1)} %copy-done.5, ...), custom_call_target="tpu_custom_call" | custom-call | tf_op jit(solution)/shard_map/lower/pallas_call | solution.py:83
  44.3 1.9 %collective-permute-start = (bf16[256,768]{1,0:T(8,128)(2,1)S(1)}, bf16[256,768]{1,0:T(8,128)(2,1)S(1)}, u32[]{:S(2)}, u32[]{:S(2)}) collective-permute-start(bf16[256,768]{1,0:T(8,128)(2,1)S(1)} %get-tuple-element.12.own_ref), channel_id=1, source_target_pairs={{0,8},{8,0},{16,24},{24,16},{32,40},{40,32},{48,56},{56,48},{64,72... | collective-permute-start | bytes 1179656 | tf_op jit(solution)/shard_map/ppermute | solution.py:376
  46.3 7.0 %collective-permute-done.pair_ref = bf16[256,768]{1,0:T(8,128)(2,1)S(1)} collective-permute-done((bf16[256,768]{1,0:T(8,128)(2,1)S(1)}, bf16[256,768]{1,0:T(8,128)(2,1)S(1)}, u32[]{:S(2)}, u32[]{:S(2)}) %collective-permute-start) | collective-permute-done | bytes 393248 | tf_op jit(solution)/shard_map/ppermute | solution.py:376
  53.3 14.3 %all-gather.4.cloned.1.call-done.weight_ref = bf16[8,256,512]{2,1,0:T(8,128)(2,1)} async-done(((bf16[1,256,512]{2,1,0:T(8,128)(2,1)}), bf16[8,256,512]{2,1,0:T(8,128)(2,1)}) %all-gather.4.cloned.1.call-update) | async-done | bytes 2097168 | tf_op jit(solution)/shard_map/all_gather | solution.py:366
  67.6 1.6 %copy-done.1 = bf16[8,256,512]{2,1,0:T(8,128)(2,1)S(1)} copy-done((bf16[8,256,512]{2,1,0:T(8,128)(2,1)S(1)}, bf16[8,256,512]{2,1,0:T(8,128)(2,1)}, u32[]{:S(2)}) %copy-start.1) | copy-done | bytes 2097176
  69.2 1.3 project_other.1
  70.5 6.1 %collective-permute-start.1 = (bf16[4,512,256]{2,1,0:T(8,128)(2,1)S(1)}, bf16[4,512,256]{2,1,0:T(8,128)(2,1)S(1)}, u32[]{:S(2)}, u32[]{:S(2)}) collective-permute-start(bf16[4,512,256]{2,1,0:T(8,128)(2,1)S(1)} %project_other.1), channel_id=1, source_target_pairs={{0,1},{1,0},{2,3},{3,2},{4,5},{5,4},{6,7},{7,6},{8,9},{9,8},{10,11... | collective-permute-start | bytes 3145736 | tf_op jit(solution)/shard_map/ppermute | solution.py:383
  76.6 1.3 project_mine.1
  77.9 1.0 collective-permute-done.1
  78.9 0.3 add_convert_fusion
  79.2 18.6 %all_to_all.16.parts_ref = bf16[4,512,256]{2,1,0:T(8,128)(2,1)S(1)} all-to-all(bf16[4,512,256]{2,1,0:T(8,128)(2,1)S(1)} %add_convert_fusion), channel_id=1, replica_groups={{0,2,4,6},{1,3,5,7},{8,10,12,14},{9,11,13,15},{16,18,20,22},{17,19,21,2..., dimensions={0} | all-to-all | bytes 2097152 | tf_op jit(solution)/shard_map/all_to_all | solution.py:386
  97.8 0.7 state.1
  98.6 15.8 %all_to_all.17.mine_ref = bf16[4,512,256]{2,1,0:T(8,128)(2,1)S(1)} all-to-all(bf16[4,512,256]{2,1,0:T(8,128)(2,1)S(1)} %state.1), channel_id=1, replica_groups={{0,2,4,6},{1,3,5,7},{8,10,12,14},{9,11,13,15},{16,18,20,22},{17,19,21,2..., dimensions={0} | all-to-all | bytes 2097152 | tf_op jit(solution)/shard_map/all_to_all | solution.py:332
  114.3 4.6 %collective-permute-start.2 = (bf16[4,512,256]{2,1,0:T(8,128)(2,1)S(1)}, bf16[4,512,256]{2,1,0:T(8,128)(2,1)S(1)}, u32[]{:S(2)}, u32[]{:S(2)}) collective-permute-start(bf16[4,512,256]{2,1,0:T(8,128)(2,1)S(1)} %all_to_all.17.mine_ref), channel_id=1, source_target_pairs={{0,1},{1,0},{2,3},{3,2},{4,5},{5,4},{6,7},{7,6},{8,9},{9,8},{10,11... | collective-permute-start | bytes 3145736 | tf_op jit(solution)/shard_map/ppermute | solution.py:333
  118.9 1.3 all-gather.6.cloned.1.call-done
  120.3 0.9 collective-permute-done.2.other_ref
  121.2 2.6 %project_kv.1 = (f32[512,256]{1,0:T(8,128)S(1)}, bf16[256,512]{1,0:T(8,128)(2,1)S(1)}) custom-call(s32[5]{0:T(128)S(1)} %stack.17.place_ref, bf16[4,512,256]{2,1,0:T(8,128)(2,1)S(1)} %all_to_all.17.mine_ref, bf16[4,512,256]{2,1,0:T(8,128)(2,1)S(1)} %collective-permute-done.2.other_ref, bf16[8,256,768]{2,1,0:T(8,128)(2,1)} %bitcast.7), custom_call_target="tpu_custom_call" | custom-call | tf_op jit(solution)/shard_map/project_kv/pallas_call | solution.py:192
  123.8 3.0 %collective-permute-start.5 = (bf16[256,512]{1,0:T(8,128)(2,1)S(1)}, bf16[256,512]{1,0:T(8,128)(2,1)S(1)}, u32[]{:S(2)}, u32[]{:S(2)}) collective-permute-start(bf16[256,512]{1,0:T(8,128)(2,1)S(1)} %get-tuple-element.18), channel_id=1, source_target_pairs={{0,8},{8,0},{16,24},{24,16},{32,40},{40,32},{48,56},{56,48},{64,72... | collective-permute-start | bytes 786440 | tf_op jit(solution)/shard_map/ppermute | solution.py:390
  126.9 3.4 %project_sibling.1 = (f32[512,128]{1,0:T(8,128)S(1)}, bf16[256,256]{1,0:T(8,128)(2,1)S(1)}, bf16[272,256]{1,0:T(8,128)(2,1)S(1)}) custom-call(s32[5]{0:T(128)S(1)} %stack.17.place_ref, bf16[4,512,256]{2,1,0:T(8,128)(2,1)S(1)} %all_to_all.17.mine_ref, bf16[4,512,256]{2,1,0:T(8,128)(2,1)S(1)} %collective-permute-done.2.other_ref, ...), custom_call_target="tpu_custom_call" | custom-call | flops 536870912 | bytes 4194304 | tf_op jit(solution)/shard_map/project_sibling/pallas_call | solution.py:248
  130.3 2.2 %collective-permute-start.4 = (bf16[272,256]{1,0:T(8,128)(2,1)S(1)}, bf16[272,256]{1,0:T(8,128)(2,1)S(1)}, u32[]{:S(2)}, u32[]{:S(2)}) collective-permute-start(bf16[272,256]{1,0:T(8,128)(2,1)S(1)} %get-tuple-element.17), channel_id=1, source_target_pairs={{0,8},{8,0},{16,24},{24,16},{32,40},{40,32},{48,56},{56,48},{64,72... | collective-permute-start | bytes 417800 | tf_op jit(solution)/shard_map/ppermute | solution.py:393
  132.6 3.0 %collective-permute-start.3 = (bf16[256,256]{1,0:T(8,128)(2,1)S(1)}, bf16[256,256]{1,0:T(8,128)(2,1)S(1)}, u32[]{:S(2)}, u32[]{:S(2)}) collective-permute-start(bf16[256,256]{1,0:T(8,128)(2,1)S(1)} %get-tuple-element.15.first_ref), channel_id=1, source_target_pairs={{0,8},{8,0},{16,24},{24,16},{32,40},{40,32},{48,56},{56,48},{64,72... | collective-permute-start | bytes 393224 | tf_op jit(solution)/shard_map/ppermute | solution.py:392
  135.6 0.0 copy-done
  135.6 1.2 project_q.1.q_ref
  136.9 3.1 %collective-permute-done.3.got_q_ref = bf16[256,256]{1,0:T(8,128)(2,1)S(1)} collective-permute-done((bf16[256,256]{1,0:T(8,128)(2,1)S(1)}, bf16[256,256]{1,0:T(8,128)(2,1)S(1)}, u32[]{:S(2)}, u32[]{:S(2)}) %collective-permute-start.3) | collective-permute-done | bytes 131104 | tf_op jit(solution)/shard_map/ppermute | solution.py:392
  140.0 0.0 collective-permute-done.4.got_last_ref
  140.0 0.0 collective-permute-done.5.got_kv_ref
  140.0 2.6 %upper.1 = bf16[256,512]{1,0:T(8,128)(2,1)} custom-call(s32[5]{0:T(128)S(1)} %stack.17.place_ref, f32[256,512]{1,0:T(8,128)S(1)} %project_q.1.q_ref, f32[512,256]{1,0:T(8,128)S(1)} %get-tuple-element.14.first_ref.kv_ref, f32[512,128]{1,0:T(8,128)S(1)} %get-tuple-element.16.square_ref, bf16[256,256]{1,0:T(8,128)(2,1)S(1)} %collective-permute-done.3.got_q_ref, ...), custom_call_target="tpu_custom_call" | custom-call | tf_op jit(solution)/shard_map/upper/pallas_call | solution.py:322
  (12 shorter events, 0.1 us)
Async XLA Ops:
  6.5 35.7 %copy-start.3 = (bf16[512,512]{1,0:T(8,128)(2,1)S(1)}, bf16[512,512]{1,0:T(8,128)(2,1)}, u32[]{:S(2)}) copy-start(bf16[512,512]{1,0:T(8,128)(2,1)} %hidden_ref.1) | copy-start | bytes 1572868
  6.5 35.7 %copy-start.2 = (bf16[512,512]{1,0:T(8,128)(2,1)S(1)}, bf16[512,512]{1,0:T(8,128)(2,1)}, u32[]{:S(2)}) copy-start(bf16[512,512]{1,0:T(8,128)(2,1)} %q_ref.1) | copy-start | bytes 1572868
  6.5 35.7 %copy-start.4 = (bf16[512,128]{1,0:T(8,128)(2,1)S(1)}, bf16[512,128]{1,0:T(8,128)(2,1)}, u32[]{:S(2)}) copy-start(bf16[512,128]{1,0:T(8,128)(2,1)} %k_ref.1) | copy-start | bytes 393220
  6.5 35.7 %copy-start.5 = (bf16[512,128]{1,0:T(8,128)(2,1)S(1)}, bf16[512,128]{1,0:T(8,128)(2,1)}, u32[]{:S(2)}) copy-start(bf16[512,128]{1,0:T(8,128)(2,1)} %v_ref.1) | copy-start | bytes 393220
  6.5 61.0 %all-gather.4.cloned.1.call-start = ((), (), s32[]{:S(2)}) async-start(), calls=%async_computation.3 | async-start | bytes 2359296 | tf_op jit(solution)/shard_map/all_gather | solution.py:366
  6.6 0.9 copy-start.6
  7.5 32.2 %copy-start.7 = (f32[4096]{0:T(1024)S(1)}, f32[4096]{0:T(1024)}, u32[]{:S(2)}) copy-start(f32[4096]{0:T(1024)} %param.16) | copy-start | bytes 49156
  7.5 32.5 %copy-start.9 = (s32[1,256]{1,0:T(1,128)S(1)}, s32[1,256]{1,0:T(1,128)}, u32[]{:S(2)}) copy-start(s32[1,256]{1,0:T(1,128)} %param.20) | copy-start | bytes 3076
  7.5 32.6 %copy-start.8 = (s32[64]{0:T(128)S(1)}, s32[64]{0:T(128)}, u32[]{:S(2)}) copy-start(s32[64]{0:T(128)} %param.21) | copy-start | bytes 772
  24.2 96.0 %all-gather.6.cloned.1.call-start = ((), (), s32[]{:S(2)}) async-start(), calls=%async_computation.4 | async-start | bytes 3538944 | tf_op jit(solution)/shard_map/all_gather | solution.py:380
  44.3 8.9 %collective-permute-start = (bf16[256,768]{1,0:T(8,128)(2,1)S(1)}, bf16[256,768]{1,0:T(8,128)(2,1)S(1)}, u32[]{:S(2)}, u32[]{:S(2)}) collective-permute-start(bf16[256,768]{1,0:T(8,128)(2,1)S(1)} %get-tuple-element.12.own_ref), channel_id=1, source_target_pairs={{0,8},{8,0},{16,24},{24,16},{32,40},{40,32},{48,56},{56,48},{64,72... | collective-permute-start | bytes 1179656 | tf_op jit(solution)/shard_map/ppermute | solution.py:376
  67.6 1.6 %copy-start.1 = (bf16[8,256,512]{2,1,0:T(8,128)(2,1)S(1)}, bf16[8,256,512]{2,1,0:T(8,128)(2,1)}, u32[]{:S(2)}) copy-start(bf16[8,256,512]{2,1,0:T(8,128)(2,1)} %all-gather.4.cloned.1.call-done.weight_ref) | copy-start | bytes 6291460
  70.5 8.4 %collective-permute-start.1 = (bf16[4,512,256]{2,1,0:T(8,128)(2,1)S(1)}, bf16[4,512,256]{2,1,0:T(8,128)(2,1)S(1)}, u32[]{:S(2)}, u32[]{:S(2)}) collective-permute-start(bf16[4,512,256]{2,1,0:T(8,128)(2,1)S(1)} %project_other.1), channel_id=1, source_target_pairs={{0,1},{1,0},{2,3},{3,2},{4,5},{5,4},{6,7},{7,6},{8,9},{9,8},{10,11... | collective-permute-start | bytes 3145736 | tf_op jit(solution)/shard_map/ppermute | solution.py:383
  114.3 6.9 %collective-permute-start.2 = (bf16[4,512,256]{2,1,0:T(8,128)(2,1)S(1)}, bf16[4,512,256]{2,1,0:T(8,128)(2,1)S(1)}, u32[]{:S(2)}, u32[]{:S(2)}) collective-permute-start(bf16[4,512,256]{2,1,0:T(8,128)(2,1)S(1)} %all_to_all.17.mine_ref), channel_id=1, source_target_pairs={{0,1},{1,0},{2,3},{3,2},{4,5},{5,4},{6,7},{7,6},{8,9},{9,8},{10,11... | collective-permute-start | bytes 3145736 | tf_op jit(solution)/shard_map/ppermute | solution.py:333
  123.8 16.2 %collective-permute-start.5 = (bf16[256,512]{1,0:T(8,128)(2,1)S(1)}, bf16[256,512]{1,0:T(8,128)(2,1)S(1)}, u32[]{:S(2)}, u32[]{:S(2)}) collective-permute-start(bf16[256,512]{1,0:T(8,128)(2,1)S(1)} %get-tuple-element.18), channel_id=1, source_target_pairs={{0,8},{8,0},{16,24},{24,16},{32,40},{40,32},{48,56},{56,48},{64,72... | collective-permute-start | bytes 786440 | tf_op jit(solution)/shard_map/ppermute | solution.py:390
  126.9 8.7 %copy-start = (bf16[2048,768]{1,0:T(8,128)(2,1)S(1)}, bf16[2048,768]{1,0:T(8,128)(2,1)}, u32[]{:S(2)}) copy-start(bf16[2048,768]{1,0:T(8,128)(2,1)} %all-gather.6.cloned.1.call-done) | copy-start | bytes 9437188
  130.3 9.7 %collective-permute-start.4 = (bf16[272,256]{1,0:T(8,128)(2,1)S(1)}, bf16[272,256]{1,0:T(8,128)(2,1)S(1)}, u32[]{:S(2)}, u32[]{:S(2)}) collective-permute-start(bf16[272,256]{1,0:T(8,128)(2,1)S(1)} %get-tuple-element.17), channel_id=1, source_target_pairs={{0,8},{8,0},{16,24},{24,16},{32,40},{40,32},{48,56},{56,48},{64,72... | collective-permute-start | bytes 417800 | tf_op jit(solution)/shard_map/ppermute | solution.py:393
  132.6 7.4 %collective-permute-start.3 = (bf16[256,256]{1,0:T(8,128)(2,1)S(1)}, bf16[256,256]{1,0:T(8,128)(2,1)S(1)}, u32[]{:S(2)}, u32[]{:S(2)}) collective-permute-start(bf16[256,256]{1,0:T(8,128)(2,1)S(1)} %get-tuple-element.15.first_ref), channel_id=1, source_target_pairs={{0,8},{8,0},{16,24},{24,16},{32,40},{40,32},{48,56},{56,48},{64,72... | collective-permute-start | bytes 393224 | tf_op jit(solution)/shard_map/ppermute | solution.py:392
Sparse Core Ops, SparseCore 0:
  24.4 43.1 all-gather.3
  69.7 50.5 all-gather.5
